TPU v7x, 32 devices: a whole 2x2x4 slice. The times are simulated.
32 devices in a mesh: pan: 16 (over z, x, core), grp: 2 (over y).
Axes of the slice: x: 2, y: 2, z: 4, core: 2. Of those that a mesh axis runs over, the one named last changes fastest.
Arguments:
- amplitudes: bfloat16 [1024, 8192], P('grp', 'pan'), may hold values from -6 to 6
- integrals: bfloat16 [8192, 32768], P('grp', 'pan'), may hold values from -0.0625 to 0.0625
- amp_screen: int32 [16, 2], replicated, may hold values from 0 to 1, as said below
- int_screen: int32 [2, 8], replicated, may hold values 0 or 1
Outputs:
- ladder_term: bfloat16 [1024, 32768], P('grp', 'pan')
Inputs may be any that keep to these rules, and one draw needn't show every extreme that they name: Take the tiles of amp_screen in blocks of 8 consecutive occupied pair tiles; in each block and column at least one and at most 4 tiles are 1, and some block and column has exactly 4.
All inputs are finite; a program needn't handle non-finite values.
Results may differ from a plain program's by a relative error of at most 0.001.
Values may be sent and summed in bfloat16 or wider, within the bound.
No kernel may reach another device: no remote copies, remote signals or barrier semaphores. Data moves between devices by JAX's collectives and lax.ppermute only.
A program may use at most 128 MiB of HBM per device.

v0:
```python
import jax
import jax.numpy as jnp
from jax import lax
from jax.sharding import PartitionSpec as P

TS = 64


def column_pairs(piece_width, pair_size, pair_count):
    col_pair = jnp.arange(piece_width) // pair_size
    return (col_pair[None, :] == jnp.arange(pair_count)[:, None]).astype(jnp.bfloat16)


def shards(amplitudes, integrals, amp_screen, int_screen):
    pair_size = TS * TS
    row_count, col_count = amplitudes.shape
    int_count, ab_count = integrals.shape
    tile_count = row_count // TS
    pair_count = amp_screen.shape[1]
    grp_index = lax.axis_index("grp")
    pan_index = lax.axis_index("pan")
    screen_rows = lax.dynamic_slice_in_dim(amp_screen, grp_index * tile_count, tile_count, 0)
    in_pair = grp_index * int_count // pair_size
    out_pair = pan_index * ab_count // pair_size
    int_keep = int_screen[in_pair, out_pair].astype(jnp.bfloat16)
    int_panel = lax.all_gather(integrals * int_keep, "grp", axis=0, tiled=True)
    panel = lax.all_gather(amplitudes, "pan", axis=1, tiled=True)
    piece_width = panel.shape[1]
    onehot = column_pairs(piece_width, pair_size, pair_count)
    keep_mask = jnp.dot(
        screen_rows.astype(jnp.bfloat16), onehot, preferred_element_type=jnp.float32
    ).astype(jnp.bfloat16)
    masked = (panel.reshape(tile_count, TS, piece_width) * keep_mask[:, None, :]).reshape(
        row_count, piece_width
    )
    summed = jnp.dot(masked, int_panel, preferred_element_type=jnp.float32)
    return summed.astype(jnp.bfloat16)


def solution(mesh):
    in_specs = (P("grp", "pan"), P("grp", "pan"), P(), P())
    out_specs = P("grp", "pan")
    return jax.shard_map(shards, mesh=mesh, in_specs=in_specs, out_specs=out_specs, check_vma=False)
```

profile of v0, /device:TPU:0, one launch (start us, length us, event | category | flops | bytes accessed | tf_op | source)
XLA Modules:
  0.0 510.1 jit_solution(2660072739913515861)
XLA Ops:
  6.5 0.0 all-gather.3.cloned.1.call-start
  6.5 0.7 all-gather.3.cloned.1.call-update
  7.3 0.0 all-gather.5.cloned.1.call-start
  7.3 1.3 dynamic_slice.7
  9.3 13.8 %broadcast_multiply_fusion = bf16[4096,2048]{1,0:T(8,128)(2,1)} fusion(bf16[4096,2048]{1,0:T(8,128)(2,1)} %param.5, bf16[]{:T(256)} %bitcast.1), kind=kLoop, calls=%fused_computation.2 | loop fusion | flops 8388608 | bytes 33554432 | tf_op jit(solution)/shard_map/mul | solution.py:26
  23.0 0.0 copy-start
  23.0 0.0 all-gather.5.cloned.1.call-update
  23.1 0.6 copy-done
  23.7 0.3 convolution_convert_fusion
  24.0 66.3 %all-gather.3.cloned.1.call-done = bf16[512,8192]{1,0:T(8,128)(2,1)} async-done(((bf16[512,512]{1,0:T(8,128)(2,1)}), bf16[512,8192]{1,0:T(8,128)(2,1)}) %all-gather.3.cloned.1.call-update) | async-done | bytes 8388624 | tf_op jit(solution)/shard_map/all_gather | solution.py:27
  90.3 8.7 %bitcast_multiply_fusion = bf16[512,8192]{1,0:T(8,128)(2,1)} fusion(bf16[512,8192]{1,0:T(8,128)(2,1)} %all-gather.3.cloned.1.call-done, bf16[8,8192]{1,0:T(8,128)(2,1)S(1)} %convolution_convert_fusion), kind=kLoop, calls=%fused_computation.1 | loop fusion | flops 4194304 | bytes 16908288 | tf_op jit(solution)/shard_map/mul | solution.py:33
  99.1 379.6 %all-gather.5.cloned.1.call-done = bf16[8192,2048]{1,0:T(8,128)(2,1)} async-done(((bf16[4096,2048]{1,0:T(8,128)(2,1)}), bf16[8192,2048]{1,0:T(8,128)(2,1)}) %all-gather.5.cloned.1.call-update) | async-done | bytes 33554448 | tf_op jit(solution)/shard_map/all_gather | solution.py:26
  478.7 24.6 %convolution_convert_fusion.1 = bf16[512,2048]{1,0:T(8,128)(2,1)} fusion(bf16[512,8192]{1,0:T(8,128)(2,1)} %bitcast_multiply_fusion, bf16[8192,2048]{1,0:T(8,128)(2,1)} %all-gather.5.cloned.1.call-done), kind=kOutput, calls=%fused_computation.3 | convolution fusion | flops 17180917760 | bytes 44040192 | tf_op jit(solution)/shard_map/dot_general | solution.py:36
  (1 shorter events, 0.0 us)
Async XLA Ops:
  6.5 83.8 %all-gather.3.cloned.1.call-start = ((), (), s32[]{:S(2)}) async-start(), calls=%async_computation | async-start | bytes 8912896 | tf_op jit(solution)/shard_map/all_gather | solution.py:27
  7.3 471.4 %all-gather.5.cloned.1.call-start = ((), (), s32[]{:S(2)}) async-start(), calls=%async_computation.1 | async-start | bytes 50331648 | tf_op jit(solution)/shard_map/all_gather | solution.py:26
  23.0 0.7 copy-start
Sparse Core Ops, SparseCore 0:
  9.5 80.7 all-gather.2
  91.9 386.7 all-gather.4
where the time goes:
time: 510 us
  waiting for transfers between devices  447 us (88%)
  matrix products  24.8 us (5%)
  other arithmetic  22.5 us (4%)
  between operations  14.1 us (3%)
    all_gather x1, waiting for transfers between devices, shards(): int_panel = lax.all_gather(integrals * int_keep, 'grp', axis=0, tiled=True)  380 us
    all_gather x1, waiting for transfers between devices, shards(): panel = lax.all_gather(amplitudes, 'pan', axis=1, tiled=True)  66.3 us
    dot_general x1, matrix products, shards(): summed = jnp.dot(masked, int_panel, preferred_element_type=jnp.float32)  24.6 us
    mul x1, other arithmetic, shards(): int_panel = lax.all_gather(integrals * int_keep, 'grp', axis=0, tiled=True)  13.8 us
  transfers between devices with their start and end apart: 2, of which 2 were waited for; matrix products, arithmetic and copies ran while one was open for 5% of the time, Pallas kernels for 0%

commit v1 on v0

--- a/solution.py
+++ b/solution.py
@@ -1,9 +1,248 @@
+import functools
+
 import jax
 import jax.numpy as jnp
 from jax import lax
+from jax.experimental import pallas as pl
+from jax.experimental.pallas import tpu as pltpu
 from jax.sharding import PartitionSpec as P
 
 TS = 64
+LIVE_MAX = 4
+BLOCK_TILES = 8
+AXES = ("pan", "grp")
+SLOT_CHUNKS = ((0, 2), (2, 4))
+CODE_MAX = 32767.0
+LEAST_SCALE = 1e-33
+COLUMN_TILE = 256
+JOIN_TILE = 512
+VMEM_BYTES = 56 * 1024 * 1024
+
+
+def live_slots(screen_ref, first_tile, column):
+    count = jnp.int32(0)
+    slots = [jnp.int32(0)] * LIVE_MAX
+    for tile in range(BLOCK_TILES):
+        live = screen_ref[first_tile + tile, column] != 0
+        for slot in range(LIVE_MAX):
+            slots[slot] = jnp.where(live & (count == slot), tile, slots[slot])
+        count = count + live.astype(jnp.int32)
+    return slots, count
+
+
+def pick_kernel(pair_size, screen_ref, amps_ref, *rest):
+    picked_refs, sem = rest[:-1], rest[-1]
+    column = lax.axis_index("pan") * amps_ref.shape[1] // pair_size
+    slots, _ = live_slots(screen_ref, lax.axis_index("grp") * BLOCK_TILES, column)
+    copies = []
+    for (first, last), picked_ref in zip(SLOT_CHUNKS, picked_refs):
+        for slot in range(first, last):
+            rows = pl.ds(pl.multiple_of(slots[slot] * TS, TS), TS)
+            copies.append(
+                pltpu.make_async_copy(
+                    amps_ref.at[rows, :],
+                    picked_ref.at[pl.ds((slot - first) * TS, TS), :],
+                    sem.at[slot],
+                )
+            )
+    for copy in copies:
+        copy.start()
+    for copy in copies:
+        copy.wait()
+
+
+def pick_live(amplitudes, amp_screen, pair_size):
+    return pl.pallas_call(
+        functools.partial(pick_kernel, pair_size),
+        out_shape=[
+            jax.ShapeDtypeStruct(((last - first) * TS, amplitudes.shape[1]), amplitudes.dtype)
+            for first, last in SLOT_CHUNKS
+        ],
+        in_specs=[pl.BlockSpec(memory_space=pltpu.SMEM), pl.BlockSpec(memory_space=pl.ANY)],
+        out_specs=[pl.BlockSpec(memory_space=pl.ANY)] * len(SLOT_CHUNKS),
+        scratch_shapes=[pltpu.SemaphoreType.DMA((LIVE_MAX,))],
+        name="pick_live",
+    )(amp_screen, amplitudes)
+
+
+def lay_out(blocks, panel):
+    depth = blocks[0].shape[1]
+    own = lax.rem(lax.axis_index("pan"), len(blocks))
+    for step, block in enumerate(blocks):
+        column = pl.multiple_of((own ^ step) * depth, depth)
+        panel[:, pl.ds(column, depth)] = block[...]
+
+
+def int_keep(screen_ref, ints_shape, pair_size):
+    in_pair = lax.axis_index("grp") * ints_shape[0] // pair_size
+    out_pair = lax.axis_index("pan") * ints_shape[1] // pair_size
+    return screen_ref[in_pair, out_pair].astype(jnp.float32)
+
+
+def own_kernel(ints_shape, pair_size, screen_ref, *refs):
+    blocks, (ints_ref, sum_ref, panel) = refs[:-3], refs[-3:]
+
+    @pl.when(pl.program_id(0) == 0)
+    def _():
+        lay_out(blocks, panel)
+
+    sums = jnp.dot(panel[...], ints_ref[...], preferred_element_type=jnp.float32)
+    sum_ref[...] = sums * int_keep(screen_ref, ints_shape, pair_size)
+
+
+def away_kernel(ints_shape, pair_size, screen_ref, *refs):
+    blocks, (ints_ref, code_ref, scale_ref, panel) = refs[:-4], refs[-4:]
+
+    @pl.when(pl.program_id(0) == 0)
+    def _():
+        lay_out(blocks, panel)
+
+    keep = int_keep(screen_ref, ints_shape, pair_size)
+    sums = jnp.dot(panel[...], ints_ref[...], preferred_element_type=jnp.float32) * keep
+    for slot in range(sums.shape[0] // TS):
+        rows = slice(slot * TS, (slot + 1) * TS)
+        part = sums[rows]
+        top = jnp.maximum(jnp.max(jnp.abs(part), axis=0, keepdims=True), LEAST_SCALE)
+        code = jnp.round(part * (CODE_MAX / top))
+        code_ref[rows, :] = code.astype(jnp.int32).astype(jnp.int16)
+        scale_ref[slot : slot + 1, :] = top * (1.0 / CODE_MAX)
+
+
+def product(kernel, blocks, integrals, int_screen, pair_size, out_rows_types, name):
+    row_count, depth = blocks[0].shape
+    int_count, ab_count = integrals.shape
+    whole = pl.BlockSpec((row_count, depth), lambda j: (0, 0))
+    return pl.pallas_call(
+        functools.partial(kernel, integrals.shape, pair_size),
+        grid=(ab_count // COLUMN_TILE,),
+        out_shape=[jax.ShapeDtypeStruct((rows, ab_count), dtype) for rows, dtype in out_rows_types],
+        in_specs=[pl.BlockSpec(memory_space=pltpu.SMEM)]
+        + [whole] * len(blocks)
+        + [pl.BlockSpec((int_count, COLUMN_TILE), lambda j: (0, j))],
+        out_specs=[pl.BlockSpec((rows, COLUMN_TILE), lambda j: (0, j)) for rows, _ in out_rows_types],
+        scratch_shapes=[pltpu.VMEM((row_count, int_count), blocks[0].dtype)],
+        compiler_params=pltpu.CompilerParams(vmem_limit_bytes=VMEM_BYTES),
+        cost_estimate=pl.CostEstimate(
+            flops=2 * row_count * int_count * ab_count,
+            bytes_accessed=2 * int_count * ab_count,
+            transcendentals=0,
+        ),
+        name=name,
+    )(int_screen, *blocks, integrals)
+
+
+def join_kernel(screen_ref, own_ref, *refs):
+    chunk_refs, (out_ref, total) = refs[:-2], refs[-2:]
+    grp_index = lax.axis_index("grp")
+    first_tile = grp_index * BLOCK_TILES
+    own_slots, own_count = live_slots(screen_ref, first_tile, grp_index)
+    away_slots, away_count = live_slots(screen_ref, first_tile, 1 - grp_index)
+    total[...] = jnp.zeros_like(total)
+    for slot in range(LIVE_MAX):
+
+        @pl.when(slot < own_count)
+        def _():
+            rows = pl.ds(pl.multiple_of(own_slots[slot] * TS, TS), TS)
+            total[rows, :] = own_ref[slot * TS : (slot + 1) * TS, :]
+
+    for chunk, (first, last) in enumerate(SLOT_CHUNKS):
+        code_ref, scale_ref = chunk_refs[2 * chunk : 2 * chunk + 2]
+        for slot in range(first, last):
+
+            @pl.when(slot < away_count)
+            def _():
+                rows = pl.ds(pl.multiple_of(away_slots[slot] * TS, TS), TS)
+                at = slot - first
+                code = code_ref[at * TS : (at + 1) * TS, :].astype(jnp.float32)
+                total[rows, :] += code * scale_ref[at : at + 1, :]
+
+    out_ref[...] = total[...].astype(out_ref.dtype)
+
+
+def join(amp_screen, own_sum, chunks, row_count):
+    ab_count = own_sum.shape[1]
+    flat = [array for chunk in chunks for array in chunk]
+
+    def tall(rows):
+        return pl.BlockSpec((rows, JOIN_TILE), lambda j: (0, j))
+
+    return pl.pallas_call(
+        join_kernel,
+        grid=(ab_count // JOIN_TILE,),
+        out_shape=jax.ShapeDtypeStruct((row_count, ab_count), jnp.bfloat16),
+        in_specs=[pl.BlockSpec(memory_space=pltpu.SMEM), tall(own_sum.shape[0])]
+        + [tall(array.shape[0]) for array in flat],
+        out_specs=tall(row_count),
+        scratch_shapes=[pltpu.VMEM((row_count, JOIN_TILE), jnp.float32)],
+        compiler_params=pltpu.CompilerParams(vmem_limit_bytes=VMEM_BYTES),
+        name="join",
+    )(amp_screen, own_sum, *flat)
+
+
+def routes(pan_count):
+    half = pan_count // 2
+    places = [(pan, grp) for pan in range(pan_count) for grp in range(2)]
+
+    def at(pan, grp):
+        return pan * 2 + grp
+
+    def away(pan, grp):
+        return pan // half != grp
+
+    def flip(bits):
+        return [(at(pan, grp), at(pan ^ bits, grp)) for pan, grp in places]
+
+    first = [
+        (at(pan, grp), at(pan, 1 - grp) if away(pan, grp) else at((pan + half) % pan_count, grp))
+        for pan, grp in places
+    ]
+    across = [
+        (at(pan, grp), at((pan + half) % pan_count, 1 - grp)) for pan, grp in places if away(pan, grp)
+    ]
+    swap = [(at(pan, grp), at(pan, 1 - grp)) for pan, grp in places]
+    return first, across, swap, flip
+
+
+def gathered(block, flip, block_count):
+    near = [lax.ppermute(block, AXES, flip(bits)) for bits in range(2, block_count, 2)]
+    blocks = [block] + near
+    other = [lax.ppermute(held, AXES, flip(1)) for held in blocks]
+    return [held for pair in zip(blocks, other) for held in pair]
+
+
+def two_group_shards(pan_count, amplitudes, integrals, amp_screen, int_screen):
+    pair_size = TS * TS
+    row_count, col_count = amplitudes.shape
+    block_count = integrals.shape[0] // col_count
+    if (
+        row_count != BLOCK_TILES * TS
+        or amp_screen.shape[1] != 2
+        or integrals.shape[0] != pair_size
+        or block_count * 2 != pan_count
+    ):
+        return shards(amplitudes, integrals, amp_screen, int_screen)
+    first, across, swap, flip = routes(pan_count)
+    is_own = lax.axis_index("pan") // (pan_count // 2) == lax.axis_index("grp")
+
+    picked = pick_live(amplitudes, amp_screen, pair_size)
+    own_parts, chunks = [], []
+    for part in picked:
+        from_first = lax.ppermute(part, AXES, first)
+        from_across = lax.ppermute(part, AXES, across)
+        own_parts.append(jnp.where(is_own, part, from_first))
+        blocks = gathered(jnp.where(is_own, from_first, from_across), flip, block_count)
+        rows = part.shape[0]
+        code, scale = product(
+            away_kernel, blocks, integrals, int_screen, pair_size,
+            ((rows, jnp.int16), (rows // TS, jnp.float32)), "away_product",
+        )
+        chunks.append((lax.ppermute(code, AXES, swap), lax.ppermute(scale, AXES, swap)))
+    own_blocks = gathered(jnp.concatenate(own_parts, axis=0), flip, block_count)
+    (own_sum,) = product(
+        own_kernel, own_blocks, integrals, int_screen, pair_size,
+        ((LIVE_MAX * TS, jnp.float32),), "own_product",
+    )
+    return join(amp_screen, own_sum, chunks, row_count)
 
 
 def column_pairs(piece_width, pair_size, pair_count):
@@ -40,4 +279,8 @@
 def solution(mesh):
     in_specs = (P("grp", "pan"), P("grp", "pan"), P(), P())
     out_specs = P("grp", "pan")
-    return jax.shard_map(shards, mesh=mesh, in_specs=in_specs, out_specs=out_specs, check_vma=False)
+    pan_count, grp_count = mesh.shape["pan"], mesh.shape["grp"]
+    body = shards
+    if grp_count == 2 and pan_count >= 4 and pan_count & (pan_count - 1) == 0:
+        body = functools.partial(two_group_shards, pan_count)
+    return jax.shard_map(body, mesh=mesh, in_specs=in_specs, out_specs=out_specs, check_vma=False)

time: 510 us -> 94.8 us (0.19)
  waiting for transfers between devices: 447 us -> 3.72 us
  Pallas kernels: 0 us -> 47.7 us
  starting transfers between devices: 0.04 us -> 36.3 us
  matrix products: 24.8 us -> 0 us
  other arithmetic: 22.5 us -> 1.89 us
  between operations: 14.1 us -> 0.37 us
    all_gather x2 -> x0, waiting for transfers between devices: 446 us -> none  [the longest x1 380 us: shards(): int_panel = lax.all_gather(integrals * int_keep, 'grp', axis=0, tiled=True)]
    pallas_call x0 -> x5, Pallas kernels: none -> 47.7 us  [the longest x3 33.4 us: product(): pl.pallas_call(functools.partial(kernel, integrals.shape, pair_size), gri...]
    ppermute x0 -> x29, starting transfers between devices: none -> 36.3 us  [the longest x9 16.8 us: gathered(): lax.ppermute(block, AXES, flip(bits))]
    dot_general x2 -> x0, matrix products: 24.8 us -> none  [the longest x1 24.6 us: shards(): summed = jnp.dot(masked, int_panel, preferred_element_type=jnp.float32)]
    mul x2 -> x0, other arithmetic: 22.5 us -> none  [the longest x1 13.8 us: shards(): int_panel = lax.all_gather(integrals * int_keep, 'grp', axis=0, tiled=True)]
  transfers between devices with their start and end apart: 2 -> 29, of which waited for: 2 -> 3; matrix products, arithmetic and copies ran while one was open for 5% -> 2% of each run, Pallas kernels for 0% -> 35%
where the time goes in v1:
time: 94.8 us; the launch traced here: 94.2 us
  Pallas kernels  47.7 us (50%)
  starting transfers between devices  36.3 us (38%)
  local copies, waits for them, and re-layouts  4.18 us (4%)
  waiting for transfers between devices  3.72 us (4%)
  other arithmetic  1.89 us (2%)
    pallas_call x3, Pallas kernels, product(): pl.pallas_call(functools.partial(kernel, integrals.shape, pair_size), gri...  33.4 us
    ppermute x9, starting transfers between devices, gathered(): lax.ppermute(block, AXES, flip(bits))  16.8 us
    ppermute x2, starting transfers between devices, two_group_shards(): from_first = lax.ppermute(part, AXES, first)  10.5 us
    pallas_call x1, Pallas kernels, pick_live(): pl.pallas_call(functools.partial(pick_kernel, pair_size), out_shape=[jax....  9.91 us
    pallas_call x1, Pallas kernels, join(): pl.pallas_call(join_kernel, grid=(ab_count // JOIN_TILE,), out_shape=jax....  4.46 us
    unnamed x59, local copies, waits for them, and re-layouts  4.18 us
    ppermute x9, waiting for transfers between devices, gathered(): lax.ppermute(block, AXES, flip(bits))  3.67 us
    ppermute x2, starting transfers between devices, two_group_shards(): lax.ppermute(code, AXES, swap)  3.39 us
  transfers between devices with their start and end apart: 29, of which 3 were waited for; matrix products, arithmetic and copies ran while one was open for 2% of the time, Pallas kernels for 35%

profile of v1, /device:TPU:0, one launch (start us, length us, event | category | flops | bytes accessed | tf_op | source)
XLA Modules:
  0.0 94.2 jit_solution(7454695773135263339)
XLA Ops:
  0.0 1.3 %copy.6.screen_ref = s32[16,2]{1,0:T(8,128)} copy(s32[16,2]{0,1:T(2,128)} %param.6) | data formatting | bytes 256 | tf_op args[2]
  1.3 9.9 %pick_live.1 = (bf16[128,512]{1,0:T(8,128)(2,1)}, bf16[128,512]{1,0:T(8,128)(2,1)}) custom-call(s32[16,2]{1,0:T(8,128)} %copy.6.screen_ref, bf16[512,512]{1,0:T(8,128)(2,1)} %amps_ref.1), custom_call_target="tpu_custom_call" | custom-call | tf_op jit(solution)/shard_map/pick_live/pallas_call | solution.py:55
  11.3 0.7 collective-permute-start.9
  11.9 6.6 %collective-permute-start = (bf16[128,512]{1,0:T(8,128)(2,1)}, bf16[128,512]{1,0:T(8,128)(2,1)S(1)}, u32[]{:S(2)}, u32[]{:S(2)}) collective-permute-start(bf16[128,512]{1,0:T(8,128)(2,1)} %get-tuple-element.11), channel_id=1, source_target_pairs={{0,16},{1,0},{2,18},{3,2},{4,20},{5,4},{6,22},{7,6},{8,24},{9,8},{... | collective-permute-start | bytes 393224 | tf_op jit(solution)/shard_map/ppermute | solution.py:230
  18.6 0.7 collective-permute-start.19
  19.2 3.8 %collective-permute-start.1 = (bf16[128,512]{1,0:T(8,128)(2,1)}, bf16[128,512]{1,0:T(8,128)(2,1)S(1)}, u32[]{:S(2)}, u32[]{:S(2)}) collective-permute-start(bf16[128,512]{1,0:T(8,128)(2,1)} %get-tuple-element.12), channel_id=1, source_target_pairs={{0,16},{1,0},{2,18},{3,2},{4,20},{5,4},{6,22},{7,6},{8,24},{9,8},{... | collective-permute-start | bytes 393224 | tf_op jit(solution)/shard_map/ppermute | solution.py:230
  23.1 0.0 collective-permute-done.9
  23.1 0.0 collective-permute-done
  23.1 0.9 broadcast_select_fusion.1
  24.0 6.4 %collective-permute-start.15 = (bf16[128,512]{1,0:T(8,128)(2,1)S(1)}, bf16[128,512]{1,0:T(8,128)(2,1)S(1)}, u32[]{:S(2)}, u32[]{:S(2)}) collective-permute-start(bf16[128,512]{1,0:T(8,128)(2,1)S(1)} %get-tuple-element.19.refs_0_), channel_id=1, source_target_pairs={{0,12},{1,13},{2,14},{3,15},{4,8},{5,9},{6,10},{7,11},{8,4},{9,5},... | collective-permute-start | bytes 393224 | tf_op jit(solution)/shard_map/ppermute | solution.py:207
  30.5 0.0 collective-permute-start.13
  30.5 0.6 collective-permute-start.11
  31.1 0.0 collective-permute-done.19
  31.1 0.0 collective-permute-start.10
  31.1 0.0 collective-permute-done.1
  31.1 0.9 broadcast_select_fusion
  32.1 0.0 copy-start.2
  32.1 2.9 %collective-permute-start.25 = (bf16[128,512]{1,0:T(8,128)(2,1)S(1)}, bf16[128,512]{1,0:T(8,128)(2,1)S(1)}, u32[]{:S(2)}, u32[]{:S(2)}) collective-permute-start(bf16[128,512]{1,0:T(8,128)(2,1)S(1)} %get-tuple-element.17.refs_0_), channel_id=1, source_target_pairs={{0,12},{1,13},{2,14},{3,15},{4,8},{5,9},{6,10},{7,11},{8,4},{9,5},... | collective-permute-start | bytes 393224 | tf_op jit(solution)/shard_map/ppermute | solution.py:207
  35.0 0.0 collective-permute-done.15.refs_6_
  35.0 1.8 %collective-permute-start.23 = (bf16[128,512]{1,0:T(8,128)(2,1)S(1)}, bf16[128,512]{1,0:T(8,128)(2,1)S(1)}, u32[]{:S(2)}, u32[]{:S(2)}) collective-permute-start(bf16[128,512]{1,0:T(8,128)(2,1)S(1)} %get-tuple-element.17.refs_0_), channel_id=1, source_target_pairs={{0,8},{1,9},{2,10},{3,11},{4,12},{5,13},{6,14},{7,15},{8,0},{9,1},... | collective-permute-start | bytes 393224 | tf_op jit(solution)/shard_map/ppermute | solution.py:207
  36.8 0.0 collective-permute-done.13.refs_4_
  36.8 1.5 %collective-permute-start.21 = (bf16[128,512]{1,0:T(8,128)(2,1)S(1)}, bf16[128,512]{1,0:T(8,128)(2,1)S(1)}, u32[]{:S(2)}, u32[]{:S(2)}) collective-permute-start(bf16[128,512]{1,0:T(8,128)(2,1)S(1)} %get-tuple-element.17.refs_0_), channel_id=1, source_target_pairs={{0,4},{1,5},{2,6},{3,7},{4,0},{5,1},{6,2},{7,3},{8,12},{9,13},{10,... | collective-permute-start | bytes 393224 | tf_op jit(solution)/shard_map/ppermute | solution.py:207
  38.3 0.0 collective-permute-done.11.refs_2_
  38.3 0.0 collective-permute-start.20
  38.3 0.0 collective-permute-done.10.refs_1_
  38.3 0.5 collective-permute-start.16
  38.8 1.3 %collective-permute-done.25.refs_6_ = bf16[128,512]{1,0:T(8,128)(2,1)S(1)} collective-permute-done((bf16[128,512]{1,0:T(8,128)(2,1)S(1)}, bf16[128,512]{1,0:T(8,128)(2,1)S(1)}, u32[]{:S(2)}, u32[]{:S(2)}) %collective-permute-start.25) | collective-permute-done | bytes 131104 | tf_op jit(solution)/shard_map/ppermute | solution.py:207
  40.2 0.0 collective-permute-start.14
  40.2 1.6 %collective-permute-done.23.refs_4_ = bf16[128,512]{1,0:T(8,128)(2,1)S(1)} collective-permute-done((bf16[128,512]{1,0:T(8,128)(2,1)S(1)}, bf16[128,512]{1,0:T(8,128)(2,1)S(1)}, u32[]{:S(2)}, u32[]{:S(2)}) %collective-permute-start.23) | collective-permute-done | bytes 131104 | tf_op jit(solution)/shard_map/ppermute | solution.py:207
  41.7 0.0 collective-permute-start.26
  41.7 0.7 collective-permute-done.21.refs_2_
  42.5 0.0 collective-permute-start.24
  42.5 0.5 collective-permute-start.22
  43.0 0.0 collective-permute-done.16.refs_7_
  43.1 2.7 %collective-permute-start.7 = (bf16[256,512]{1,0:T(8,128)(2,1)S(1)}, bf16[256,512]{1,0:T(8,128)(2,1)S(1)}, u32[]{:S(2)}, u32[]{:S(2)}) collective-permute-start(bf16[256,512]{1,0:T(8,128)(2,1)S(1)} %pad_maximum_fusion.refs_0_), channel_id=1, source_target_pairs={{0,12},{1,13},{2,14},{3,15},{4,8},{5,9},{6,10},{7,11},{8,4},{9,5},... | collective-permute-start | bytes 786440 | tf_op jit(solution)/shard_map/ppermute | solution.py:207
  45.8 0.0 collective-permute-done.26.refs_7_
  45.8 0.9 collective-permute-start.3
  46.6 0.0 collective-permute-start.2
  46.6 0.0 collective-permute-done.22.refs_3_
  46.7 0.5 collective-permute-start.12
  47.2 0.1 copy-done.23
  47.3 0.1 copy-done.24
  47.4 10.5 %away_product.3 = (s16[128,2048]{1,0:T(8,128)(2,1)}, f32[2,2048]{1,0:T(2,128)}) custom-call(s32[2,8]{1,0:T(2,128)} %screen_ref.7, bf16[128,512]{1,0:T(8,128)(2,1)} %copy-done.2, bf16[128,512]{1,0:T(8,128)(2,1)} %copy-done.21, bf16[128,512]{1,0:T(8,128)(2,1)} %copy-done.20, bf16[128,512]{1,0:T(8,128)(2,1)} %copy-done.24, bf16[128,512]{1,0:T(8,128)(2,1)} %copy-done.19, ...), custom_call_target="tpu_custom_call" | custom-call | flops 2147483648 | bytes 16777216 | tf_op jit(solution)/shard_map/away_product/pallas_call | solution.py:115
  58.0 3.0 %collective-permute-start.27 = (s16[128,2048]{1,0:T(8,128)(2,1)}, s16[128,2048]{1,0:T(8,128)(2,1)S(1)}, u32[]{:S(2)}, u32[]{:S(2)}) collective-permute-start(s16[128,2048]{1,0:T(8,128)(2,1)} %get-tuple-element.15), channel_id=1, source_target_pairs={{0,1},{1,0},{2,3},{3,2},{4,5},{5,4},{6,7},{7,6},{8,9},{9,8},{10,11... | collective-permute-start | bytes 1572872 | tf_op jit(solution)/shard_map/ppermute | solution.py:239
  60.9 0.0 collective-permute-done.7.refs_6_
  60.9 0.2 collective-permute-start.8
  61.1 0.3 collective-permute-start.6
  61.5 0.2 collective-permute-start.4
  61.6 10.5 %away_product.2 = (s16[128,2048]{1,0:T(8,128)(2,1)}, f32[2,2048]{1,0:T(2,128)}) custom-call(s32[2,8]{1,0:T(2,128)} %screen_ref.7, bf16[128,512]{1,0:T(8,128)(2,1)} %copy-done.1, bf16[128,512]{1,0:T(8,128)(2,1)} %copy-done.15, bf16[128,512]{1,0:T(8,128)(2,1)} %copy-done.14, bf16[128,512]{1,0:T(8,128)(2,1)} %copy-done.25, bf16[128,512]{1,0:T(8,128)(2,1)} %copy-done.13, ...), custom_call_target="tpu_custom_call" | custom-call | flops 2147483648 | bytes 16777216 | tf_op jit(solution)/shard_map/away_product/pallas_call | solution.py:115
  72.2 0.4 collective-permute-start.17
  72.7 0.0 collective-permute-done.8.refs_7_
  72.7 1.7 %collective-permute-start.18 = (f32[2,2048]{1,0:T(2,128)}, f32[2,2048]{1,0:T(2,128)S(1)}, u32[]{:S(2)}, u32[]{:S(2)}) collective-permute-start(f32[2,2048]{1,0:T(2,128)} %get-tuple-element.14), channel_id=1, source_target_pairs={{0,1},{1,0},{2,3},{3,2},{4,5},{5,4},{6,7},{7,6},{8,9},{9,8},{10,11... | collective-permute-start | bytes 49160 | tf_op jit(solution)/shard_map/ppermute | solution.py:239
  74.3 0.4 collective-permute-start.28
  74.8 0.3 copy-done.10
  75.1 0.7 copy-done.11
  75.8 12.3 %own_product.1.own_ref = f32[256,2048]{1,0:T(8,128)} custom-call(s32[2,8]{1,0:T(2,128)} %screen_ref.7, bf16[256,512]{1,0:T(8,128)(2,1)} %copy-done, bf16[256,512]{1,0:T(8,128)(2,1)} %copy-done.8, bf16[256,512]{1,0:T(8,128)(2,1)} %copy-done.7, bf16[256,512]{1,0:T(8,128)(2,1)} %copy-done.11, bf16[256,512]{1,0:T(8,128)(2,1)} %copy-done.6, ...), custom_call_target="tpu_custom_call" | custom-call | flops 4294967296 | bytes 16777216 | tf_op jit(solution)/shard_map/own_product/pallas_call | solution.py:115
  88.1 0.0 collective-permute-done.18.refs_1_
  88.1 0.0 collective-permute-done.28.refs_3_
  88.1 0.0 collective-permute-done.27.refs_2_
  88.1 0.5 copy-done.26
  88.7 0.0 copy-done.27
  88.7 0.2 copy-done.3
  88.9 0.8 copy-done.4
  89.7 4.5 %join.1 = bf16[512,2048]{1,0:T(8,128)(2,1)} custom-call(s32[16,2]{1,0:T(8,128)} %copy.6.screen_ref, f32[256,2048]{1,0:T(8,128)} %own_product.1.own_ref, s16[128,2048]{1,0:T(8,128)(2,1)} %copy-done.4, f32[2,2048]{1,0:T(2,128)} %copy-done.26, s16[128,2048]{1,0:T(8,128)(2,1)} %copy-done.3, f32[2,2048]{1,0:T(2,128)} %copy-done.27), custom_call_target="tpu_custom_call" | custom-call | tf_op jit(solution)/shard_map/join/pallas_call | solution.py:169
  (61 shorter events, 0.1 us)
Async XLA Ops:
  11.3 11.8 %collective-permute-start.9 = (bf16[128,512]{1,0:T(8,128)(2,1)}, bf16[128,512]{1,0:T(8,128)(2,1)S(1)}, u32[]{:S(2)}, u32[]{:S(2)}) collective-permute-start(bf16[128,512]{1,0:T(8,128)(2,1)} %get-tuple-element.11), channel_id=1, source_target_pairs={{1,16},{3,18},{5,20},{7,22},{9,24},{11,26},{13,28},{15,30},{16,1},... | collective-permute-start | bytes 393224 | tf_op jit(solution)/shard_map/ppermute | solution.py:231
  11.9 11.1 %collective-permute-start = (bf16[128,512]{1,0:T(8,128)(2,1)}, bf16[128,512]{1,0:T(8,128)(2,1)S(1)}, u32[]{:S(2)}, u32[]{:S(2)}) collective-permute-start(bf16[128,512]{1,0:T(8,128)(2,1)} %get-tuple-element.11), channel_id=1, source_target_pairs={{0,16},{1,0},{2,18},{3,2},{4,20},{5,4},{6,22},{7,6},{8,24},{9,8},{... | collective-permute-start | bytes 393224 | tf_op jit(solution)/shard_map/ppermute | solution.py:230
  18.6 12.5 %collective-permute-start.19 = (bf16[128,512]{1,0:T(8,128)(2,1)}, bf16[128,512]{1,0:T(8,128)(2,1)S(1)}, u32[]{:S(2)}, u32[]{:S(2)}) collective-permute-start(bf16[128,512]{1,0:T(8,128)(2,1)} %get-tuple-element.12), channel_id=1, source_target_pairs={{1,16},{3,18},{5,20},{7,22},{9,24},{11,26},{13,28},{15,30},{16,1},... | collective-permute-start | bytes 393224 | tf_op jit(solution)/shard_map/ppermute | solution.py:231
  19.2 11.9 %collective-permute-start.1 = (bf16[128,512]{1,0:T(8,128)(2,1)}, bf16[128,512]{1,0:T(8,128)(2,1)S(1)}, u32[]{:S(2)}, u32[]{:S(2)}) collective-permute-start(bf16[128,512]{1,0:T(8,128)(2,1)} %get-tuple-element.12), channel_id=1, source_target_pairs={{0,16},{1,0},{2,18},{3,2},{4,20},{5,4},{6,22},{7,6},{8,24},{9,8},{... | collective-permute-start | bytes 393224 | tf_op jit(solution)/shard_map/ppermute | solution.py:230
  24.0 33.9 %copy-start.1 = (bf16[128,512]{1,0:T(8,128)(2,1)}, bf16[128,512]{1,0:T(8,128)(2,1)S(1)}, u32[]{:S(2)}) copy-start(bf16[128,512]{1,0:T(8,128)(2,1)S(1)} %get-tuple-element.19.refs_0_) | copy-start | bytes 393220
  24.0 11.0 %collective-permute-start.15 = (bf16[128,512]{1,0:T(8,128)(2,1)S(1)}, bf16[128,512]{1,0:T(8,128)(2,1)S(1)}, u32[]{:S(2)}, u32[]{:S(2)}) collective-permute-start(bf16[128,512]{1,0:T(8,128)(2,1)S(1)} %get-tuple-element.19.refs_0_), channel_id=1, source_target_pairs={{0,12},{1,13},{2,14},{3,15},{4,8},{5,9},{6,10},{7,11},{8,4},{9,5},... | collective-permute-start | bytes 393224 | tf_op jit(solution)/shard_map/ppermute | solution.py:207
  30.5 6.4 %collective-permute-start.13 = (bf16[128,512]{1,0:T(8,128)(2,1)S(1)}, bf16[128,512]{1,0:T(8,128)(2,1)S(1)}, u32[]{:S(2)}, u32[]{:S(2)}) collective-permute-start(bf16[128,512]{1,0:T(8,128)(2,1)S(1)} %get-tuple-element.19.refs_0_), channel_id=1, source_target_pairs={{0,8},{1,9},{2,10},{3,11},{4,12},{5,13},{6,14},{7,15},{8,0},{9,1},... | collective-permute-start | bytes 393224 | tf_op jit(solution)/shard_map/ppermute | solution.py:207
  30.5 7.8 %collective-permute-start.11 = (bf16[128,512]{1,0:T(8,128)(2,1)S(1)}, bf16[128,512]{1,0:T(8,128)(2,1)S(1)}, u32[]{:S(2)}, u32[]{:S(2)}) collective-permute-start(bf16[128,512]{1,0:T(8,128)(2,1)S(1)} %get-tuple-element.19.refs_0_), channel_id=1, source_target_pairs={{0,4},{1,5},{2,6},{3,7},{4,0},{5,1},{6,2},{7,3},{8,12},{9,13},{10,... | collective-permute-start | bytes 393224 | tf_op jit(solution)/shard_map/ppermute | solution.py:207
  31.1 7.2 %collective-permute-start.10 = (bf16[128,512]{1,0:T(8,128)(2,1)S(1)}, bf16[128,512]{1,0:T(8,128)(2,1)S(1)}, u32[]{:S(2)}, u32[]{:S(2)}) collective-permute-start(bf16[128,512]{1,0:T(8,128)(2,1)S(1)} %get-tuple-element.19.refs_0_), channel_id=1, source_target_pairs={{0,2},{1,3},{2,0},{3,1},{4,6},{5,7},{6,4},{7,5},{8,10},{9,11},{10,... | collective-permute-start | bytes 393224 | tf_op jit(solution)/shard_map/ppermute | solution.py:209
  32.1 15.1 %copy-start.2 = (bf16[128,512]{1,0:T(8,128)(2,1)}, bf16[128,512]{1,0:T(8,128)(2,1)S(1)}, u32[]{:S(2)}) copy-start(bf16[128,512]{1,0:T(8,128)(2,1)S(1)} %get-tuple-element.17.refs_0_) | copy-start | bytes 393220
  32.1 8.1 %collective-permute-start.25 = (bf16[128,512]{1,0:T(8,128)(2,1)S(1)}, bf16[128,512]{1,0:T(8,128)(2,1)S(1)}, u32[]{:S(2)}, u32[]{:S(2)}) collective-permute-start(bf16[128,512]{1,0:T(8,128)(2,1)S(1)} %get-tuple-element.17.refs_0_), channel_id=1, source_target_pairs={{0,12},{1,13},{2,14},{3,15},{4,8},{5,9},{6,10},{7,11},{8,4},{9,5},... | collective-permute-start | bytes 393224 | tf_op jit(solution)/shard_map/ppermute | solution.py:207
  35.0 22.9 %copy-start.12 = (bf16[128,512]{1,0:T(8,128)(2,1)}, bf16[128,512]{1,0:T(8,128)(2,1)S(1)}, u32[]{:S(2)}) copy-start(bf16[128,512]{1,0:T(8,128)(2,1)S(1)} %collective-permute-done.15.refs_6_) | copy-start | bytes 393220
  35.0 6.8 %collective-permute-start.23 = (bf16[128,512]{1,0:T(8,128)(2,1)S(1)}, bf16[128,512]{1,0:T(8,128)(2,1)S(1)}, u32[]{:S(2)}, u32[]{:S(2)}) collective-permute-start(bf16[128,512]{1,0:T(8,128)(2,1)S(1)} %get-tuple-element.17.refs_0_), channel_id=1, source_target_pairs={{0,8},{1,9},{2,10},{3,11},{4,12},{5,13},{6,14},{7,15},{8,0},{9,1},... | collective-permute-start | bytes 393224 | tf_op jit(solution)/shard_map/ppermute | solution.py:207
  36.8 21.1 %copy-start.13 = (bf16[128,512]{1,0:T(8,128)(2,1)}, bf16[128,512]{1,0:T(8,128)(2,1)S(1)}, u32[]{:S(2)}) copy-start(bf16[128,512]{1,0:T(8,128)(2,1)S(1)} %collective-permute-done.13.refs_4_) | copy-start | bytes 393220
  36.8 5.7 %collective-permute-start.21 = (bf16[128,512]{1,0:T(8,128)(2,1)S(1)}, bf16[128,512]{1,0:T(8,128)(2,1)S(1)}, u32[]{:S(2)}, u32[]{:S(2)}) collective-permute-start(bf16[128,512]{1,0:T(8,128)(2,1)S(1)} %get-tuple-element.17.refs_0_), channel_id=1, source_target_pairs={{0,4},{1,5},{2,6},{3,7},{4,0},{5,1},{6,2},{7,3},{8,12},{9,13},{10,... | collective-permute-start | bytes 393224 | tf_op jit(solution)/shard_map/ppermute | solution.py:207
  38.3 19.6 %copy-start.14 = (bf16[128,512]{1,0:T(8,128)(2,1)}, bf16[128,512]{1,0:T(8,128)(2,1)S(1)}, u32[]{:S(2)}) copy-start(bf16[128,512]{1,0:T(8,128)(2,1)S(1)} %collective-permute-done.11.refs_2_) | copy-start | bytes 393220
  38.3 4.2 %collective-permute-start.20 = (bf16[128,512]{1,0:T(8,128)(2,1)S(1)}, bf16[128,512]{1,0:T(8,128)(2,1)S(1)}, u32[]{:S(2)}, u32[]{:S(2)}) collective-permute-start(bf16[128,512]{1,0:T(8,128)(2,1)S(1)} %get-tuple-element.17.refs_0_), channel_id=1, source_target_pairs={{0,2},{1,3},{2,0},{3,1},{4,6},{5,7},{6,4},{7,5},{8,10},{9,11},{10,... | collective-permute-start | bytes 393224 | tf_op jit(solution)/shard_map/ppermute | solution.py:209
  38.3 19.6 %copy-start.15 = (bf16[128,512]{1,0:T(8,128)(2,1)}, bf16[128,512]{1,0:T(8,128)(2,1)S(1)}, u32[]{:S(2)}) copy-start(bf16[128,512]{1,0:T(8,128)(2,1)S(1)} %collective-permute-done.10.refs_1_) | copy-start | bytes 393220
  38.3 4.7 %collective-permute-start.16 = (bf16[128,512]{1,0:T(8,128)(2,1)S(1)}, bf16[128,512]{1,0:T(8,128)(2,1)S(1)}, u32[]{:S(2)}, u32[]{:S(2)}) collective-permute-start(bf16[128,512]{1,0:T(8,128)(2,1)S(1)} %collective-permute-done.15.refs_6_), channel_id=1, source_target_pairs={{0,2},{1,3},{2,0},{3,1},{4,6},{5,7},{6,4},{7,5},{8,10},{9,11},{10,... | collective-permute-start | bytes 393224 | tf_op jit(solution)/shard_map/ppermute | solution.py:209
  40.2 7.0 %copy-start.18 = (bf16[128,512]{1,0:T(8,128)(2,1)}, bf16[128,512]{1,0:T(8,128)(2,1)S(1)}, u32[]{:S(2)}) copy-start(bf16[128,512]{1,0:T(8,128)(2,1)S(1)} %collective-permute-done.25.refs_6_) | copy-start | bytes 393220
  40.2 5.6 %collective-permute-start.14 = (bf16[128,512]{1,0:T(8,128)(2,1)S(1)}, bf16[128,512]{1,0:T(8,128)(2,1)S(1)}, u32[]{:S(2)}, u32[]{:S(2)}) collective-permute-start(bf16[128,512]{1,0:T(8,128)(2,1)S(1)} %collective-permute-done.13.refs_4_), channel_id=1, source_target_pairs={{0,2},{1,3},{2,0},{3,1},{4,6},{5,7},{6,4},{7,5},{8,10},{9,11},{10,... | collective-permute-start | bytes 393224 | tf_op jit(solution)/shard_map/ppermute | solution.py:209
  41.7 5.4 %copy-start.19 = (bf16[128,512]{1,0:T(8,128)(2,1)}, bf16[128,512]{1,0:T(8,128)(2,1)S(1)}, u32[]{:S(2)}) copy-start(bf16[128,512]{1,0:T(8,128)(2,1)S(1)} %collective-permute-done.23.refs_4_) | copy-start | bytes 393220
  41.7 4.0 %collective-permute-start.26 = (bf16[128,512]{1,0:T(8,128)(2,1)S(1)}, bf16[128,512]{1,0:T(8,128)(2,1)S(1)}, u32[]{:S(2)}, u32[]{:S(2)}) collective-permute-start(bf16[128,512]{1,0:T(8,128)(2,1)S(1)} %collective-permute-done.25.refs_6_), channel_id=1, source_target_pairs={{0,2},{1,3},{2,0},{3,1},{4,6},{5,7},{6,4},{7,5},{8,10},{9,11},{10,... | collective-permute-start | bytes 393224 | tf_op jit(solution)/shard_map/ppermute | solution.py:209
  42.5 4.7 %copy-start.20 = (bf16[128,512]{1,0:T(8,128)(2,1)}, bf16[128,512]{1,0:T(8,128)(2,1)S(1)}, u32[]{:S(2)}) copy-start(bf16[128,512]{1,0:T(8,128)(2,1)S(1)} %collective-permute-done.21.refs_2_) | copy-start | bytes 393220
  42.5 4.1 %collective-permute-start.24 = (bf16[128,512]{1,0:T(8,128)(2,1)S(1)}, bf16[128,512]{1,0:T(8,128)(2,1)S(1)}, u32[]{:S(2)}, u32[]{:S(2)}) collective-permute-start(bf16[128,512]{1,0:T(8,128)(2,1)S(1)} %collective-permute-done.23.refs_4_), channel_id=1, source_target_pairs={{0,2},{1,3},{2,0},{3,1},{4,6},{5,7},{6,4},{7,5},{8,10},{9,11},{10,... | collective-permute-start | bytes 393224 | tf_op jit(solution)/shard_map/ppermute | solution.py:209
  42.5 4.7 %copy-start.21 = (bf16[128,512]{1,0:T(8,128)(2,1)}, bf16[128,512]{1,0:T(8,128)(2,1)S(1)}, u32[]{:S(2)}) copy-start(bf16[128,512]{1,0:T(8,128)(2,1)S(1)} %collective-permute-done.20.refs_1_) | copy-start | bytes 393220
  42.5 4.1 %collective-permute-start.22 = (bf16[128,512]{1,0:T(8,128)(2,1)S(1)}, bf16[128,512]{1,0:T(8,128)(2,1)S(1)}, u32[]{:S(2)}, u32[]{:S(2)}) collective-permute-start(bf16[128,512]{1,0:T(8,128)(2,1)S(1)} %collective-permute-done.21.refs_2_), channel_id=1, source_target_pairs={{0,2},{1,3},{2,0},{3,1},{4,6},{5,7},{6,4},{7,5},{8,10},{9,11},{10,... | collective-permute-start | bytes 393224 | tf_op jit(solution)/shard_map/ppermute | solution.py:209
  43.0 14.9 %copy-start = (bf16[256,512]{1,0:T(8,128)(2,1)}, bf16[256,512]{1,0:T(8,128)(2,1)S(1)}, u32[]{:S(2)}) copy-start(bf16[256,512]{1,0:T(8,128)(2,1)S(1)} %pad_maximum_fusion.refs_0_) | copy-start | bytes 786436
  43.1 14.9 %copy-start.16 = (bf16[128,512]{1,0:T(8,128)(2,1)}, bf16[128,512]{1,0:T(8,128)(2,1)S(1)}, u32[]{:S(2)}) copy-start(bf16[128,512]{1,0:T(8,128)(2,1)S(1)} %collective-permute-done.16.refs_7_) | copy-start | bytes 393220
  43.1 17.9 %collective-permute-start.7 = (bf16[256,512]{1,0:T(8,128)(2,1)S(1)}, bf16[256,512]{1,0:T(8,128)(2,1)S(1)}, u32[]{:S(2)}, u32[]{:S(2)}) collective-permute-start(bf16[256,512]{1,0:T(8,128)(2,1)S(1)} %pad_maximum_fusion.refs_0_), channel_id=1, source_target_pairs={{0,12},{1,13},{2,14},{3,15},{4,8},{5,9},{6,10},{7,11},{8,4},{9,5},... | collective-permute-start | bytes 786440 | tf_op jit(solution)/shard_map/ppermute | solution.py:207
  45.7 12.2 %copy-start.17 = (bf16[128,512]{1,0:T(8,128)(2,1)}, bf16[128,512]{1,0:T(8,128)(2,1)S(1)}, u32[]{:S(2)}) copy-start(bf16[128,512]{1,0:T(8,128)(2,1)S(1)} %collective-permute-done.14.refs_5_) | copy-start | bytes 393220
  45.8 15.4 %collective-permute-start.5 = (bf16[256,512]{1,0:T(8,128)(2,1)S(1)}, bf16[256,512]{1,0:T(8,128)(2,1)S(1)}, u32[]{:S(2)}, u32[]{:S(2)}) collective-permute-start(bf16[256,512]{1,0:T(8,128)(2,1)S(1)} %pad_maximum_fusion.refs_0_), channel_id=1, source_target_pairs={{0,8},{1,9},{2,10},{3,11},{4,12},{5,13},{6,14},{7,15},{8,0},{9,1},... | collective-permute-start | bytes 786440 | tf_op jit(solution)/shard_map/ppermute | solution.py:207
  45.8 1.4 %copy-start.22 = (bf16[128,512]{1,0:T(8,128)(2,1)}, bf16[128,512]{1,0:T(8,128)(2,1)S(1)}, u32[]{:S(2)}) copy-start(bf16[128,512]{1,0:T(8,128)(2,1)S(1)} %collective-permute-done.26.refs_7_) | copy-start | bytes 393220
  45.8 15.7 %collective-permute-start.3 = (bf16[256,512]{1,0:T(8,128)(2,1)S(1)}, bf16[256,512]{1,0:T(8,128)(2,1)S(1)}, u32[]{:S(2)}, u32[]{:S(2)}) collective-permute-start(bf16[256,512]{1,0:T(8,128)(2,1)S(1)} %pad_maximum_fusion.refs_0_), channel_id=1, source_target_pairs={{0,4},{1,5},{2,6},{3,7},{4,0},{5,1},{6,2},{7,3},{8,12},{9,13},{10,... | collective-permute-start | bytes 786440 | tf_op jit(solution)/shard_map/ppermute | solution.py:207
  46.6 0.6 copy-start.23
  46.6 25.6 %collective-permute-start.2 = (bf16[256,512]{1,0:T(8,128)(2,1)S(1)}, bf16[256,512]{1,0:T(8,128)(2,1)S(1)}, u32[]{:S(2)}, u32[]{:S(2)}) collective-permute-start(bf16[256,512]{1,0:T(8,128)(2,1)S(1)} %pad_maximum_fusion.refs_0_), channel_id=1, source_target_pairs={{0,2},{1,3},{2,0},{3,1},{4,6},{5,7},{6,4},{7,5},{8,10},{9,11},{10,... | collective-permute-start | bytes 786440 | tf_op jit(solution)/shard_map/ppermute | solution.py:209
  46.7 0.7 copy-start.24
  46.7 11.3 %collective-permute-start.12 = (bf16[128,512]{1,0:T(8,128)(2,1)S(1)}, bf16[128,512]{1,0:T(8,128)(2,1)S(1)}, u32[]{:S(2)}, u32[]{:S(2)}) collective-permute-start(bf16[128,512]{1,0:T(8,128)(2,1)S(1)} %collective-permute-done.11.refs_2_), channel_id=1, source_target_pairs={{0,2},{1,3},{2,0},{3,1},{4,6},{5,7},{6,4},{7,5},{8,10},{9,11},{10,... | collective-permute-start | bytes 393224 | tf_op jit(solution)/shard_map/ppermute | solution.py:209
  58.0 3.7 %copy-start.25 = (bf16[128,512]{1,0:T(8,128)(2,1)}, bf16[128,512]{1,0:T(8,128)(2,1)S(1)}, u32[]{:S(2)}) copy-start(bf16[128,512]{1,0:T(8,128)(2,1)S(1)} %collective-permute-done.12.refs_3_) | copy-start | bytes 393220
  58.0 16.4 %copy-start.28 = (f32[2,2048]{1,0:T(2,128)S(1)}, f32[2,2048]{1,0:T(2,128)}, u32[]{:S(2)}) copy-start(f32[2,2048]{1,0:T(2,128)} %get-tuple-element.16) | copy-start | bytes 49156
  58.0 30.1 %collective-permute-start.27 = (s16[128,2048]{1,0:T(8,128)(2,1)}, s16[128,2048]{1,0:T(8,128)(2,1)S(1)}, u32[]{:S(2)}, u32[]{:S(2)}) collective-permute-start(s16[128,2048]{1,0:T(8,128)(2,1)} %get-tuple-element.15), channel_id=1, source_target_pairs={{0,1},{1,0},{2,3},{3,2},{4,5},{5,4},{6,7},{7,6},{8,9},{9,8},{10,11... | collective-permute-start | bytes 1572872 | tf_op jit(solution)/shard_map/ppermute | solution.py:239
  60.9 11.2 %copy-start.5 = (bf16[256,512]{1,0:T(8,128)(2,1)}, bf16[256,512]{1,0:T(8,128)(2,1)S(1)}, u32[]{:S(2)}) copy-start(bf16[256,512]{1,0:T(8,128)(2,1)S(1)} %collective-permute-done.7.refs_6_) | copy-start | bytes 786436
  60.9 11.7 %collective-permute-start.8 = (bf16[256,512]{1,0:T(8,128)(2,1)S(1)}, bf16[256,512]{1,0:T(8,128)(2,1)S(1)}, u32[]{:S(2)}, u32[]{:S(2)}) collective-permute-start(bf16[256,512]{1,0:T(8,128)(2,1)S(1)} %collective-permute-done.7.refs_6_), channel_id=1, source_target_pairs={{0,2},{1,3},{2,0},{3,1},{4,6},{5,7},{6,4},{7,5},{8,10},{9,11},{10,... | collective-permute-start | bytes 786440 | tf_op jit(solution)/shard_map/ppermute | solution.py:209
  61.1 11.1 %copy-start.6 = (bf16[256,512]{1,0:T(8,128)(2,1)}, bf16[256,512]{1,0:T(8,128)(2,1)S(1)}, u32[]{:S(2)}) copy-start(bf16[256,512]{1,0:T(8,128)(2,1)S(1)} %collective-permute-done.5.refs_4_) | copy-start | bytes 786436
  61.1 13.2 %collective-permute-start.6 = (bf16[256,512]{1,0:T(8,128)(2,1)S(1)}, bf16[256,512]{1,0:T(8,128)(2,1)S(1)}, u32[]{:S(2)}, u32[]{:S(2)}) collective-permute-start(bf16[256,512]{1,0:T(8,128)(2,1)S(1)} %collective-permute-done.5.refs_4_), channel_id=1, source_target_pairs={{0,2},{1,3},{2,0},{3,1},{4,6},{5,7},{6,4},{7,5},{8,10},{9,11},{10,... | collective-permute-start | bytes 786440 | tf_op jit(solution)/shard_map/ppermute | solution.py:209
  61.5 10.7 %copy-start.7 = (bf16[256,512]{1,0:T(8,128)(2,1)}, bf16[256,512]{1,0:T(8,128)(2,1)S(1)}, u32[]{:S(2)}) copy-start(bf16[256,512]{1,0:T(8,128)(2,1)S(1)} %collective-permute-done.3.refs_2_) | copy-start | bytes 786436
  61.5 13.3 %collective-permute-start.4 = (bf16[256,512]{1,0:T(8,128)(2,1)S(1)}, bf16[256,512]{1,0:T(8,128)(2,1)S(1)}, u32[]{:S(2)}, u32[]{:S(2)}) collective-permute-start(bf16[256,512]{1,0:T(8,128)(2,1)S(1)} %collective-permute-done.3.refs_2_), channel_id=1, source_target_pairs={{0,2},{1,3},{2,0},{3,1},{4,6},{5,7},{6,4},{7,5},{8,10},{9,11},{10,... | collective-permute-start | bytes 786440 | tf_op jit(solution)/shard_map/ppermute | solution.py:209
  72.2 2.6 %copy-start.8 = (bf16[256,512]{1,0:T(8,128)(2,1)}, bf16[256,512]{1,0:T(8,128)(2,1)S(1)}, u32[]{:S(2)}) copy-start(bf16[256,512]{1,0:T(8,128)(2,1)S(1)} %collective-permute-done.2.refs_1_) | copy-start | bytes 786436
  72.2 15.9 %collective-permute-start.17 = (s16[128,2048]{1,0:T(8,128)(2,1)}, s16[128,2048]{1,0:T(8,128)(2,1)S(1)}, u32[]{:S(2)}, u32[]{:S(2)}) collective-permute-start(s16[128,2048]{1,0:T(8,128)(2,1)} %get-tuple-element.13), channel_id=1, source_target_pairs={{0,1},{1,0},{2,3},{3,2},{4,5},{5,4},{6,7},{7,6},{8,9},{9,8},{10,11... | collective-permute-start | bytes 1572872 | tf_op jit(solution)/shard_map/ppermute | solution.py:239
  72.7 2.1 %copy-start.9 = (bf16[256,512]{1,0:T(8,128)(2,1)}, bf16[256,512]{1,0:T(8,128)(2,1)S(1)}, u32[]{:S(2)}) copy-start(bf16[256,512]{1,0:T(8,128)(2,1)S(1)} %collective-permute-done.8.refs_7_) | copy-start | bytes 786436
  72.7 15.4 %collective-permute-start.18 = (f32[2,2048]{1,0:T(2,128)}, f32[2,2048]{1,0:T(2,128)S(1)}, u32[]{:S(2)}, u32[]{:S(2)}) collective-permute-start(f32[2,2048]{1,0:T(2,128)} %get-tuple-element.14), channel_id=1, source_target_pairs={{0,1},{1,0},{2,3},{3,2},{4,5},{5,4},{6,7},{7,6},{8,9},{9,8},{10,11... | collective-permute-start | bytes 49160 | tf_op jit(solution)/shard_map/ppermute | solution.py:239
  74.3 0.7 copy-start.10
  74.3 13.7 %collective-permute-start.28 = (f32[2,2048]{1,0:T(2,128)S(1)}, f32[2,2048]{1,0:T(2,128)S(1)}, u32[]{:S(2)}, u32[]{:S(2)}) collective-permute-start(f32[2,2048]{1,0:T(2,128)S(1)} %copy-done.28), channel_id=1, source_target_pairs={{0,1},{1,0},{2,3},{3,2},{4,5},{5,4},{6,7},{7,6},{8,9},{9,8},{10,11... | collective-permute-start | bytes 49160 | tf_op jit(solution)/shard_map/ppermute | solution.py:239
  75.1 0.7 copy-start.11
  88.1 0.6 copy-start.26
  88.1 0.6 copy-start.27
  88.1 0.8 copy-start.3
  88.9 0.8 copy-start.4

commit v2 on v1

--- a/solution.py
+++ b/solution.py
@@ -16,7 +16,9 @@
 LEAST_SCALE = 1e-33
 COLUMN_TILE = 256
 JOIN_TILE = 512
-VMEM_BYTES = 56 * 1024 * 1024
+SMALL_VMEM = 8 * 1024 * 1024
+PRODUCT_VMEM = 16 * 1024 * 1024
+WHOLE = pl.BlockSpec(memory_space=pltpu.VMEM)
 
 
 def live_slots(screen_ref, first_tile, column):
@@ -30,8 +32,11 @@
     return slots, count
 
 
-def pick_kernel(pair_size, screen_ref, amps_ref, *rest):
-    picked_refs, sem = rest[:-1], rest[-1]
+def pick_kernel(pair_size, screen_hbm, amps_ref, *rest):
+    picked_refs, (screen_ref, screen_sem, sem) = rest[:-3], rest[-3:]
+    screen_copy = pltpu.make_async_copy(screen_hbm, screen_ref, screen_sem)
+    screen_copy.start()
+    screen_copy.wait()
     column = lax.axis_index("pan") * amps_ref.shape[1] // pair_size
     slots, _ = live_slots(screen_ref, lax.axis_index("grp") * BLOCK_TILES, column)
     copies = []
@@ -58,9 +63,14 @@
             jax.ShapeDtypeStruct(((last - first) * TS, amplitudes.shape[1]), amplitudes.dtype)
             for first, last in SLOT_CHUNKS
         ],
-        in_specs=[pl.BlockSpec(memory_space=pltpu.SMEM), pl.BlockSpec(memory_space=pl.ANY)],
-        out_specs=[pl.BlockSpec(memory_space=pl.ANY)] * len(SLOT_CHUNKS),
-        scratch_shapes=[pltpu.SemaphoreType.DMA((LIVE_MAX,))],
+        in_specs=[pl.BlockSpec(memory_space=pl.ANY)] * 2,
+        out_specs=[WHOLE] * len(SLOT_CHUNKS),
+        scratch_shapes=[
+            pltpu.SMEM(amp_screen.shape, amp_screen.dtype),
+            pltpu.SemaphoreType.DMA,
+            pltpu.SemaphoreType.DMA((LIVE_MAX,)),
+        ],
+        compiler_params=pltpu.CompilerParams(vmem_limit_bytes=SMALL_VMEM),
         name="pick_live",
     )(amp_screen, amplitudes)
 
@@ -79,88 +89,79 @@
     return screen_ref[in_pair, out_pair].astype(jnp.float32)
 
 
-def own_kernel(ints_shape, pair_size, screen_ref, *refs):
-    blocks, (ints_ref, sum_ref, panel) = refs[:-3], refs[-3:]
-
-    @pl.when(pl.program_id(0) == 0)
-    def _():
-        lay_out(blocks, panel)
-
-    sums = jnp.dot(panel[...], ints_ref[...], preferred_element_type=jnp.float32)
-    sum_ref[...] = sums * int_keep(screen_ref, ints_shape, pair_size)
-
-
-def away_kernel(ints_shape, pair_size, screen_ref, *refs):
+def own_kernel(pair_size, int_screen_ref, amp_screen_ref, *refs):
+    blocks, (ints_ref, total_ref, panel) = refs[:-3], refs[-3:]
+    grp_index = lax.axis_index("grp")
+    slots, count = live_slots(amp_screen_ref, grp_index * BLOCK_TILES, grp_index)
+    keep = int_keep(int_screen_ref, ints_ref.shape, pair_size)
+    lay_out(blocks, panel)
+    total_ref[...] = jnp.zeros_like(total_ref)
+    for column in range(0, ints_ref.shape[1], COLUMN_TILE):
+        columns = slice(column, column + COLUMN_TILE)
+        sums = jnp.dot(panel[...], ints_ref[:, columns], preferred_element_type=jnp.float32) * keep
+        for slot in range(LIVE_MAX):
+
+            @pl.when(slot < count)
+            def _():
+                rows = pl.ds(pl.multiple_of(slots[slot] * TS, TS), TS)
+                total_ref[rows, columns] = sums[slot * TS : (slot + 1) * TS]
+
+
+def away_kernel(pair_size, int_screen_ref, *refs):
     blocks, (ints_ref, code_ref, scale_ref, panel) = refs[:-4], refs[-4:]
-
-    @pl.when(pl.program_id(0) == 0)
-    def _():
-        lay_out(blocks, panel)
-
-    keep = int_keep(screen_ref, ints_shape, pair_size)
-    sums = jnp.dot(panel[...], ints_ref[...], preferred_element_type=jnp.float32) * keep
-    for slot in range(sums.shape[0] // TS):
-        rows = slice(slot * TS, (slot + 1) * TS)
-        part = sums[rows]
-        top = jnp.maximum(jnp.max(jnp.abs(part), axis=0, keepdims=True), LEAST_SCALE)
-        code = jnp.round(part * (CODE_MAX / top))
-        code_ref[rows, :] = code.astype(jnp.int32).astype(jnp.int16)
-        scale_ref[slot : slot + 1, :] = top * (1.0 / CODE_MAX)
-
-
-def product(kernel, blocks, integrals, int_screen, pair_size, out_rows_types, name):
-    row_count, depth = blocks[0].shape
-    int_count, ab_count = integrals.shape
-    whole = pl.BlockSpec((row_count, depth), lambda j: (0, 0))
+    keep = int_keep(int_screen_ref, ints_ref.shape, pair_size)
+    lay_out(blocks, panel)
+    for column in range(0, ints_ref.shape[1], COLUMN_TILE):
+        columns = slice(column, column + COLUMN_TILE)
+        sums = jnp.dot(panel[...], ints_ref[:, columns], preferred_element_type=jnp.float32) * keep
+        for slot in range(sums.shape[0] // TS):
+            rows = slice(slot * TS, (slot + 1) * TS)
+            part = sums[rows]
+            top = jnp.maximum(jnp.max(jnp.abs(part), axis=0, keepdims=True), LEAST_SCALE)
+            code = jnp.round(part * (CODE_MAX / top))
+            code_ref[rows, columns] = code.astype(jnp.int32).astype(jnp.int16)
+            scale_ref[slot : slot + 1, columns] = top * (1.0 / CODE_MAX)
+
+
+def product(kernel, screens, blocks, ints, pair_size, out_rows_types, name):
+    row_count = blocks[0].shape[0]
+    int_count, ab_count = ints.shape
     return pl.pallas_call(
-        functools.partial(kernel, integrals.shape, pair_size),
-        grid=(ab_count // COLUMN_TILE,),
+        functools.partial(kernel, pair_size),
         out_shape=[jax.ShapeDtypeStruct((rows, ab_count), dtype) for rows, dtype in out_rows_types],
-        in_specs=[pl.BlockSpec(memory_space=pltpu.SMEM)]
-        + [whole] * len(blocks)
-        + [pl.BlockSpec((int_count, COLUMN_TILE), lambda j: (0, j))],
-        out_specs=[pl.BlockSpec((rows, COLUMN_TILE), lambda j: (0, j)) for rows, _ in out_rows_types],
+        in_specs=[pl.BlockSpec(memory_space=pltpu.SMEM)] * len(screens) + [WHOLE] * (len(blocks) + 1),
+        out_specs=[WHOLE] * len(out_rows_types),
         scratch_shapes=[pltpu.VMEM((row_count, int_count), blocks[0].dtype)],
-        compiler_params=pltpu.CompilerParams(vmem_limit_bytes=VMEM_BYTES),
+        compiler_params=pltpu.CompilerParams(vmem_limit_bytes=PRODUCT_VMEM),
         cost_estimate=pl.CostEstimate(
             flops=2 * row_count * int_count * ab_count,
             bytes_accessed=2 * int_count * ab_count,
             transcendentals=0,
         ),
         name=name,
-    )(int_screen, *blocks, integrals)
+    )(*screens, *blocks, ints)
 
 
 def join_kernel(screen_ref, own_ref, *refs):
-    chunk_refs, (out_ref, total) = refs[:-2], refs[-2:]
+    chunk_refs, out_ref = refs[:-1], refs[-1]
     grp_index = lax.axis_index("grp")
-    first_tile = grp_index * BLOCK_TILES
-    own_slots, own_count = live_slots(screen_ref, first_tile, grp_index)
-    away_slots, away_count = live_slots(screen_ref, first_tile, 1 - grp_index)
-    total[...] = jnp.zeros_like(total)
-    for slot in range(LIVE_MAX):
-
-        @pl.when(slot < own_count)
-        def _():
-            rows = pl.ds(pl.multiple_of(own_slots[slot] * TS, TS), TS)
-            total[rows, :] = own_ref[slot * TS : (slot + 1) * TS, :]
-
+    slots, count = live_slots(screen_ref, grp_index * BLOCK_TILES, 1 - grp_index)
+    out_ref[...] = own_ref[...].astype(out_ref.dtype)
     for chunk, (first, last) in enumerate(SLOT_CHUNKS):
         code_ref, scale_ref = chunk_refs[2 * chunk : 2 * chunk + 2]
         for slot in range(first, last):
 
-            @pl.when(slot < away_count)
+            @pl.when(slot < count)
             def _():
-                rows = pl.ds(pl.multiple_of(away_slots[slot] * TS, TS), TS)
+                rows = pl.ds(pl.multiple_of(slots[slot] * TS, TS), TS)
                 at = slot - first
                 code = code_ref[at * TS : (at + 1) * TS, :].astype(jnp.float32)
-                total[rows, :] += code * scale_ref[at : at + 1, :]
-
-    out_ref[...] = total[...].astype(out_ref.dtype)
-
-
-def join(amp_screen, own_sum, chunks, row_count):
-    ab_count = own_sum.shape[1]
+                total = own_ref[rows, :] + code * scale_ref[at : at + 1, :]
+                out_ref[rows, :] = total.astype(out_ref.dtype)
+
+
+def join(amp_screen, own_sum, chunks):
+    row_count, ab_count = own_sum.shape
     flat = [array for chunk in chunks for array in chunk]
 
     def tall(rows):
@@ -170,11 +171,10 @@
         join_kernel,
         grid=(ab_count // JOIN_TILE,),
         out_shape=jax.ShapeDtypeStruct((row_count, ab_count), jnp.bfloat16),
-        in_specs=[pl.BlockSpec(memory_space=pltpu.SMEM), tall(own_sum.shape[0])]
+        in_specs=[pl.BlockSpec(memory_space=pltpu.SMEM), tall(row_count)]
         + [tall(array.shape[0]) for array in flat],
         out_specs=tall(row_count),
-        scratch_shapes=[pltpu.VMEM((row_count, JOIN_TILE), jnp.float32)],
-        compiler_params=pltpu.CompilerParams(vmem_limit_bytes=VMEM_BYTES),
+        compiler_params=pltpu.CompilerParams(vmem_limit_bytes=SMALL_VMEM),
         name="join",
     )(amp_screen, own_sum, *flat)
 
@@ -197,7 +197,8 @@
         for pan, grp in places
     ]
     across = [
-        (at(pan, grp), at((pan + half) % pan_count, 1 - grp)) for pan, grp in places if away(pan, grp)
+        (at(pan, grp), at((pan + half) % pan_count, 1 - grp) if away(pan, grp) else at(pan ^ 1, grp))
+        for pan, grp in places
     ]
     swap = [(at(pan, grp), at(pan, 1 - grp)) for pan, grp in places]
     return first, across, swap, flip
@@ -224,6 +225,7 @@
     first, across, swap, flip = routes(pan_count)
     is_own = lax.axis_index("pan") // (pan_count // 2) == lax.axis_index("grp")
 
+    ints = pltpu.with_memory_space_constraint(integrals, pltpu.VMEM)
     picked = pick_live(amplitudes, amp_screen, pair_size)
     own_parts, chunks = [], []
     for part in picked:
@@ -233,16 +235,16 @@
         blocks = gathered(jnp.where(is_own, from_first, from_across), flip, block_count)
         rows = part.shape[0]
         code, scale = product(
-            away_kernel, blocks, integrals, int_screen, pair_size,
+            away_kernel, (int_screen,), blocks, ints, pair_size,
             ((rows, jnp.int16), (rows // TS, jnp.float32)), "away_product",
         )
         chunks.append((lax.ppermute(code, AXES, swap), lax.ppermute(scale, AXES, swap)))
     own_blocks = gathered(jnp.concatenate(own_parts, axis=0), flip, block_count)
     (own_sum,) = product(
-        own_kernel, own_blocks, integrals, int_screen, pair_size,
-        ((LIVE_MAX * TS, jnp.float32),), "own_product",
+        own_kernel, (int_screen, amp_screen), own_blocks, ints, pair_size,
+        ((row_count, jnp.float32),), "own_product",
     )
-    return join(amp_screen, own_sum, chunks, row_count)
+    return join(amp_screen, own_sum, chunks)
 
 
 def column_pairs(piece_width, pair_size, pair_count):

time: 94.8 us -> 76.4 us (0.81)
  Pallas kernels: 47.7 us -> 21.4 us
  waiting for transfers between devices: 3.72 us -> 13.5 us
  local copies, waits for them, and re-layouts: 4.18 us -> 8.26 us
  starting transfers between devices: 36.3 us -> 32.8 us
  other arithmetic: 1.89 us -> 0.07 us
    pallas_call x3, Pallas kernels: 33.4 us -> 17.4 us  [product(): pl.pallas_call(functools.partial(kernel, pair_size), out_shape=[jax.Shape...]
    pallas_call x1, Pallas kernels: 9.91 us -> 1.11 us  [pick_live(): pl.pallas_call(functools.partial(pick_kernel, pair_size), out_shape=[jax....]
    ppermute x2, waiting for transfers between devices: 0.01 us -> 6.42 us  [two_group_shards(): lax.ppermute(scale, AXES, swap)]
    unnamed x59 -> x15, local copies, waits for them, and re-layouts: 4.18 us -> 8.26 us
    ppermute x2, starting transfers between devices: 10.5 us -> 7.41 us  [two_group_shards(): from_first = lax.ppermute(part, AXES, first)]
    ppermute x9, waiting for transfers between devices: 3.67 us -> 6 us  [gathered(): lax.ppermute(block, AXES, flip(bits))]
    select_n x2, other arithmetic: 1.87 us -> 0.05 us  [two_group_shards(): jnp.where(is_own, from_first, from_across)]
    pallas_call x1, Pallas kernels: 4.46 us -> 2.89 us  [join(): pl.pallas_call(join_kernel, grid=(ab_count // JOIN_TILE,), out_shape=jax....]
  transfers between devices with their start and end apart: 29 -> 29, of which waited for: 3 -> 8; matrix products, arithmetic and copies ran while one was open for 2% -> 0% of each run, Pallas kernels for 35% -> 23%
where the time goes in v2:
time: 76.4 us; the launch traced here: 76.2 us
  starting transfers between devices  32.8 us (43%)
  Pallas kernels  21.4 us (28%)
  waiting for transfers between devices  13.5 us (18%)
  local copies, waits for them, and re-layouts  8.26 us (11%)
    pallas_call x3, Pallas kernels, product(): pl.pallas_call(functools.partial(kernel, pair_size), out_shape=[jax.Shape...  17.4 us
    ppermute x9, starting transfers between devices, gathered(): lax.ppermute(block, AXES, flip(bits))  17.2 us
    unnamed x15, local copies, waits for them, and re-layouts  8.26 us
    ppermute x2, starting transfers between devices, two_group_shards(): from_first = lax.ppermute(part, AXES, first)  7.41 us
    ppermute x2, waiting for transfers between devices, two_group_shards(): lax.ppermute(scale, AXES, swap)  6.42 us
    ppermute x9, waiting for transfers between devices, gathered(): lax.ppermute(block, AXES, flip(bits))  6 us
    ppermute x2, starting transfers between devices, two_group_shards(): lax.ppermute(code, AXES, swap)  3.53 us
    pallas_call x1, Pallas kernels, join(): pl.pallas_call(join_kernel, grid=(ab_count // JOIN_TILE,), out_shape=jax....  2.89 us
  transfers between devices with their start and end apart: 29, of which 8 were waited for; matrix products, arithmetic and copies ran while one was open for 0% of the time, Pallas kernels for 23%

profile of v2, /device:TPU:0, one launch (start us, length us, event | category | flops | bytes accessed | tf_op | source)
XLA Modules:
  0.0 76.2 jit_solution(14224275723421366071)
XLA Ops:
  0.0 0.8 copy.7.screen_hbm.amp_screen_ref.screen_ref
  0.8 1.0 %copy-done.1 = bf16[512,512]{1,0:T(8,128)(2,1)S(1)} copy-done((bf16[512,512]{1,0:T(8,128)(2,1)S(1)}, bf16[512,512]{1,0:T(8,128)(2,1)}, u32[]{:S(2)}) %copy-start.1) | copy-done | bytes 524312
  1.8 1.1 %pick_live.1 = (bf16[128,512]{1,0:T(8,128)(2,1)S(1)}, bf16[128,512]{1,0:T(8,128)(2,1)S(1)}) custom-call(s32[16,2]{1,0:T(8,128)S(1)} %copy.7.screen_hbm.amp_screen_ref.screen_ref, bf16[512,512]{1,0:T(8,128)(2,1)S(1)} %copy-done.1), custom_call_target="tpu_custom_call" | custom-call | tf_op jit(solution)/shard_map/pick_live/pallas_call | solution.py:60
  2.9 0.5 collective-permute-start.9
  3.4 4.9 %collective-permute-start = (bf16[128,512]{1,0:T(8,128)(2,1)S(1)}, bf16[128,512]{1,0:T(8,128)(2,1)S(1)}, u32[]{:S(2)}, u32[]{:S(2)}) collective-permute-start(bf16[128,512]{1,0:T(8,128)(2,1)S(1)} %get-tuple-element.11), channel_id=1, source_target_pairs={{0,16},{1,0},{2,18},{3,2},{4,20},{5,4},{6,22},{7,6},{8,24},{9,8},{... | collective-permute-start | bytes 393224 | tf_op jit(solution)/shard_map/ppermute | solution.py:232
  8.3 0.0 collective-permute-start.19
  8.3 2.5 %collective-permute-start.1 = (bf16[128,512]{1,0:T(8,128)(2,1)S(1)}, bf16[128,512]{1,0:T(8,128)(2,1)S(1)}, u32[]{:S(2)}, u32[]{:S(2)}) collective-permute-start(bf16[128,512]{1,0:T(8,128)(2,1)S(1)} %get-tuple-element.12), channel_id=1, source_target_pairs={{0,16},{1,0},{2,18},{3,2},{4,20},{5,4},{6,22},{7,6},{8,24},{9,8},{... | collective-permute-start | bytes 393224 | tf_op jit(solution)/shard_map/ppermute | solution.py:232
  10.8 0.0 collective-permute-done.9
  10.9 1.1 %collective-permute-done = bf16[128,512]{1,0:T(8,128)(2,1)S(1)} collective-permute-done((bf16[128,512]{1,0:T(8,128)(2,1)S(1)}, bf16[128,512]{1,0:T(8,128)(2,1)S(1)}, u32[]{:S(2)}, u32[]{:S(2)}) %collective-permute-start) | collective-permute-done | bytes 131104 | tf_op jit(solution)/shard_map/ppermute | solution.py:232
  12.0 7.0 %collective-permute-start.15 = (bf16[128,512]{1,0:T(8,128)(2,1)S(1)}, bf16[128,512]{1,0:T(8,128)(2,1)S(1)}, u32[]{:S(2)}, u32[]{:S(2)}) collective-permute-start(bf16[128,512]{1,0:T(8,128)(2,1)S(1)} %get-tuple-element.19.refs_0_), channel_id=1, source_target_pairs={{0,12},{1,13},{2,14},{3,15},{4,8},{5,9},{6,10},{7,11},{8,4},{9,5},... | collective-permute-start | bytes 393224 | tf_op jit(solution)/shard_map/ppermute | solution.py:208
  19.0 0.0 collective-permute-start.13
  19.0 0.6 collective-permute-start.11
  19.6 0.0 collective-permute-done.19
  19.6 0.0 collective-permute-start.10
  19.6 0.0 collective-permute-done.1
  19.7 2.9 %collective-permute-start.25 = (bf16[128,512]{1,0:T(8,128)(2,1)S(1)}, bf16[128,512]{1,0:T(8,128)(2,1)S(1)}, u32[]{:S(2)}, u32[]{:S(2)}) collective-permute-start(bf16[128,512]{1,0:T(8,128)(2,1)S(1)} %get-tuple-element.17.refs_0_), channel_id=1, source_target_pairs={{0,12},{1,13},{2,14},{3,15},{4,8},{5,9},{6,10},{7,11},{8,4},{9,5},... | collective-permute-start | bytes 393224 | tf_op jit(solution)/shard_map/ppermute | solution.py:208
  22.6 1.2 %collective-permute-done.15.refs_6_ = bf16[128,512]{1,0:T(8,128)(2,1)S(1)} collective-permute-done((bf16[128,512]{1,0:T(8,128)(2,1)S(1)}, bf16[128,512]{1,0:T(8,128)(2,1)S(1)}, u32[]{:S(2)}, u32[]{:S(2)}) %collective-permute-start.15) | collective-permute-done | bytes 131104 | tf_op jit(solution)/shard_map/ppermute | solution.py:208
  23.8 1.5 %collective-permute-start.23 = (bf16[128,512]{1,0:T(8,128)(2,1)S(1)}, bf16[128,512]{1,0:T(8,128)(2,1)S(1)}, u32[]{:S(2)}, u32[]{:S(2)}) collective-permute-start(bf16[128,512]{1,0:T(8,128)(2,1)S(1)} %get-tuple-element.17.refs_0_), channel_id=1, source_target_pairs={{0,8},{1,9},{2,10},{3,11},{4,12},{5,13},{6,14},{7,15},{8,0},{9,1},... | collective-permute-start | bytes 393224 | tf_op jit(solution)/shard_map/ppermute | solution.py:208
  25.3 0.4 collective-permute-done.13.refs_4_
  25.7 1.5 %collective-permute-start.21 = (bf16[128,512]{1,0:T(8,128)(2,1)S(1)}, bf16[128,512]{1,0:T(8,128)(2,1)S(1)}, u32[]{:S(2)}, u32[]{:S(2)}) collective-permute-start(bf16[128,512]{1,0:T(8,128)(2,1)S(1)} %get-tuple-element.17.refs_0_), channel_id=1, source_target_pairs={{0,4},{1,5},{2,6},{3,7},{4,0},{5,1},{6,2},{7,3},{8,12},{9,13},{10,... | collective-permute-start | bytes 393224 | tf_op jit(solution)/shard_map/ppermute | solution.py:208
  27.2 0.0 collective-permute-done.11.refs_2_
  27.2 0.0 collective-permute-start.20
  27.2 0.0 collective-permute-done.10.refs_1_
  27.2 0.5 collective-permute-start.16
  27.7 1.8 %collective-permute-done.25.refs_6_ = bf16[128,512]{1,0:T(8,128)(2,1)S(1)} collective-permute-done((bf16[128,512]{1,0:T(8,128)(2,1)S(1)}, bf16[128,512]{1,0:T(8,128)(2,1)S(1)}, u32[]{:S(2)}, u32[]{:S(2)}) %collective-permute-start.25) | collective-permute-done | bytes 131104 | tf_op jit(solution)/shard_map/ppermute | solution.py:208
  29.5 0.0 collective-permute-start.14
  29.5 1.8 %collective-permute-done.23.refs_4_ = bf16[128,512]{1,0:T(8,128)(2,1)S(1)} collective-permute-done((bf16[128,512]{1,0:T(8,128)(2,1)S(1)}, bf16[128,512]{1,0:T(8,128)(2,1)S(1)}, u32[]{:S(2)}, u32[]{:S(2)}) %collective-permute-start.23) | collective-permute-done | bytes 131104 | tf_op jit(solution)/shard_map/ppermute | solution.py:208
  31.2 0.0 collective-permute-start.26
  31.3 0.9 %collective-permute-done.21.refs_2_ = bf16[128,512]{1,0:T(8,128)(2,1)S(1)} collective-permute-done((bf16[128,512]{1,0:T(8,128)(2,1)S(1)}, bf16[128,512]{1,0:T(8,128)(2,1)S(1)}, u32[]{:S(2)}, u32[]{:S(2)}) %collective-permute-start.21) | collective-permute-done | bytes 131104 | tf_op jit(solution)/shard_map/ppermute | solution.py:208
  32.2 0.0 collective-permute-start.24
  32.2 0.0 collective-permute-done.20.refs_1_
  32.2 0.5 collective-permute-start.22
  32.7 0.0 collective-permute-done.16.refs_7_
  32.7 1.5 %collective-permute-start.7 = (bf16[256,512]{1,0:T(8,128)(2,1)S(1)}, bf16[256,512]{1,0:T(8,128)(2,1)S(1)}, u32[]{:S(2)}, u32[]{:S(2)}) collective-permute-start(bf16[256,512]{1,0:T(8,128)(2,1)S(1)} %pad_maximum_fusion.refs_0_), channel_id=1, source_target_pairs={{0,12},{1,13},{2,14},{3,15},{4,8},{5,9},{6,10},{7,11},{8,4},{9,5},... | collective-permute-start | bytes 786440 | tf_op jit(solution)/shard_map/ppermute | solution.py:208
  34.2 0.0 collective-permute-done.14.refs_5_
  34.3 0.6 collective-permute-start.5
  34.9 0.0 collective-permute-done.26.refs_7_
  34.9 1.4 %collective-permute-start.3 = (bf16[256,512]{1,0:T(8,128)(2,1)S(1)}, bf16[256,512]{1,0:T(8,128)(2,1)S(1)}, u32[]{:S(2)}, u32[]{:S(2)}) collective-permute-start(bf16[256,512]{1,0:T(8,128)(2,1)S(1)} %pad_maximum_fusion.refs_0_), channel_id=1, source_target_pairs={{0,4},{1,5},{2,6},{3,7},{4,0},{5,1},{6,2},{7,3},{8,12},{9,13},{10,... | collective-permute-start | bytes 786440 | tf_op jit(solution)/shard_map/ppermute | solution.py:208
  36.3 0.0 collective-permute-done.24.refs_5_
  36.3 0.0 collective-permute-start.2
  36.3 0.0 collective-permute-done.22.refs_3_
  36.3 0.5 collective-permute-start.12
  36.8 5.8 %copy-done = bf16[4096,2048]{1,0:T(8,128)(2,1)S(1)} copy-done((bf16[4096,2048]{1,0:T(8,128)(2,1)S(1)}, bf16[4096,2048]{1,0:T(8,128)(2,1)}, u32[]{:S(2)}) %copy-start) | copy-done | bytes 16777240
  42.6 0.7 copy-done.2
  43.2 3.1 %away_product.3 = (s16[128,2048]{1,0:T(8,128)(2,1)S(1)}, f32[2,2048]{1,0:T(2,128)S(1)}) custom-call(s32[2,8]{1,0:T(2,128)S(1)} %copy-done.2, bf16[128,512]{1,0:T(8,128)(2,1)S(1)} %get-tuple-element.17.refs_0_, bf16[128,512]{1,0:T(8,128)(2,1)S(1)} %collective-permute-done.20.refs_1_, bf16[128,512]{1,0:T(8,128)(2,1)S(1)} %collective-permute-done.21.refs_2_, ...), custom_call_target="tpu_custom_call" | custom-call | flops 2147483648 | bytes 16777216 | tf_op jit(solution)/shard_map/away_product/pallas_call | solution.py:129
  46.4 0.0 collective-permute-done.12.refs_3_
  46.4 0.0 slice-start.2
  46.4 0.0 slice-start.3
  46.4 2.8 %collective-permute-start.27 = (s16[128,2048]{1,0:T(8,128)(2,1)S(1)}, s16[128,2048]{1,0:T(8,128)(2,1)S(1)}, u32[]{:S(2)}, u32[]{:S(2)}) collective-permute-start(s16[128,2048]{1,0:T(8,128)(2,1)S(1)} %get-tuple-element.15), channel_id=1, source_target_pairs={{0,1},{1,0},{2,3},{3,2},{4,5},{5,4},{6,7},{7,6},{8,9},{9,8},{10,11... | collective-permute-start | bytes 1572872 | tf_op jit(solution)/shard_map/ppermute | solution.py:241
  49.2 0.0 collective-permute-start.8
  49.2 0.0 collective-permute-done.5.refs_4_
  49.2 0.5 collective-permute-start.6
  49.7 0.1 collective-permute-start.4
  49.8 3.1 %away_product.2 = (s16[128,2048]{1,0:T(8,128)(2,1)S(1)}, f32[2,2048]{1,0:T(2,128)S(1)}) custom-call(s32[2,8]{1,0:T(2,128)S(1)} %copy-done.2, bf16[128,512]{1,0:T(8,128)(2,1)S(1)} %get-tuple-element.19.refs_0_, bf16[128,512]{1,0:T(8,128)(2,1)S(1)} %collective-permute-done.10.refs_1_, bf16[128,512]{1,0:T(8,128)(2,1)S(1)} %collective-permute-done.11.refs_2_, ...), custom_call_target="tpu_custom_call" | custom-call | flops 2147483648 | bytes 16777216 | tf_op jit(solution)/shard_map/away_product/pallas_call | solution.py:129
  52.9 0.7 collective-permute-start.17
  53.6 1.4 %collective-permute-start.18 = (f32[2,2048]{1,0:T(2,128)S(1)}, f32[2,2048]{1,0:T(2,128)S(1)}, u32[]{:S(2)}, u32[]{:S(2)}) collective-permute-start(f32[2,2048]{1,0:T(2,128)S(1)} %get-tuple-element.14), channel_id=1, source_target_pairs={{0,1},{1,0},{2,3},{3,2},{4,5},{5,4},{6,7},{7,6},{8,9},{9,8},{10,11... | collective-permute-start | bytes 49160 | tf_op jit(solution)/shard_map/ppermute | solution.py:241
  55.0 0.6 collective-permute-start.28
  55.7 0.0 collective-permute-done.4.refs_3_
  55.7 11.2 %own_product.1.own_ref = f32[512,2048]{1,0:T(8,128)S(1)} custom-call(s32[2,8]{1,0:T(2,128)S(1)} %copy-done.2, s32[16,2]{1,0:T(8,128)S(1)} %copy.7.screen_hbm.amp_screen_ref.screen_ref, bf16[256,512]{1,0:T(8,128)(2,1)S(1)} %pad_maximum_fusion.refs_0_, bf16[256,512]{1,0:T(8,128)(2,1)S(1)} %collective-permute-done.2.refs_1_, ...), custom_call_target="tpu_custom_call" | custom-call | flops 4294967296 | bytes 16777216 | tf_op jit(solution)/shard_map/own_product/pallas_call | solution.py:129
  66.9 6.2 %collective-permute-done.18.refs_1_ = f32[2,2048]{1,0:T(2,128)S(1)} collective-permute-done((f32[2,2048]{1,0:T(2,128)S(1)}, f32[2,2048]{1,0:T(2,128)S(1)}, u32[]{:S(2)}, u32[]{:S(2)}) %collective-permute-start.18) | collective-permute-done | bytes 16416 | tf_op jit(solution)/shard_map/ppermute | solution.py:241
  73.2 0.2 collective-permute-done.28.refs_3_
  73.3 0.0 collective-permute-done.27.refs_2_
  73.3 0.0 collective-permute-done.17.refs_0_
  73.3 2.9 %join.1 = bf16[512,2048]{1,0:T(8,128)(2,1)} custom-call(s32[16,2]{1,0:T(8,128)S(1)} %copy.7.screen_hbm.amp_screen_ref.screen_ref, f32[512,2048]{1,0:T(8,128)S(1)} %own_product.1.own_ref, s16[128,2048]{1,0:T(8,128)(2,1)S(1)} %collective-permute-done.17.refs_0_, f32[2,2048]{1,0:T(2,128)S(1)} %collective-permute-done.18.refs_1_, ...), custom_call_target="tpu_custom_call" | custom-call | tf_op jit(solution)/shard_map/join/pallas_call | solution.py:170
  (18 shorter events, 0.1 us)
Async XLA Ops:
  0.8 1.0 %copy-start.1 = (bf16[512,512]{1,0:T(8,128)(2,1)S(1)}, bf16[512,512]{1,0:T(8,128)(2,1)}, u32[]{:S(2)}) copy-start(bf16[512,512]{1,0:T(8,128)(2,1)} %amps_ref.1) | copy-start | bytes 1572868
  2.9 7.9 %collective-permute-start.9 = (bf16[128,512]{1,0:T(8,128)(2,1)S(1)}, bf16[128,512]{1,0:T(8,128)(2,1)S(1)}, u32[]{:S(2)}, u32[]{:S(2)}) collective-permute-start(bf16[128,512]{1,0:T(8,128)(2,1)S(1)} %get-tuple-element.11), channel_id=1, source_target_pairs={{0,2},{1,16},{2,0},{3,18},{4,6},{5,20},{6,4},{7,22},{8,10},{9,24},... | collective-permute-start | bytes 393224 | tf_op jit(solution)/shard_map/ppermute | solution.py:233
  3.4 8.5 %collective-permute-start = (bf16[128,512]{1,0:T(8,128)(2,1)S(1)}, bf16[128,512]{1,0:T(8,128)(2,1)S(1)}, u32[]{:S(2)}, u32[]{:S(2)}) collective-permute-start(bf16[128,512]{1,0:T(8,128)(2,1)S(1)} %get-tuple-element.11), channel_id=1, source_target_pairs={{0,16},{1,0},{2,18},{3,2},{4,20},{5,4},{6,22},{7,6},{8,24},{9,8},{... | collective-permute-start | bytes 393224 | tf_op jit(solution)/shard_map/ppermute | solution.py:232
  8.3 11.3 %collective-permute-start.19 = (bf16[128,512]{1,0:T(8,128)(2,1)S(1)}, bf16[128,512]{1,0:T(8,128)(2,1)S(1)}, u32[]{:S(2)}, u32[]{:S(2)}) collective-permute-start(bf16[128,512]{1,0:T(8,128)(2,1)S(1)} %get-tuple-element.12), channel_id=1, source_target_pairs={{0,2},{1,16},{2,0},{3,18},{4,6},{5,20},{6,4},{7,22},{8,10},{9,24},... | collective-permute-start | bytes 393224 | tf_op jit(solution)/shard_map/ppermute | solution.py:233
  8.3 11.3 %collective-permute-start.1 = (bf16[128,512]{1,0:T(8,128)(2,1)S(1)}, bf16[128,512]{1,0:T(8,128)(2,1)S(1)}, u32[]{:S(2)}, u32[]{:S(2)}) collective-permute-start(bf16[128,512]{1,0:T(8,128)(2,1)S(1)} %get-tuple-element.12), channel_id=1, source_target_pairs={{0,16},{1,0},{2,18},{3,2},{4,20},{5,4},{6,22},{7,6},{8,24},{9,8},{... | collective-permute-start | bytes 393224 | tf_op jit(solution)/shard_map/ppermute | solution.py:232
  12.0 11.8 %collective-permute-start.15 = (bf16[128,512]{1,0:T(8,128)(2,1)S(1)}, bf16[128,512]{1,0:T(8,128)(2,1)S(1)}, u32[]{:S(2)}, u32[]{:S(2)}) collective-permute-start(bf16[128,512]{1,0:T(8,128)(2,1)S(1)} %get-tuple-element.19.refs_0_), channel_id=1, source_target_pairs={{0,12},{1,13},{2,14},{3,15},{4,8},{5,9},{6,10},{7,11},{8,4},{9,5},... | collective-permute-start | bytes 393224 | tf_op jit(solution)/shard_map/ppermute | solution.py:208
  19.0 6.7 %collective-permute-start.13 = (bf16[128,512]{1,0:T(8,128)(2,1)S(1)}, bf16[128,512]{1,0:T(8,128)(2,1)S(1)}, u32[]{:S(2)}, u32[]{:S(2)}) collective-permute-start(bf16[128,512]{1,0:T(8,128)(2,1)S(1)} %get-tuple-element.19.refs_0_), channel_id=1, source_target_pairs={{0,8},{1,9},{2,10},{3,11},{4,12},{5,13},{6,14},{7,15},{8,0},{9,1},... | collective-permute-start | bytes 393224 | tf_op jit(solution)/shard_map/ppermute | solution.py:208
  19.0 8.2 %collective-permute-start.11 = (bf16[128,512]{1,0:T(8,128)(2,1)S(1)}, bf16[128,512]{1,0:T(8,128)(2,1)S(1)}, u32[]{:S(2)}, u32[]{:S(2)}) collective-permute-start(bf16[128,512]{1,0:T(8,128)(2,1)S(1)} %get-tuple-element.19.refs_0_), channel_id=1, source_target_pairs={{0,4},{1,5},{2,6},{3,7},{4,0},{5,1},{6,2},{7,3},{8,12},{9,13},{10,... | collective-permute-start | bytes 393224 | tf_op jit(solution)/shard_map/ppermute | solution.py:208
  19.6 7.5 %collective-permute-start.10 = (bf16[128,512]{1,0:T(8,128)(2,1)S(1)}, bf16[128,512]{1,0:T(8,128)(2,1)S(1)}, u32[]{:S(2)}, u32[]{:S(2)}) collective-permute-start(bf16[128,512]{1,0:T(8,128)(2,1)S(1)} %get-tuple-element.19.refs_0_), channel_id=1, source_target_pairs={{0,2},{1,3},{2,0},{3,1},{4,6},{5,7},{6,4},{7,5},{8,10},{9,11},{10,... | collective-permute-start | bytes 393224 | tf_op jit(solution)/shard_map/ppermute | solution.py:210
  19.7 9.8 %collective-permute-start.25 = (bf16[128,512]{1,0:T(8,128)(2,1)S(1)}, bf16[128,512]{1,0:T(8,128)(2,1)S(1)}, u32[]{:S(2)}, u32[]{:S(2)}) collective-permute-start(bf16[128,512]{1,0:T(8,128)(2,1)S(1)} %get-tuple-element.17.refs_0_), channel_id=1, source_target_pairs={{0,12},{1,13},{2,14},{3,15},{4,8},{5,9},{6,10},{7,11},{8,4},{9,5},... | collective-permute-start | bytes 393224 | tf_op jit(solution)/shard_map/ppermute | solution.py:208
  23.8 7.4 %collective-permute-start.23 = (bf16[128,512]{1,0:T(8,128)(2,1)S(1)}, bf16[128,512]{1,0:T(8,128)(2,1)S(1)}, u32[]{:S(2)}, u32[]{:S(2)}) collective-permute-start(bf16[128,512]{1,0:T(8,128)(2,1)S(1)} %get-tuple-element.17.refs_0_), channel_id=1, source_target_pairs={{0,8},{1,9},{2,10},{3,11},{4,12},{5,13},{6,14},{7,15},{8,0},{9,1},... | collective-permute-start | bytes 393224 | tf_op jit(solution)/shard_map/ppermute | solution.py:208
  25.7 6.5 %collective-permute-start.21 = (bf16[128,512]{1,0:T(8,128)(2,1)S(1)}, bf16[128,512]{1,0:T(8,128)(2,1)S(1)}, u32[]{:S(2)}, u32[]{:S(2)}) collective-permute-start(bf16[128,512]{1,0:T(8,128)(2,1)S(1)} %get-tuple-element.17.refs_0_), channel_id=1, source_target_pairs={{0,4},{1,5},{2,6},{3,7},{4,0},{5,1},{6,2},{7,3},{8,12},{9,13},{10,... | collective-permute-start | bytes 393224 | tf_op jit(solution)/shard_map/ppermute | solution.py:208
  27.2 5.0 %collective-permute-start.20 = (bf16[128,512]{1,0:T(8,128)(2,1)S(1)}, bf16[128,512]{1,0:T(8,128)(2,1)S(1)}, u32[]{:S(2)}, u32[]{:S(2)}) collective-permute-start(bf16[128,512]{1,0:T(8,128)(2,1)S(1)} %get-tuple-element.17.refs_0_), channel_id=1, source_target_pairs={{0,2},{1,3},{2,0},{3,1},{4,6},{5,7},{6,4},{7,5},{8,10},{9,11},{10,... | collective-permute-start | bytes 393224 | tf_op jit(solution)/shard_map/ppermute | solution.py:210
  27.2 5.5 %collective-permute-start.16 = (bf16[128,512]{1,0:T(8,128)(2,1)S(1)}, bf16[128,512]{1,0:T(8,128)(2,1)S(1)}, u32[]{:S(2)}, u32[]{:S(2)}) collective-permute-start(bf16[128,512]{1,0:T(8,128)(2,1)S(1)} %collective-permute-done.15.refs_6_), channel_id=1, source_target_pairs={{0,2},{1,3},{2,0},{3,1},{4,6},{5,7},{6,4},{7,5},{8,10},{9,11},{10,... | collective-permute-start | bytes 393224 | tf_op jit(solution)/shard_map/ppermute | solution.py:210
  29.5 4.8 %collective-permute-start.14 = (bf16[128,512]{1,0:T(8,128)(2,1)S(1)}, bf16[128,512]{1,0:T(8,128)(2,1)S(1)}, u32[]{:S(2)}, u32[]{:S(2)}) collective-permute-start(bf16[128,512]{1,0:T(8,128)(2,1)S(1)} %collective-permute-done.13.refs_4_), channel_id=1, source_target_pairs={{0,2},{1,3},{2,0},{3,1},{4,6},{5,7},{6,4},{7,5},{8,10},{9,11},{10,... | collective-permute-start | bytes 393224 | tf_op jit(solution)/shard_map/ppermute | solution.py:210
  31.2 3.6 %collective-permute-start.26 = (bf16[128,512]{1,0:T(8,128)(2,1)S(1)}, bf16[128,512]{1,0:T(8,128)(2,1)S(1)}, u32[]{:S(2)}, u32[]{:S(2)}) collective-permute-start(bf16[128,512]{1,0:T(8,128)(2,1)S(1)} %collective-permute-done.25.refs_6_), channel_id=1, source_target_pairs={{0,2},{1,3},{2,0},{3,1},{4,6},{5,7},{6,4},{7,5},{8,10},{9,11},{10,... | collective-permute-start | bytes 393224 | tf_op jit(solution)/shard_map/ppermute | solution.py:210
  32.2 4.1 %collective-permute-start.24 = (bf16[128,512]{1,0:T(8,128)(2,1)S(1)}, bf16[128,512]{1,0:T(8,128)(2,1)S(1)}, u32[]{:S(2)}, u32[]{:S(2)}) collective-permute-start(bf16[128,512]{1,0:T(8,128)(2,1)S(1)} %collective-permute-done.23.refs_4_), channel_id=1, source_target_pairs={{0,2},{1,3},{2,0},{3,1},{4,6},{5,7},{6,4},{7,5},{8,10},{9,11},{10,... | collective-permute-start | bytes 393224 | tf_op jit(solution)/shard_map/ppermute | solution.py:210
  32.2 4.1 %collective-permute-start.22 = (bf16[128,512]{1,0:T(8,128)(2,1)S(1)}, bf16[128,512]{1,0:T(8,128)(2,1)S(1)}, u32[]{:S(2)}, u32[]{:S(2)}) collective-permute-start(bf16[128,512]{1,0:T(8,128)(2,1)S(1)} %collective-permute-done.21.refs_2_), channel_id=1, source_target_pairs={{0,2},{1,3},{2,0},{3,1},{4,6},{5,7},{6,4},{7,5},{8,10},{9,11},{10,... | collective-permute-start | bytes 393224 | tf_op jit(solution)/shard_map/ppermute | solution.py:210
  32.7 16.5 %collective-permute-start.7 = (bf16[256,512]{1,0:T(8,128)(2,1)S(1)}, bf16[256,512]{1,0:T(8,128)(2,1)S(1)}, u32[]{:S(2)}, u32[]{:S(2)}) collective-permute-start(bf16[256,512]{1,0:T(8,128)(2,1)S(1)} %pad_maximum_fusion.refs_0_), channel_id=1, source_target_pairs={{0,12},{1,13},{2,14},{3,15},{4,8},{5,9},{6,10},{7,11},{8,4},{9,5},... | collective-permute-start | bytes 786440 | tf_op jit(solution)/shard_map/ppermute | solution.py:208
  34.3 15.0 %collective-permute-start.5 = (bf16[256,512]{1,0:T(8,128)(2,1)S(1)}, bf16[256,512]{1,0:T(8,128)(2,1)S(1)}, u32[]{:S(2)}, u32[]{:S(2)}) collective-permute-start(bf16[256,512]{1,0:T(8,128)(2,1)S(1)} %pad_maximum_fusion.refs_0_), channel_id=1, source_target_pairs={{0,8},{1,9},{2,10},{3,11},{4,12},{5,13},{6,14},{7,15},{8,0},{9,1},... | collective-permute-start | bytes 786440 | tf_op jit(solution)/shard_map/ppermute | solution.py:208
  34.9 14.9 %collective-permute-start.3 = (bf16[256,512]{1,0:T(8,128)(2,1)S(1)}, bf16[256,512]{1,0:T(8,128)(2,1)S(1)}, u32[]{:S(2)}, u32[]{:S(2)}) collective-permute-start(bf16[256,512]{1,0:T(8,128)(2,1)S(1)} %pad_maximum_fusion.refs_0_), channel_id=1, source_target_pairs={{0,4},{1,5},{2,6},{3,7},{4,0},{5,1},{6,2},{7,3},{8,12},{9,13},{10,... | collective-permute-start | bytes 786440 | tf_op jit(solution)/shard_map/ppermute | solution.py:208
  36.3 16.7 %collective-permute-start.2 = (bf16[256,512]{1,0:T(8,128)(2,1)S(1)}, bf16[256,512]{1,0:T(8,128)(2,1)S(1)}, u32[]{:S(2)}, u32[]{:S(2)}) collective-permute-start(bf16[256,512]{1,0:T(8,128)(2,1)S(1)} %pad_maximum_fusion.refs_0_), channel_id=1, source_target_pairs={{0,2},{1,3},{2,0},{3,1},{4,6},{5,7},{6,4},{7,5},{8,10},{9,11},{10,... | collective-permute-start | bytes 786440 | tf_op jit(solution)/shard_map/ppermute | solution.py:210
  36.3 10.1 %collective-permute-start.12 = (bf16[128,512]{1,0:T(8,128)(2,1)S(1)}, bf16[128,512]{1,0:T(8,128)(2,1)S(1)}, u32[]{:S(2)}, u32[]{:S(2)}) collective-permute-start(bf16[128,512]{1,0:T(8,128)(2,1)S(1)} %collective-permute-done.11.refs_2_), channel_id=1, source_target_pairs={{0,2},{1,3},{2,0},{3,1},{4,6},{5,7},{6,4},{7,5},{8,10},{9,11},{10,... | collective-permute-start | bytes 393224 | tf_op jit(solution)/shard_map/ppermute | solution.py:210
  36.8 5.8 %copy-start = (bf16[4096,2048]{1,0:T(8,128)(2,1)S(1)}, bf16[4096,2048]{1,0:T(8,128)(2,1)}, u32[]{:S(2)}) copy-start(bf16[4096,2048]{1,0:T(8,128)(2,1)} %refs_8_.5) | copy-start | bytes 50331652
  42.6 0.7 copy-start.2
  43.2 12.4 %slice-start = ((s8[16777216]{0:T(1024)(128)(4,1)}), s8[4194304]{0:T(1024)(128)(4,1)S(1)}, s32[]{:S(2)}) async-start(s8[16777216]{0:T(1024)(128)(4,1)} %bitcast), calls=%async_computation | async-start | bytes 8388608
  43.2 12.4 %slice-start.1 = ((s8[16777216]{0:T(1024)(128)(4,1)}), s8[4194304]{0:T(1024)(128)(4,1)S(1)}, s32[]{:S(2)}) async-start(s8[16777216]{0:T(1024)(128)(4,1)} %bitcast), calls=%async_computation.1 | async-start | bytes 8388608
  46.4 9.3 %slice-start.2 = ((s8[16777216]{0:T(1024)(128)(4,1)}), s8[4194304]{0:T(1024)(128)(4,1)S(1)}, s32[]{:S(2)}) async-start(s8[16777216]{0:T(1024)(128)(4,1)} %bitcast), calls=%async_computation.2 | async-start | bytes 8388608
  46.4 9.3 %slice-start.3 = ((s8[16777216]{0:T(1024)(128)(4,1)}), s8[4194304]{0:T(1024)(128)(4,1)S(1)}, s32[]{:S(2)}) async-start(s8[16777216]{0:T(1024)(128)(4,1)} %bitcast), calls=%async_computation.3 | async-start | bytes 8388608
  46.4 26.9 %collective-permute-start.27 = (s16[128,2048]{1,0:T(8,128)(2,1)S(1)}, s16[128,2048]{1,0:T(8,128)(2,1)S(1)}, u32[]{:S(2)}, u32[]{:S(2)}) collective-permute-start(s16[128,2048]{1,0:T(8,128)(2,1)S(1)} %get-tuple-element.15), channel_id=1, source_target_pairs={{0,1},{1,0},{2,3},{3,2},{4,5},{5,4},{6,7},{7,6},{8,9},{9,8},{10,11... | collective-permute-start | bytes 1572872 | tf_op jit(solution)/shard_map/ppermute | solution.py:241
  49.2 4.4 %collective-permute-start.8 = (bf16[256,512]{1,0:T(8,128)(2,1)S(1)}, bf16[256,512]{1,0:T(8,128)(2,1)S(1)}, u32[]{:S(2)}, u32[]{:S(2)}) collective-permute-start(bf16[256,512]{1,0:T(8,128)(2,1)S(1)} %collective-permute-done.7.refs_6_), channel_id=1, source_target_pairs={{0,2},{1,3},{2,0},{3,1},{4,6},{5,7},{6,4},{7,5},{8,10},{9,11},{10,... | collective-permute-start | bytes 786440 | tf_op jit(solution)/shard_map/ppermute | solution.py:210
  49.2 5.8 %collective-permute-start.6 = (bf16[256,512]{1,0:T(8,128)(2,1)S(1)}, bf16[256,512]{1,0:T(8,128)(2,1)S(1)}, u32[]{:S(2)}, u32[]{:S(2)}) collective-permute-start(bf16[256,512]{1,0:T(8,128)(2,1)S(1)} %collective-permute-done.5.refs_4_), channel_id=1, source_target_pairs={{0,2},{1,3},{2,0},{3,1},{4,6},{5,7},{6,4},{7,5},{8,10},{9,11},{10,... | collective-permute-start | bytes 786440 | tf_op jit(solution)/shard_map/ppermute | solution.py:210
  49.7 5.9 %collective-permute-start.4 = (bf16[256,512]{1,0:T(8,128)(2,1)S(1)}, bf16[256,512]{1,0:T(8,128)(2,1)S(1)}, u32[]{:S(2)}, u32[]{:S(2)}) collective-permute-start(bf16[256,512]{1,0:T(8,128)(2,1)S(1)} %collective-permute-done.3.refs_2_), channel_id=1, source_target_pairs={{0,2},{1,3},{2,0},{3,1},{4,6},{5,7},{6,4},{7,5},{8,10},{9,11},{10,... | collective-permute-start | bytes 786440 | tf_op jit(solution)/shard_map/ppermute | solution.py:210
  52.9 20.4 %collective-permute-start.17 = (s16[128,2048]{1,0:T(8,128)(2,1)S(1)}, s16[128,2048]{1,0:T(8,128)(2,1)S(1)}, u32[]{:S(2)}, u32[]{:S(2)}) collective-permute-start(s16[128,2048]{1,0:T(8,128)(2,1)S(1)} %get-tuple-element.13), channel_id=1, source_target_pairs={{0,1},{1,0},{2,3},{3,2},{4,5},{5,4},{6,7},{7,6},{8,9},{9,8},{10,11... | collective-permute-start | bytes 1572872 | tf_op jit(solution)/shard_map/ppermute | solution.py:241
  53.6 19.5 %collective-permute-start.18 = (f32[2,2048]{1,0:T(2,128)S(1)}, f32[2,2048]{1,0:T(2,128)S(1)}, u32[]{:S(2)}, u32[]{:S(2)}) collective-permute-start(f32[2,2048]{1,0:T(2,128)S(1)} %get-tuple-element.14), channel_id=1, source_target_pairs={{0,1},{1,0},{2,3},{3,2},{4,5},{5,4},{6,7},{7,6},{8,9},{9,8},{10,11... | collective-permute-start | bytes 49160 | tf_op jit(solution)/shard_map/ppermute | solution.py:241
  55.0 18.3 %collective-permute-start.28 = (f32[2,2048]{1,0:T(2,128)S(1)}, f32[2,2048]{1,0:T(2,128)S(1)}, u32[]{:S(2)}, u32[]{:S(2)}) collective-permute-start(f32[2,2048]{1,0:T(2,128)S(1)} %get-tuple-element.16), channel_id=1, source_target_pairs={{0,1},{1,0},{2,3},{3,2},{4,5},{5,4},{6,7},{7,6},{8,9},{9,8},{10,11... | collective-permute-start | bytes 49160 | tf_op jit(solution)/shard_map/ppermute | solution.py:241

commit v3 on v2

v3 whole, which is shorter than its diff:
```python
import functools

import jax
import jax.numpy as jnp
from jax import lax
from jax.experimental import pallas as pl
from jax.experimental.pallas import tpu as pltpu
from jax.sharding import PartitionSpec as P

TS = 64
LIVE_MAX = 4
BLOCK_TILES = 8
AXES = ("pan", "grp")
SLOT_CHUNKS = ((0, 2), (2, 4))
CODE_MAX = 32767.0
STAGE_COPIES = 8
LEAST_SCALE = 1e-33
ROW_TILE = 128
COLUMN_TILE = 256
JOIN_TILE = 512
SMALL_VMEM = 8 * 1024 * 1024
PRODUCT_VMEM = 16 * 1024 * 1024
LIGHT = pl.CostEstimate(flops=1, bytes_accessed=1, transcendentals=0)
WHOLE = pl.BlockSpec(memory_space=pltpu.VMEM)


def live_slots(screen_ref, first_tile, column):
    count = jnp.int32(0)
    slots = [jnp.int32(0)] * LIVE_MAX
    for tile in range(BLOCK_TILES):
        live = screen_ref[column, first_tile + tile] != 0
        for slot in range(LIVE_MAX):
            slots[slot] = jnp.where(live & (count == slot), tile, slots[slot])
        count = count + live.astype(jnp.int32)
    return slots, count


def pick_kernel(pair_size, screen_hbm, amps_ref, *rest):
    picked_refs, (screen_ref, screen_sem, sem) = rest[:-3], rest[-3:]
    screen_copy = pltpu.make_async_copy(screen_hbm, screen_ref, screen_sem)
    screen_copy.start()
    screen_copy.wait()
    column = lax.axis_index("pan") * amps_ref.shape[1] // pair_size
    slots, _ = live_slots(screen_ref, lax.axis_index("grp") * BLOCK_TILES, column)
    copies = []
    for (first, last), picked_ref in zip(SLOT_CHUNKS, picked_refs):
        for slot in range(first, last):
            rows = pl.ds(pl.multiple_of(slots[slot] * TS, TS), TS)
            copies.append(
                pltpu.make_async_copy(
                    amps_ref.at[rows, :],
                    picked_ref.at[pl.ds((slot - first) * TS, TS), :],
                    sem.at[slot],
                )
            )
    for copy in copies:
        copy.start()
    for copy in copies:
        copy.wait()


def pick_live(amplitudes, amp_screen, pair_size):
    return pl.pallas_call(
        functools.partial(pick_kernel, pair_size),
        out_shape=[
            jax.ShapeDtypeStruct(((last - first) * TS, amplitudes.shape[1]), amplitudes.dtype)
            for first, last in SLOT_CHUNKS
        ],
        in_specs=[pl.BlockSpec(memory_space=pl.ANY), pl.BlockSpec(memory_space=pltpu.HBM)],
        out_specs=[WHOLE] * len(SLOT_CHUNKS),
        scratch_shapes=[
            pltpu.SMEM(amp_screen.shape, amp_screen.dtype),
            pltpu.SemaphoreType.DMA,
            pltpu.SemaphoreType.DMA((LIVE_MAX,)),
        ],
        compiler_params=pltpu.CompilerParams(vmem_limit_bytes=SMALL_VMEM),
        name="pick_live",
    )(amp_screen, pltpu.with_memory_space_constraint(amplitudes, pltpu.HBM))


def stage_kernel(ints_hbm, after, ints_ref, staged_ref, sem):
    del after
    staged_ref[...] = jnp.zeros_like(staged_ref)
    rows = ints_hbm.shape[0] // STAGE_COPIES
    copies = [
        pltpu.make_async_copy(
            ints_hbm.at[pl.ds(part * rows, rows), :], ints_ref.at[pl.ds(part * rows, rows), :], sem.at[part]
        )
        for part in range(STAGE_COPIES)
    ]
    for copy in copies:
        copy.start()
    for copy in copies:
        copy.wait()


def stage(integrals, after):
    return pl.pallas_call(
        stage_kernel,
        out_shape=[pltpu.VMEM(integrals.shape, integrals.dtype), jax.ShapeDtypeStruct((8, 128), jnp.float32)],
        in_specs=[pl.BlockSpec(memory_space=pltpu.HBM), pl.BlockSpec(memory_space=pl.ANY)],
        out_specs=[WHOLE] * 2,
        scratch_shapes=[pltpu.SemaphoreType.DMA((STAGE_COPIES,))],
        compiler_params=pltpu.CompilerParams(vmem_limit_bytes=SMALL_VMEM),
        cost_estimate=LIGHT,
        name="stage_integrals",
    )(pltpu.with_memory_space_constraint(integrals, pltpu.HBM), after)


def lay_out(near, other_ref, panel):
    depth = other_ref.shape[2]
    own = lax.rem(lax.axis_index("pan"), 2 * other_ref.shape[0])
    for step in range(2 * other_ref.shape[0]):
        held = other_ref[step // 2] if step % 2 else near[step // 2][...]
        panel[:, pl.ds(pl.multiple_of((own ^ step) * depth, depth), depth)] = held


def int_keep(screen_ref, ints_shape, pair_size):
    in_pair = lax.axis_index("grp") * ints_shape[0] // pair_size
    out_pair = lax.axis_index("pan") * ints_shape[1] // pair_size
    return screen_ref[in_pair, out_pair].astype(jnp.float32)


def product_blocks(panel, ints_ref):
    row_step = min(ROW_TILE, panel.shape[0])
    return [
        (row, column)
        for column in range(0, ints_ref.shape[1], COLUMN_TILE)
        for row in range(0, panel.shape[0], row_step)
    ]


def block_sums(panel, ints_ref, row, column):
    rows = slice(row, row + min(ROW_TILE, panel.shape[0]))
    ints = ints_ref[:, column : column + COLUMN_TILE]
    return jnp.dot(panel[rows, :], ints, preferred_element_type=jnp.float32)


def own_kernel(pair_size, int_screen_ref, near_ref, other_ref, ints_ref, *refs):
    sum_ref, panel = refs[-2:]
    keep = int_keep(int_screen_ref, ints_ref.shape, pair_size)
    lay_out([near_ref.at[place] for place in range(near_ref.shape[0])], other_ref, panel)
    for row, column in product_blocks(panel, ints_ref):
        sums = block_sums(panel, ints_ref, row, column) * keep
        sum_ref[row : row + sums.shape[0], column : column + COLUMN_TILE] = sums


def away_kernel(pair_size, near_count, int_screen_ref, *refs):
    near, (other_ref, ints_ref, before_ref) = refs[:near_count], refs[near_count : near_count + 3]
    code_ref, scale_ref, panel = refs[-3:]
    keep = int_keep(int_screen_ref, ints_ref.shape, pair_size)
    lay_out(near, other_ref, panel)
    first = scale_ref.shape[0] - code_ref.shape[0] // TS
    if first:
        scale_ref[:first, :] = before_ref[...]
    for row, column in product_blocks(panel, ints_ref):
        sums = block_sums(panel, ints_ref, row, column) * keep
        columns = slice(column, column + COLUMN_TILE)
        for at in range(0, sums.shape[0], TS):
            slot, rows = first + (row + at) // TS, slice(row + at, row + at + TS)
            part = sums[at : at + TS]
            top = jnp.maximum(jnp.max(jnp.abs(part), axis=0, keepdims=True), LEAST_SCALE)
            code = jnp.round(part * (CODE_MAX / top))
            code_ref[rows, columns] = code.astype(jnp.int32).astype(jnp.int16)
            scale_ref[slot : slot + 1, columns] = top * (1.0 / CODE_MAX)


def product(kernel, int_screen, arrays, gates, row_count, ints, out_rows_types, name):
    int_count, ab_count = ints.shape
    return pl.pallas_call(
        kernel,
        out_shape=[jax.ShapeDtypeStruct((rows, ab_count), dtype) for rows, dtype in out_rows_types],
        in_specs=[pl.BlockSpec(memory_space=pltpu.SMEM)]
        + [WHOLE] * len(arrays)
        + [pl.BlockSpec(memory_space=pl.ANY)] * len(gates),
        out_specs=[WHOLE] * len(out_rows_types),
        scratch_shapes=[pltpu.VMEM((row_count, int_count), ints.dtype)],
        compiler_params=pltpu.CompilerParams(vmem_limit_bytes=PRODUCT_VMEM),
        cost_estimate=LIGHT,
        name=name,
    )(int_screen, *arrays, *gates)


def join_kernel(screen_ref, own_ref, scale_ref, *refs):
    code_refs, (out_ref, total) = refs[:-2], refs[-2:]
    grp_index = lax.axis_index("grp")
    first_tile = grp_index * BLOCK_TILES
    own_slots, own_count = live_slots(screen_ref, first_tile, grp_index)
    slots, count = live_slots(screen_ref, first_tile, 1 - grp_index)
    total[...] = jnp.zeros_like(total)
    for slot in range(LIVE_MAX):

        @pl.when(slot < own_count)
        def _():
            rows = pl.ds(pl.multiple_of(own_slots[slot] * TS, TS), TS)
            total[rows, :] = own_ref[slot * TS : (slot + 1) * TS, :]

    for (first, last), code_ref in zip(SLOT_CHUNKS, code_refs):
        for slot in range(first, last):

            @pl.when(slot < count)
            def _():
                rows = pl.ds(pl.multiple_of(slots[slot] * TS, TS), TS)
                code = code_ref[(slot - first) * TS : (slot - first + 1) * TS, :].astype(jnp.float32)
                total[rows, :] += code * scale_ref[slot : slot + 1, :]

    out_ref[...] = total[...].astype(out_ref.dtype)


def join(amp_screen, own_sum, scales, codes, row_count):
    ab_count = own_sum.shape[1]
    arrays = [own_sum, scales, *codes]

    def tall(rows):
        return pl.BlockSpec((rows, JOIN_TILE), lambda j: (0, j))

    return pl.pallas_call(
        join_kernel,
        grid=(ab_count // JOIN_TILE,),
        out_shape=jax.ShapeDtypeStruct((row_count, ab_count), jnp.bfloat16),
        in_specs=[pl.BlockSpec(memory_space=pltpu.SMEM)] + [tall(array.shape[0]) for array in arrays],
        out_specs=tall(row_count),
        scratch_shapes=[pltpu.VMEM((row_count, JOIN_TILE), jnp.float32)],
        compiler_params=pltpu.CompilerParams(vmem_limit_bytes=SMALL_VMEM),
        name="join",
    )(amp_screen, *arrays)


def routes(pan_count):
    half = pan_count // 2
    places = [(pan, grp) for pan in range(pan_count) for grp in range(2)]

    def at(pan, grp):
        return pan * 2 + grp

    def away(pan, grp):
        return pan // half != grp

    def flip(bits):
        return [(at(pan, grp), at(pan ^ bits, grp)) for pan, grp in places]

    first = [
        (at(pan, grp), at(pan, 1 - grp) if away(pan, grp) else at((pan + half) % pan_count, grp))
        for pan, grp in places
    ]
    across = [
        (at(pan, grp), at((pan + half) % pan_count, 1 - grp) if away(pan, grp) else at(pan ^ 1, grp))
        for pan, grp in places
    ]
    swap = [(at(pan, grp), at(pan, 1 - grp)) for pan, grp in places]
    return first, across, swap, flip


def near_blocks(block, flip, block_count):
    return [block] + [lax.ppermute(block, AXES, flip(bits)) for bits in range(2, block_count, 2)]


def two_group_shards(pan_count, amplitudes, integrals, amp_screen, int_screen):
    pair_size = TS * TS
    row_count, col_count = amplitudes.shape
    block_count = integrals.shape[0] // col_count
    if (
        row_count != BLOCK_TILES * TS
        or amp_screen.shape[1] != 2
        or integrals.shape[0] != pair_size
        or block_count * 2 != pan_count
    ):
        return shards(amplitudes, integrals, amp_screen, int_screen)
    first, across, swap, flip = routes(pan_count)
    is_own = lax.axis_index("pan") // (pan_count // 2) == lax.axis_index("grp")

    amp_screen = amp_screen.T
    picked = pick_live(amplitudes, amp_screen, pair_size)

    def away_product(near, before, gates):
        other = lax.ppermute(jnp.stack(near), AXES, flip(1))
        rows = near[0].shape[0]
        scale_rows = rows // TS + (0 if before is None else before.shape[0])
        before = gates[0] if before is None else before
        return product(
            functools.partial(away_kernel, pair_size, len(near)), int_screen, [*near, other, ints, before], gates,
            rows, ints, ((rows, jnp.int16), (scale_rows, jnp.float32)), "away_product",
        )

    arrived = [(lax.ppermute(part, AXES, first), lax.ppermute(part, AXES, across)) for part in picked]
    own_block = jnp.concatenate([jnp.where(is_own, part, pair[0]) for part, pair in zip(picked, arrived)], axis=0)
    away_a, away_b = [jnp.where(is_own, *pair) for pair in arrived]
    ints, staged = stage(integrals, away_a)

    near_a = near_blocks(away_a, flip, block_count)
    near_a, staged = lax.optimization_barrier((near_a, staged))
    away_b, near_a = lax.optimization_barrier((away_b, near_a))
    near_b = near_blocks(away_b, flip, block_count)
    code_a, scale_a = away_product(near_a, None, [staged])
    came_a = lax.ppermute(code_a, AXES, swap)
    near_b, scale_a = lax.optimization_barrier((near_b, scale_a))
    own_block, near_b = lax.optimization_barrier((own_block, near_b))
    own_near = near_blocks(own_block, flip, block_count)
    code_b, scales = away_product(near_b, scale_a, [])
    came_b, came_scales = lax.ppermute(code_b, AXES, swap), lax.ppermute(scales, AXES, swap)
    own_other = jnp.stack([lax.ppermute(block, AXES, flip(1)) for block in own_near])
    (own_sum,) = product(
        functools.partial(own_kernel, pair_size), int_screen, [jnp.stack(own_near), own_other, ints], [],
        own_block.shape[0], ints, ((own_block.shape[0], jnp.float32),), "own_product",
    )
    return join(amp_screen, own_sum, came_scales, (came_a, came_b), row_count)


def column_pairs(piece_width, pair_size, pair_count):
    col_pair = jnp.arange(piece_width) // pair_size
    return (col_pair[None, :] == jnp.arange(pair_count)[:, None]).astype(jnp.bfloat16)


def shards(amplitudes, integrals, amp_screen, int_screen):
    pair_size = TS * TS
    row_count, col_count = amplitudes.shape
    int_count, ab_count = integrals.shape
    tile_count = row_count // TS
    pair_count = amp_screen.shape[1]
    grp_index = lax.axis_index("grp")
    pan_index = lax.axis_index("pan")
    screen_rows = lax.dynamic_slice_in_dim(amp_screen, grp_index * tile_count, tile_count, 0)
    in_pair = grp_index * int_count // pair_size
    out_pair = pan_index * ab_count // pair_size
    int_keep = int_screen[in_pair, out_pair].astype(jnp.bfloat16)
    int_panel = lax.all_gather(integrals * int_keep, "grp", axis=0, tiled=True)
    panel = lax.all_gather(amplitudes, "pan", axis=1, tiled=True)
    piece_width = panel.shape[1]
    onehot = column_pairs(piece_width, pair_size, pair_count)
    keep_mask = jnp.dot(
        screen_rows.astype(jnp.bfloat16), onehot, preferred_element_type=jnp.float32
    ).astype(jnp.bfloat16)
    masked = (panel.reshape(tile_count, TS, piece_width) * keep_mask[:, None, :]).reshape(
        row_count, piece_width
    )
    summed = jnp.dot(masked, int_panel, preferred_element_type=jnp.float32)
    return summed.astype(jnp.bfloat16)


def solution(mesh):
    in_specs = (P("grp", "pan"), P("grp", "pan"), P(), P())
    out_specs = P("grp", "pan")
    pan_count, grp_count = mesh.shape["pan"], mesh.shape["grp"]
    body = shards
    if grp_count == 2 and pan_count >= 4 and pan_count & (pan_count - 1) == 0:
        body = functools.partial(two_group_shards, pan_count)
    return jax.shard_map(body, mesh=mesh, in_specs=in_specs, out_specs=out_specs, check_vma=False)
```

time: 76.4 us -> 70.7 us (0.925)
  local copies, waits for them, and re-layouts: 8.26 us -> 0.7 us
  Pallas kernels: 21.4 us -> 22.4 us
    unnamed x15 -> x6, local copies, waits for them, and re-layouts: 8.26 us -> 0.7 us
    ppermute x29 -> x22, waiting for transfers between devices: 13.5 us -> 14.2 us  [the longest x9 7.5 us: near_blocks(): lax.ppermute(block, AXES, flip(bits))]
    pallas_call x3 -> x4, Pallas kernels: 17.4 us -> 17.6 us  [the longest x3 11.6 us: product(): pl.pallas_call(kernel, out_shape=[jax.ShapeDtypeStruct((rows, ab_count),...]
    ppermute x29 -> x22, starting transfers between devices: 32.8 us -> 32.6 us  [the longest x9 14.8 us: near_blocks(): lax.ppermute(block, AXES, flip(bits))]
  transfers between devices with their start and end apart: 29 -> 22, of which waited for: 8 -> 8; matrix products, arithmetic and copies ran while one was open for 0% -> 0% of each run, Pallas kernels for 23% -> 25%
where the time goes in v3:
time: 70.7 us; the launch traced here: 70.6 us
  starting transfers between devices  32.6 us (46%)
  Pallas kernels  22.4 us (32%)
  waiting for transfers between devices  14.2 us (20%)
    ppermute x9, starting transfers between devices, near_blocks(): lax.ppermute(block, AXES, flip(bits))  14.8 us
    pallas_call x3, Pallas kernels, product(): pl.pallas_call(kernel, out_shape=[jax.ShapeDtypeStruct((rows, ab_count),...  11.6 us
    ppermute x9, waiting for transfers between devices, near_blocks(): lax.ppermute(block, AXES, flip(bits))  7.5 us
    ppermute x2, starting transfers between devices, two_group_shards(): lax.ppermute(part, AXES, first)  7.41 us
    pallas_call x1, Pallas kernels, stage(): pl.pallas_call(stage_kernel, out_shape=[pltpu.VMEM(integrals.shape, integ...  5.92 us
    ppermute x1, waiting for transfers between devices, two_group_shards(): lax.ppermute(scales, AXES, swap)  5.66 us
    ppermute x1, starting transfers between devices, two_group_shards(): lax.ppermute(scales, AXES, swap)  4.81 us
    ppermute x1, starting transfers between devices, two_group_shards(): came_a = lax.ppermute(code_a, AXES, swap)  4.25 us
  transfers between devices with their start and end apart: 22, of which 8 were waited for; matrix products, arithmetic and copies ran while one was open for 0% of the time, Pallas kernels for 25%

profile of v3, /device:TPU:0, one launch (start us, length us, event | category | flops | bytes accessed | tf_op | source)
XLA Modules:
  0.0 70.6 jit_solution(2648131421317093304)
XLA Ops:
  0.0 0.0 copy-start
  0.0 0.0 copy-start.1
  0.0 0.7 copy-done.1
  0.7 1.6 %pick_live.1 = (bf16[128,512]{1,0:T(8,128)(2,1)S(1)}, bf16[128,512]{1,0:T(8,128)(2,1)S(1)}) custom-call(s32[2,16]{1,0:T(2,128)S(1)} %bitcast.25, bf16[512,512]{1,0:T(8,128)(2,1)} %amps_ref.1), custom_call_target="tpu_custom_call" | custom-call | tf_op jit(solution)/shard_map/pick_live/pallas_call | solution.py:63
  2.3 0.5 collective-permute-start.3
  2.8 4.9 %collective-permute-start = (bf16[128,512]{1,0:T(8,128)(2,1)S(1)}, bf16[128,512]{1,0:T(8,128)(2,1)S(1)}, u32[]{:S(2)}, u32[]{:S(2)}) collective-permute-start(bf16[128,512]{1,0:T(8,128)(2,1)S(1)} %get-tuple-element.33), channel_id=1, source_target_pairs={{0,16},{1,0},{2,18},{3,2},{4,20},{5,4},{6,22},{7,6},{8,24},{9,8},{... | collective-permute-start | bytes 393224 | tf_op jit(solution)/shard_map/ppermute | solution.py:285
  7.7 0.0 collective-permute-start.2
  7.7 2.5 %collective-permute-start.1 = (bf16[128,512]{1,0:T(8,128)(2,1)S(1)}, bf16[128,512]{1,0:T(8,128)(2,1)S(1)}, u32[]{:S(2)}, u32[]{:S(2)}) collective-permute-start(bf16[128,512]{1,0:T(8,128)(2,1)S(1)} %get-tuple-element.34), channel_id=1, source_target_pairs={{0,16},{1,0},{2,18},{3,2},{4,20},{5,4},{6,22},{7,6},{8,24},{9,8},{... | collective-permute-start | bytes 393224 | tf_op jit(solution)/shard_map/ppermute | solution.py:285
  10.2 0.0 collective-permute-done.3
  10.2 1.0 %collective-permute-done = bf16[128,512]{1,0:T(8,128)(2,1)S(1)} collective-permute-done((bf16[128,512]{1,0:T(8,128)(2,1)S(1)}, bf16[128,512]{1,0:T(8,128)(2,1)S(1)}, u32[]{:S(2)}, u32[]{:S(2)}) %collective-permute-start) | collective-permute-done | bytes 131104 | tf_op jit(solution)/shard_map/ppermute | solution.py:285
  11.2 7.1 %collective-permute-start.6 = (bf16[128,512]{1,0:T(8,128)(2,1)S(1)}, bf16[128,512]{1,0:T(8,128)(2,1)S(1)}, u32[]{:S(2)}, u32[]{:S(2)}) collective-permute-start(bf16[128,512]{1,0:T(8,128)(2,1)S(1)} %get-tuple-element.41.after.refs_0_), channel_id=1, source_target_pairs={{0,12},{1,13},{2,14},{3,15},{4,8},{5,9},{6,10},{7,11},{8,4},{9,5},... | collective-permute-start | bytes 393224 | tf_op jit(solution)/shard_map/ppermute | solution.py:255
  18.4 0.0 collective-permute-start.5
  18.4 0.6 collective-permute-start.4
  19.0 5.9 %stage_integrals.1 = (bf16[4096,2048]{1,0:T(8,128)(2,1)S(1)}, f32[8,128]{1,0:T(8,128)S(1)}) custom-call(bf16[4096,2048]{1,0:T(8,128)(2,1)} %ints_hbm.1, bf16[128,512]{1,0:T(8,128)(2,1)S(1)} %get-tuple-element.41.after.refs_0_), custom_call_target="tpu_custom_call" | custom-call | flops 1 | bytes 1 | tf_op jit(solution)/shard_map/stage_integrals/pallas_call | solution.py:98
  25.0 0.0 collective-permute-done.2
  25.0 0.0 collective-permute-done.1
  25.0 0.0 collective-permute-done.6.refs_3_
  25.0 0.0 collective-permute-done.5.refs_2_
  25.0 0.9 %collective-permute-done.4.refs_1_ = bf16[128,512]{1,0:T(8,128)(2,1)S(1)} collective-permute-done((bf16[128,512]{1,0:T(8,128)(2,1)S(1)}, bf16[128,512]{1,0:T(8,128)(2,1)S(1)}, u32[]{:S(2)}, u32[]{:S(2)}) %collective-permute-start.4) | collective-permute-done | bytes 131104 | tf_op jit(solution)/shard_map/ppermute | solution.py:255
  25.9 0.1 pad_maximum_fusion.2
  26.0 0.1 collective-permute-start.10
  26.1 2.1 %collective-permute-start.9 = (bf16[128,512]{1,0:T(8,128)(2,1)S(1)}, bf16[128,512]{1,0:T(8,128)(2,1)S(1)}, u32[]{:S(2)}, u32[]{:S(2)}) collective-permute-start(bf16[128,512]{1,0:T(8,128)(2,1)S(1)} %get-tuple-element.53.refs_0_), channel_id=1, source_target_pairs={{0,12},{1,13},{2,14},{3,15},{4,8},{5,9},{6,10},{7,11},{8,4},{9,5},... | collective-permute-start | bytes 393224 | tf_op jit(solution)/shard_map/ppermute | solution.py:255
  28.1 0.1 collective-permute-start.8
  28.2 1.4 %collective-permute-start.7 = (bf16[128,512]{1,0:T(8,128)(2,1)S(1)}, bf16[128,512]{1,0:T(8,128)(2,1)S(1)}, u32[]{:S(2)}, u32[]{:S(2)}) collective-permute-start(bf16[128,512]{1,0:T(8,128)(2,1)S(1)} %get-tuple-element.53.refs_0_), channel_id=1, source_target_pairs={{0,4},{1,5},{2,6},{3,7},{4,0},{5,1},{6,2},{7,3},{8,12},{9,13},{10,... | collective-permute-start | bytes 393224 | tf_op jit(solution)/shard_map/ppermute | solution.py:255
  29.6 0.0 collective-permute-done.10.refs_4_
  29.6 0.0 copy-done
  29.7 3.1 %away_product.2 = (s16[128,2048]{1,0:T(8,128)(2,1)S(1)}, f32[2,2048]{1,0:T(2,128)S(1)}) custom-call(s32[2,8]{1,0:T(2,128)S(1)} %copy-done, bf16[128,512]{1,0:T(8,128)(2,1)S(1)} %get-tuple-element.41.after.refs_0_, bf16[128,512]{1,0:T(8,128)(2,1)S(1)} %collective-permute-done.4.refs_1_, bf16[128,512]{1,0:T(8,128)(2,1)S(1)} %collective-permute-done.5.refs_2_, ...), custom_call_target="tpu_custom_call" | custom-call | flops 1 | bytes 1 | tf_op jit(solution)/shard_map/away_product/pallas_call | solution.py:170
  32.8 0.5 collective-permute-done.9.refs_3_
  33.3 1.5 %collective-permute-done.8.refs_2_ = bf16[128,512]{1,0:T(8,128)(2,1)S(1)} collective-permute-done((bf16[128,512]{1,0:T(8,128)(2,1)S(1)}, bf16[128,512]{1,0:T(8,128)(2,1)S(1)}, u32[]{:S(2)}, u32[]{:S(2)}) %collective-permute-start.8) | collective-permute-done | bytes 131104 | tf_op jit(solution)/shard_map/ppermute | solution.py:255
  34.8 0.9 %collective-permute-done.7.refs_1_ = bf16[128,512]{1,0:T(8,128)(2,1)S(1)} collective-permute-done((bf16[128,512]{1,0:T(8,128)(2,1)S(1)}, bf16[128,512]{1,0:T(8,128)(2,1)S(1)}, u32[]{:S(2)}, u32[]{:S(2)}) %collective-permute-start.7) | collective-permute-done | bytes 131104 | tf_op jit(solution)/shard_map/ppermute | solution.py:255
  35.7 0.1 pad_maximum_fusion.3
  35.8 0.1 collective-permute-start.18
  35.9 0.5 collective-permute-start.14
  36.3 2.0 %collective-permute-start.13 = (bf16[256,512]{1,0:T(8,128)(2,1)S(1)}, bf16[256,512]{1,0:T(8,128)(2,1)S(1)}, u32[]{:S(2)}, u32[]{:S(2)}) collective-permute-start(bf16[256,512]{1,0:T(8,128)(2,1)S(1)} %pad_maximum_fusion.4), channel_id=1, source_target_pairs={{0,12},{1,13},{2,14},{3,15},{4,8},{5,9},{6,10},{7,11},{8,4},{9,5},... | collective-permute-start | bytes 786440 | tf_op jit(solution)/shard_map/ppermute | solution.py:255
  38.3 0.1 collective-permute-start.12
  38.4 1.4 %collective-permute-start.11 = (bf16[256,512]{1,0:T(8,128)(2,1)S(1)}, bf16[256,512]{1,0:T(8,128)(2,1)S(1)}, u32[]{:S(2)}, u32[]{:S(2)}) collective-permute-start(bf16[256,512]{1,0:T(8,128)(2,1)S(1)} %pad_maximum_fusion.4), channel_id=1, source_target_pairs={{0,4},{1,5},{2,6},{3,7},{4,0},{5,1},{6,2},{7,3},{8,12},{9,13},{10,... | collective-permute-start | bytes 786440 | tf_op jit(solution)/shard_map/ppermute | solution.py:255
  39.8 0.0 collective-permute-done.18.refs_4_
  39.8 4.2 %collective-permute-start.20 = (s16[128,2048]{1,0:T(8,128)(2,1)S(1)}, s16[128,2048]{1,0:T(8,128)(2,1)S(1)}, u32[]{:S(2)}, u32[]{:S(2)}) collective-permute-start(s16[128,2048]{1,0:T(8,128)(2,1)S(1)} %get-tuple-element.59), channel_id=1, source_target_pairs={{0,1},{1,0},{2,3},{3,2},{4,5},{5,4},{6,7},{7,6},{8,9},{9,8},{10,11... | collective-permute-start | bytes 1572872 | tf_op jit(solution)/shard_map/ppermute | solution.py:295
  44.1 3.1 %away_product.3 = (s16[128,2048]{1,0:T(8,128)(2,1)S(1)}, f32[4,2048]{1,0:T(4,128)S(1)}) custom-call(s32[2,8]{1,0:T(2,128)S(1)} %copy-done, bf16[128,512]{1,0:T(8,128)(2,1)S(1)} %get-tuple-element.53.refs_0_, bf16[128,512]{1,0:T(8,128)(2,1)S(1)} %collective-permute-done.7.refs_1_, bf16[128,512]{1,0:T(8,128)(2,1)S(1)} %collective-permute-done.8.refs_2_, ...), custom_call_target="tpu_custom_call" | custom-call | flops 1 | bytes 1 | tf_op jit(solution)/shard_map/away_product/pallas_call | solution.py:170
  47.2 0.0 copy-start.2
  47.2 0.0 collective-permute-done.14
  47.2 0.1 collective-permute-start.21
  47.3 0.0 collective-permute-done.13
  47.3 0.1 collective-permute-start.17
  47.4 2.9 %collective-permute-done.12 = bf16[256,512]{1,0:T(8,128)(2,1)S(1)} collective-permute-done((bf16[256,512]{1,0:T(8,128)(2,1)S(1)}, bf16[256,512]{1,0:T(8,128)(2,1)S(1)}, u32[]{:S(2)}, u32[]{:S(2)}) %collective-permute-start.12) | collective-permute-done | bytes 262176 | tf_op jit(solution)/shard_map/ppermute | solution.py:255
  50.3 0.0 collective-permute-start.16
  50.3 0.8 %collective-permute-done.11 = bf16[256,512]{1,0:T(8,128)(2,1)S(1)} collective-permute-done((bf16[256,512]{1,0:T(8,128)(2,1)S(1)}, bf16[256,512]{1,0:T(8,128)(2,1)S(1)}, u32[]{:S(2)}, u32[]{:S(2)}) %collective-permute-start.11) | collective-permute-done | bytes 262176 | tf_op jit(solution)/shard_map/ppermute | solution.py:255
  51.1 0.0 collective-permute-start.15
  51.2 0.1 pad_maximum_fusion.near_ref
  51.3 0.0 collective-permute-done.17
  51.3 4.8 %collective-permute-start.19 = (f32[4,2048]{1,0:T(4,128)S(1)}, f32[4,2048]{1,0:T(4,128)S(1)}, u32[]{:S(2)}, u32[]{:S(2)}) collective-permute-start(f32[4,2048]{1,0:T(4,128)S(1)} %get-tuple-element.58), channel_id=1, source_target_pairs={{0,1},{1,0},{2,3},{3,2},{4,5},{5,4},{6,7},{7,6},{8,9},{9,8},{10,11... | collective-permute-start | bytes 98312 | tf_op jit(solution)/shard_map/ppermute | solution.py:300
  56.1 0.0 collective-permute-done.16
  56.1 0.0 collective-permute-done.15
  56.1 0.1 pad_maximum_fusion.1.other_ref
  56.3 5.4 %own_product.1.own_ref = f32[256,2048]{1,0:T(8,128)S(1)} custom-call(s32[2,8]{1,0:T(2,128)S(1)} %copy-done, bf16[4,256,512]{2,1,0:T(8,128)(2,1)S(1)} %pad_maximum_fusion.near_ref, bf16[4,256,512]{2,1,0:T(8,128)(2,1)S(1)} %pad_maximum_fusion.1.other_ref, bf16[4096,2048]{1,0:T(8,128)(2,1)S(1)} %get-tuple-element.45.refs_5_.ints_ref), custom_call_target="tpu_custom_call" | custom-call | flops 1 | bytes 1 | tf_op jit(solution)/shard_map/own_product/pallas_call | solution.py:170
  61.7 0.0 collective-permute-done.20.refs_0_
  61.7 5.7 %collective-permute-done.19.scale_ref = f32[4,2048]{1,0:T(4,128)S(1)} collective-permute-done((f32[4,2048]{1,0:T(4,128)S(1)}, f32[4,2048]{1,0:T(4,128)S(1)}, u32[]{:S(2)}, u32[]{:S(2)}) %collective-permute-start.19) | collective-permute-done | bytes 32800 | tf_op jit(solution)/shard_map/ppermute | solution.py:300
  67.3 0.0 collective-permute-done.21.refs_1_
  67.3 0.0 copy-done.2
  67.3 3.2 %join.1 = bf16[512,2048]{1,0:T(8,128)(2,1)} custom-call(s32[2,16]{1,0:T(2,128)S(1)} %bitcast.26, f32[256,2048]{1,0:T(8,128)S(1)} %own_product.1.own_ref, f32[4,2048]{1,0:T(4,128)S(1)} %collective-permute-done.19.scale_ref, s16[128,2048]{1,0:T(8,128)(2,1)S(1)} %collective-permute-done.20.refs_0_, s16[128,2048]{1,0:T(8,128)(2,1)S(1)} %collective-permute-done.21.refs_1_), custom_call_target="tpu_custom_call" | custom-call | tf_op jit(solution)/shard_map/join/pallas_call | solution.py:217
  (3 shorter events, 0.1 us)
Async XLA Ops:
  0.0 29.6 %copy-start = (s32[2,8]{1,0:T(2,128)S(1)}, s32[2,8]{1,0:T(2,128)}, u32[]{:S(2)}) copy-start(s32[2,8]{1,0:T(2,128)} %int_screen_ref.5) | copy-start | bytes 196
  0.0 0.7 copy-start.1
  2.3 7.9 %collective-permute-start.3 = (bf16[128,512]{1,0:T(8,128)(2,1)S(1)}, bf16[128,512]{1,0:T(8,128)(2,1)S(1)}, u32[]{:S(2)}, u32[]{:S(2)}) collective-permute-start(bf16[128,512]{1,0:T(8,128)(2,1)S(1)} %get-tuple-element.33), channel_id=1, source_target_pairs={{0,2},{1,16},{2,0},{3,18},{4,6},{5,20},{6,4},{7,22},{8,10},{9,24},... | collective-permute-start | bytes 393224 | tf_op jit(solution)/shard_map/ppermute | solution.py:285
  2.8 8.4 %collective-permute-start = (bf16[128,512]{1,0:T(8,128)(2,1)S(1)}, bf16[128,512]{1,0:T(8,128)(2,1)S(1)}, u32[]{:S(2)}, u32[]{:S(2)}) collective-permute-start(bf16[128,512]{1,0:T(8,128)(2,1)S(1)} %get-tuple-element.33), channel_id=1, source_target_pairs={{0,16},{1,0},{2,18},{3,2},{4,20},{5,4},{6,22},{7,6},{8,24},{9,8},{... | collective-permute-start | bytes 393224 | tf_op jit(solution)/shard_map/ppermute | solution.py:285
  7.7 17.2 %collective-permute-start.2 = (bf16[128,512]{1,0:T(8,128)(2,1)S(1)}, bf16[128,512]{1,0:T(8,128)(2,1)S(1)}, u32[]{:S(2)}, u32[]{:S(2)}) collective-permute-start(bf16[128,512]{1,0:T(8,128)(2,1)S(1)} %get-tuple-element.34), channel_id=1, source_target_pairs={{0,2},{1,16},{2,0},{3,18},{4,6},{5,20},{6,4},{7,22},{8,10},{9,24},... | collective-permute-start | bytes 393224 | tf_op jit(solution)/shard_map/ppermute | solution.py:285
  7.7 17.3 %collective-permute-start.1 = (bf16[128,512]{1,0:T(8,128)(2,1)S(1)}, bf16[128,512]{1,0:T(8,128)(2,1)S(1)}, u32[]{:S(2)}, u32[]{:S(2)}) collective-permute-start(bf16[128,512]{1,0:T(8,128)(2,1)S(1)} %get-tuple-element.34), channel_id=1, source_target_pairs={{0,16},{1,0},{2,18},{3,2},{4,20},{5,4},{6,22},{7,6},{8,24},{9,8},{... | collective-permute-start | bytes 393224 | tf_op jit(solution)/shard_map/ppermute | solution.py:285
  11.2 13.8 %collective-permute-start.6 = (bf16[128,512]{1,0:T(8,128)(2,1)S(1)}, bf16[128,512]{1,0:T(8,128)(2,1)S(1)}, u32[]{:S(2)}, u32[]{:S(2)}) collective-permute-start(bf16[128,512]{1,0:T(8,128)(2,1)S(1)} %get-tuple-element.41.after.refs_0_), channel_id=1, source_target_pairs={{0,12},{1,13},{2,14},{3,15},{4,8},{5,9},{6,10},{7,11},{8,4},{9,5},... | collective-permute-start | bytes 393224 | tf_op jit(solution)/shard_map/ppermute | solution.py:255
  18.4 6.6 %collective-permute-start.5 = (bf16[128,512]{1,0:T(8,128)(2,1)S(1)}, bf16[128,512]{1,0:T(8,128)(2,1)S(1)}, u32[]{:S(2)}, u32[]{:S(2)}) collective-permute-start(bf16[128,512]{1,0:T(8,128)(2,1)S(1)} %get-tuple-element.41.after.refs_0_), channel_id=1, source_target_pairs={{0,8},{1,9},{2,10},{3,11},{4,12},{5,13},{6,14},{7,15},{8,0},{9,1},... | collective-permute-start | bytes 393224 | tf_op jit(solution)/shard_map/ppermute | solution.py:255
  18.4 7.5 %collective-permute-start.4 = (bf16[128,512]{1,0:T(8,128)(2,1)S(1)}, bf16[128,512]{1,0:T(8,128)(2,1)S(1)}, u32[]{:S(2)}, u32[]{:S(2)}) collective-permute-start(bf16[128,512]{1,0:T(8,128)(2,1)S(1)} %get-tuple-element.41.after.refs_0_), channel_id=1, source_target_pairs={{0,4},{1,5},{2,6},{3,7},{4,0},{5,1},{6,2},{7,3},{8,12},{9,13},{10,... | collective-permute-start | bytes 393224 | tf_op jit(solution)/shard_map/ppermute | solution.py:255
  26.0 3.7 %collective-permute-start.10 = (bf16[4,128,512]{2,1,0:T(8,128)(2,1)S(1)}, bf16[4,128,512]{2,1,0:T(8,128)(2,1)S(1)}, u32[]{:S(2)}, u32[]{:S(2)}) collective-permute-start(bf16[4,128,512]{2,1,0:T(8,128)(2,1)S(1)} %pad_maximum_fusion.2), channel_id=1, source_target_pairs={{0,2},{1,3},{2,0},{3,1},{4,6},{5,7},{6,4},{7,5},{8,10},{9,11},{10,... | collective-permute-start | bytes 1572872 | tf_op jit(solution)/shard_map/ppermute | solution.py:276
  26.1 7.3 %collective-permute-start.9 = (bf16[128,512]{1,0:T(8,128)(2,1)S(1)}, bf16[128,512]{1,0:T(8,128)(2,1)S(1)}, u32[]{:S(2)}, u32[]{:S(2)}) collective-permute-start(bf16[128,512]{1,0:T(8,128)(2,1)S(1)} %get-tuple-element.53.refs_0_), channel_id=1, source_target_pairs={{0,12},{1,13},{2,14},{3,15},{4,8},{5,9},{6,10},{7,11},{8,4},{9,5},... | collective-permute-start | bytes 393224 | tf_op jit(solution)/shard_map/ppermute | solution.py:255
  28.1 6.7 %collective-permute-start.8 = (bf16[128,512]{1,0:T(8,128)(2,1)S(1)}, bf16[128,512]{1,0:T(8,128)(2,1)S(1)}, u32[]{:S(2)}, u32[]{:S(2)}) collective-permute-start(bf16[128,512]{1,0:T(8,128)(2,1)S(1)} %get-tuple-element.53.refs_0_), channel_id=1, source_target_pairs={{0,8},{1,9},{2,10},{3,11},{4,12},{5,13},{6,14},{7,15},{8,0},{9,1},... | collective-permute-start | bytes 393224 | tf_op jit(solution)/shard_map/ppermute | solution.py:255
  28.2 7.5 %collective-permute-start.7 = (bf16[128,512]{1,0:T(8,128)(2,1)S(1)}, bf16[128,512]{1,0:T(8,128)(2,1)S(1)}, u32[]{:S(2)}, u32[]{:S(2)}) collective-permute-start(bf16[128,512]{1,0:T(8,128)(2,1)S(1)} %get-tuple-element.53.refs_0_), channel_id=1, source_target_pairs={{0,4},{1,5},{2,6},{3,7},{4,0},{5,1},{6,2},{7,3},{8,12},{9,13},{10,... | collective-permute-start | bytes 393224 | tf_op jit(solution)/shard_map/ppermute | solution.py:255
  35.8 4.1 %collective-permute-start.18 = (bf16[4,128,512]{2,1,0:T(8,128)(2,1)S(1)}, bf16[4,128,512]{2,1,0:T(8,128)(2,1)S(1)}, u32[]{:S(2)}, u32[]{:S(2)}) collective-permute-start(bf16[4,128,512]{2,1,0:T(8,128)(2,1)S(1)} %pad_maximum_fusion.3), channel_id=1, source_target_pairs={{0,2},{1,3},{2,0},{3,1},{4,6},{5,7},{6,4},{7,5},{8,10},{9,11},{10,... | collective-permute-start | bytes 1572872 | tf_op jit(solution)/shard_map/ppermute | solution.py:276
  35.9 11.4 %collective-permute-start.14 = (bf16[256,512]{1,0:T(8,128)(2,1)S(1)}, bf16[256,512]{1,0:T(8,128)(2,1)S(1)}, u32[]{:S(2)}, u32[]{:S(2)}) collective-permute-start(bf16[256,512]{1,0:T(8,128)(2,1)S(1)} %pad_maximum_fusion.4), channel_id=1, source_target_pairs={{0,2},{1,3},{2,0},{3,1},{4,6},{5,7},{6,4},{7,5},{8,10},{9,11},{10,... | collective-permute-start | bytes 786440 | tf_op jit(solution)/shard_map/ppermute | solution.py:301
  36.3 11.0 %collective-permute-start.13 = (bf16[256,512]{1,0:T(8,128)(2,1)S(1)}, bf16[256,512]{1,0:T(8,128)(2,1)S(1)}, u32[]{:S(2)}, u32[]{:S(2)}) collective-permute-start(bf16[256,512]{1,0:T(8,128)(2,1)S(1)} %pad_maximum_fusion.4), channel_id=1, source_target_pairs={{0,12},{1,13},{2,14},{3,15},{4,8},{5,9},{6,10},{7,11},{8,4},{9,5},... | collective-permute-start | bytes 786440 | tf_op jit(solution)/shard_map/ppermute | solution.py:255
  38.3 12.0 %collective-permute-start.12 = (bf16[256,512]{1,0:T(8,128)(2,1)S(1)}, bf16[256,512]{1,0:T(8,128)(2,1)S(1)}, u32[]{:S(2)}, u32[]{:S(2)}) collective-permute-start(bf16[256,512]{1,0:T(8,128)(2,1)S(1)} %pad_maximum_fusion.4), channel_id=1, source_target_pairs={{0,8},{1,9},{2,10},{3,11},{4,12},{5,13},{6,14},{7,15},{8,0},{9,1},... | collective-permute-start | bytes 786440 | tf_op jit(solution)/shard_map/ppermute | solution.py:255
  38.4 12.7 %collective-permute-start.11 = (bf16[256,512]{1,0:T(8,128)(2,1)S(1)}, bf16[256,512]{1,0:T(8,128)(2,1)S(1)}, u32[]{:S(2)}, u32[]{:S(2)}) collective-permute-start(bf16[256,512]{1,0:T(8,128)(2,1)S(1)} %pad_maximum_fusion.4), channel_id=1, source_target_pairs={{0,4},{1,5},{2,6},{3,7},{4,0},{5,1},{6,2},{7,3},{8,12},{9,13},{10,... | collective-permute-start | bytes 786440 | tf_op jit(solution)/shard_map/ppermute | solution.py:255
  39.8 21.8 %collective-permute-start.20 = (s16[128,2048]{1,0:T(8,128)(2,1)S(1)}, s16[128,2048]{1,0:T(8,128)(2,1)S(1)}, u32[]{:S(2)}, u32[]{:S(2)}) collective-permute-start(s16[128,2048]{1,0:T(8,128)(2,1)S(1)} %get-tuple-element.59), channel_id=1, source_target_pairs={{0,1},{1,0},{2,3},{3,2},{4,5},{5,4},{6,7},{7,6},{8,9},{9,8},{10,11... | collective-permute-start | bytes 1572872 | tf_op jit(solution)/shard_map/ppermute | solution.py:295
  47.2 20.1 %copy-start.2 = (s32[16,2]{0,1:T(2,128)S(1)}, s32[16,2]{0,1:T(2,128)}, u32[]{:S(2)}) copy-start(s32[16,2]{0,1:T(2,128)} %param.6) | copy-start | bytes 388
  47.2 20.1 %collective-permute-start.21 = (s16[128,2048]{1,0:T(8,128)(2,1)S(1)}, s16[128,2048]{1,0:T(8,128)(2,1)S(1)}, u32[]{:S(2)}, u32[]{:S(2)}) collective-permute-start(s16[128,2048]{1,0:T(8,128)(2,1)S(1)} %get-tuple-element.60), channel_id=1, source_target_pairs={{0,1},{1,0},{2,3},{3,2},{4,5},{5,4},{6,7},{7,6},{8,9},{9,8},{10,11... | collective-permute-start | bytes 1572872 | tf_op jit(solution)/shard_map/ppermute | solution.py:300
  47.3 4.0 %collective-permute-start.17 = (bf16[256,512]{1,0:T(8,128)(2,1)S(1)}, bf16[256,512]{1,0:T(8,128)(2,1)S(1)}, u32[]{:S(2)}, u32[]{:S(2)}) collective-permute-start(bf16[256,512]{1,0:T(8,128)(2,1)S(1)} %collective-permute-done.13), channel_id=1, source_target_pairs={{0,2},{1,3},{2,0},{3,1},{4,6},{5,7},{6,4},{7,5},{8,10},{9,11},{10,... | collective-permute-start | bytes 786440 | tf_op jit(solution)/shard_map/ppermute | solution.py:301
  50.3 5.8 %collective-permute-start.16 = (bf16[256,512]{1,0:T(8,128)(2,1)S(1)}, bf16[256,512]{1,0:T(8,128)(2,1)S(1)}, u32[]{:S(2)}, u32[]{:S(2)}) collective-permute-start(bf16[256,512]{1,0:T(8,128)(2,1)S(1)} %collective-permute-done.12), channel_id=1, source_target_pairs={{0,2},{1,3},{2,0},{3,1},{4,6},{5,7},{6,4},{7,5},{8,10},{9,11},{10,... | collective-permute-start | bytes 786440 | tf_op jit(solution)/shard_map/ppermute | solution.py:301
  51.1 5.0 %collective-permute-start.15 = (bf16[256,512]{1,0:T(8,128)(2,1)S(1)}, bf16[256,512]{1,0:T(8,128)(2,1)S(1)}, u32[]{:S(2)}, u32[]{:S(2)}) collective-permute-start(bf16[256,512]{1,0:T(8,128)(2,1)S(1)} %collective-permute-done.11), channel_id=1, source_target_pairs={{0,2},{1,3},{2,0},{3,1},{4,6},{5,7},{6,4},{7,5},{8,10},{9,11},{10,... | collective-permute-start | bytes 786440 | tf_op jit(solution)/shard_map/ppermute | solution.py:301
  51.3 16.0 %collective-permute-start.19 = (f32[4,2048]{1,0:T(4,128)S(1)}, f32[4,2048]{1,0:T(4,128)S(1)}, u32[]{:S(2)}, u32[]{:S(2)}) collective-permute-start(f32[4,2048]{1,0:T(4,128)S(1)} %get-tuple-element.58), channel_id=1, source_target_pairs={{0,1},{1,0},{2,3},{3,2},{4,5},{5,4},{6,7},{7,6},{8,9},{9,8},{10,11... | collective-permute-start | bytes 98312 | tf_op jit(solution)/shard_map/ppermute | solution.py:300

commit v4 on v3

--- a/solution.py
+++ b/solution.py
@@ -35,28 +35,20 @@
     return slots, count
 
 
-def pick_kernel(pair_size, screen_hbm, amps_ref, *rest):
-    picked_refs, (screen_ref, screen_sem, sem) = rest[:-3], rest[-3:]
-    screen_copy = pltpu.make_async_copy(screen_hbm, screen_ref, screen_sem)
+def pick_kernel(pair_size, screen_hbm, amps_hbm, *rest):
+    picked_refs, (screen_ref, amps_ref, sem) = rest[:-3], rest[-3:]
+    screen_copy = pltpu.make_async_copy(screen_hbm, screen_ref, sem.at[0])
+    amps_copy = pltpu.make_async_copy(amps_hbm, amps_ref, sem.at[1])
     screen_copy.start()
+    amps_copy.start()
     screen_copy.wait()
     column = lax.axis_index("pan") * amps_ref.shape[1] // pair_size
     slots, _ = live_slots(screen_ref, lax.axis_index("grp") * BLOCK_TILES, column)
-    copies = []
+    amps_copy.wait()
     for (first, last), picked_ref in zip(SLOT_CHUNKS, picked_refs):
         for slot in range(first, last):
             rows = pl.ds(pl.multiple_of(slots[slot] * TS, TS), TS)
-            copies.append(
-                pltpu.make_async_copy(
-                    amps_ref.at[rows, :],
-                    picked_ref.at[pl.ds((slot - first) * TS, TS), :],
-                    sem.at[slot],
-                )
-            )
-    for copy in copies:
-        copy.start()
-    for copy in copies:
-        copy.wait()
+            picked_ref[(slot - first) * TS : (slot - first + 1) * TS, :] = amps_ref[rows, :]
 
 
 def pick_live(amplitudes, amp_screen, pair_size):
@@ -66,16 +58,20 @@
             jax.ShapeDtypeStruct(((last - first) * TS, amplitudes.shape[1]), amplitudes.dtype)
             for first, last in SLOT_CHUNKS
         ],
-        in_specs=[pl.BlockSpec(memory_space=pl.ANY), pl.BlockSpec(memory_space=pltpu.HBM)],
+        in_specs=[pl.BlockSpec(memory_space=pltpu.HBM)] * 2,
         out_specs=[WHOLE] * len(SLOT_CHUNKS),
         scratch_shapes=[
             pltpu.SMEM(amp_screen.shape, amp_screen.dtype),
-            pltpu.SemaphoreType.DMA,
-            pltpu.SemaphoreType.DMA((LIVE_MAX,)),
+            pltpu.VMEM(amplitudes.shape, amplitudes.dtype),
+            pltpu.SemaphoreType.DMA((2,)),
         ],
         compiler_params=pltpu.CompilerParams(vmem_limit_bytes=SMALL_VMEM),
         name="pick_live",
-    )(amp_screen, pltpu.with_memory_space_constraint(amplitudes, pltpu.HBM))
+    )(in_hbm(amp_screen), in_hbm(amplitudes))
+
+
+def in_hbm(array):
+    return pltpu.with_memory_space_constraint(array, pltpu.HBM)
 
 
 def stage_kernel(ints_hbm, after, ints_ref, staged_ref, sem):
@@ -104,7 +100,7 @@
         compiler_params=pltpu.CompilerParams(vmem_limit_bytes=SMALL_VMEM),
         cost_estimate=LIGHT,
         name="stage_integrals",
-    )(pltpu.with_memory_space_constraint(integrals, pltpu.HBM), after)
+    )(in_hbm(integrals), after)
 
 
 def lay_out(near, other_ref, panel):
@@ -182,46 +178,59 @@
 
 
 def join_kernel(screen_ref, own_ref, scale_ref, *refs):
-    code_refs, (out_ref, total) = refs[:-2], refs[-2:]
+    code_refs, (out_hbm, held, sem) = refs[: len(SLOT_CHUNKS)], refs[len(SLOT_CHUNKS) :]
     grp_index = lax.axis_index("grp")
     first_tile = grp_index * BLOCK_TILES
     own_slots, own_count = live_slots(screen_ref, first_tile, grp_index)
     slots, count = live_slots(screen_ref, first_tile, 1 - grp_index)
-    total[...] = jnp.zeros_like(total)
-    for slot in range(LIVE_MAX):
-
-        @pl.when(slot < own_count)
-        def _():
-            rows = pl.ds(pl.multiple_of(own_slots[slot] * TS, TS), TS)
-            total[rows, :] = own_ref[slot * TS : (slot + 1) * TS, :]
-
-    for (first, last), code_ref in zip(SLOT_CHUNKS, code_refs):
-        for slot in range(first, last):
-
-            @pl.when(slot < count)
+
+    def tile_rows(slot):
+        return pl.ds(pl.multiple_of(slot * TS, TS), TS)
+
+    copies = []
+    for part in range(own_ref.shape[1] // JOIN_TILE):
+        columns = slice(part * JOIN_TILE, (part + 1) * JOIN_TILE)
+        held_part = held.at[part]
+        held_part[...] = jnp.zeros_like(held_part)
+        for slot in range(LIVE_MAX):
+
+            @pl.when(slot < own_count)
             def _():
-                rows = pl.ds(pl.multiple_of(slots[slot] * TS, TS), TS)
-                code = code_ref[(slot - first) * TS : (slot - first + 1) * TS, :].astype(jnp.float32)
-                total[rows, :] += code * scale_ref[slot : slot + 1, :]
-
-    out_ref[...] = total[...].astype(out_ref.dtype)
+                held_part[tile_rows(own_slots[slot]), :] = own_ref[slot * TS : (slot + 1) * TS, columns].astype(held.dtype)
+
+        for (first, last), code_ref in zip(SLOT_CHUNKS, code_refs):
+            for slot in range(first, last):
+
+                @pl.when(slot < count)
+                def _():
+                    code = code_ref[(slot - first) * TS : (slot - first + 1) * TS, columns].astype(jnp.float32)
+                    away = code * scale_ref[slot : slot + 1, columns]
+                    at = jnp.int32(-1)
+                    for own_slot in range(LIVE_MAX):
+                        at = jnp.where((own_slot < own_count) & (own_slots[own_slot] == slots[slot]), own_slot, at)
+                    own = own_ref[tile_rows(jnp.maximum(at, 0)), columns]
+                    total = away + jnp.where(at >= 0, own, 0.0)
+                    held_part[tile_rows(slots[slot]), :] = total.astype(held.dtype)
+
+        copies.append(pltpu.make_async_copy(held_part, out_hbm.at[:, columns], sem.at[part]))
+        copies[-1].start()
+    for copy in copies:
+        copy.wait()
 
 
 def join(amp_screen, own_sum, scales, codes, row_count):
     ab_count = own_sum.shape[1]
     arrays = [own_sum, scales, *codes]
-
-    def tall(rows):
-        return pl.BlockSpec((rows, JOIN_TILE), lambda j: (0, j))
-
     return pl.pallas_call(
         join_kernel,
-        grid=(ab_count // JOIN_TILE,),
         out_shape=jax.ShapeDtypeStruct((row_count, ab_count), jnp.bfloat16),
-        in_specs=[pl.BlockSpec(memory_space=pltpu.SMEM)] + [tall(array.shape[0]) for array in arrays],
-        out_specs=tall(row_count),
-        scratch_shapes=[pltpu.VMEM((row_count, JOIN_TILE), jnp.float32)],
-        compiler_params=pltpu.CompilerParams(vmem_limit_bytes=SMALL_VMEM),
+        in_specs=[pl.BlockSpec(memory_space=pltpu.SMEM)] + [WHOLE] * len(arrays),
+        out_specs=pl.BlockSpec(memory_space=pltpu.HBM),
+        scratch_shapes=[
+            pltpu.VMEM((ab_count // JOIN_TILE, row_count, JOIN_TILE), jnp.bfloat16),
+            pltpu.SemaphoreType.DMA((ab_count // JOIN_TILE,)),
+        ],
+        compiler_params=pltpu.CompilerParams(vmem_limit_bytes=PRODUCT_VMEM),
         name="join",
     )(amp_screen, *arrays)
 
@@ -298,6 +307,7 @@
     own_near = near_blocks(own_block, flip, block_count)
     code_b, scales = away_product(near_b, scale_a, [])
     came_b, came_scales = lax.ppermute(code_b, AXES, swap), lax.ppermute(scales, AXES, swap)
+    own_near, came_a = lax.optimization_barrier((own_near, came_a))
     own_other = jnp.stack([lax.ppermute(block, AXES, flip(1)) for block in own_near])
     (own_sum,) = product(
         functools.partial(own_kernel, pair_size), int_screen, [jnp.stack(own_near), own_other, ints], [],

time: 70.7 us -> 64.7 us (0.915)
  starting transfers between devices: 32.6 us -> 24.7 us
  waiting for transfers between devices: 14.2 us -> 18.5 us
  Pallas kernels: 22.4 us -> 20.8 us
    ppermute x9, waiting for transfers between devices: 7.5 us -> 13.7 us  [near_blocks(): lax.ppermute(block, AXES, flip(bits))]
    ppermute x1, waiting for transfers between devices: 5.66 us -> 1.06 us  [two_group_shards(): lax.ppermute(scales, AXES, swap)]
    ppermute x1, starting transfers between devices: 4.81 us -> 0.27 us  [two_group_shards(): lax.ppermute(scales, AXES, swap)]
    ppermute x2, starting transfers between devices: 7.41 us -> 5.61 us  [two_group_shards(): lax.ppermute(part, AXES, first)]
    ppermute x2, waiting for transfers between devices: 1.01 us -> 2.42 us  [two_group_shards(): lax.ppermute(part, AXES, first)]
    ppermute x1, starting transfers between devices: 4.25 us -> 2.91 us  [two_group_shards(): came_a = lax.ppermute(code_a, AXES, swap)]
    ppermute x4, waiting for transfers between devices: 0.01 us -> 1.23 us  [two_group_shards(): lax.ppermute(block, AXES, flip(1))]
    pallas_call x1, Pallas kernels: 3.24 us -> 2.15 us  [join(): pl.pallas_call(join_kernel, out_shape=jax.ShapeDtypeStruct((row_count, ab...]
  transfers between devices with their start and end apart: 22 -> 22, of which waited for: 8 -> 12; matrix products, arithmetic and copies ran while one was open for 0% -> 1% of each run, Pallas kernels for 25% -> 27%
where the time goes in v4:
time: 64.7 us; the launch traced here: 64.6 us
  starting transfers between devices  24.7 us (38%)
  Pallas kernels  20.8 us (32%)
  waiting for transfers between devices  18.5 us (29%)
    ppermute x9, starting transfers between devices, near_blocks(): lax.ppermute(block, AXES, flip(bits))  14.6 us
    ppermute x9, waiting for transfers between devices, near_blocks(): lax.ppermute(block, AXES, flip(bits))  13.7 us
    pallas_call x3, Pallas kernels, product(): pl.pallas_call(kernel, out_shape=[jax.ShapeDtypeStruct((rows, ab_count),...  11.6 us
    pallas_call x1, Pallas kernels, stage(): pl.pallas_call(stage_kernel, out_shape=[pltpu.VMEM(integrals.shape, integ...  5.92 us
    ppermute x2, starting transfers between devices, two_group_shards(): lax.ppermute(part, AXES, first)  5.61 us
    ppermute x1, starting transfers between devices, two_group_shards(): came_a = lax.ppermute(code_a, AXES, swap)  2.91 us
    ppermute x2, waiting for transfers between devices, two_group_shards(): lax.ppermute(part, AXES, first)  2.42 us
    pallas_call x1, Pallas kernels, join(): pl.pallas_call(join_kernel, out_shape=jax.ShapeDtypeStruct((row_count, ab...  2.15 us
  transfers between devices with their start and end apart: 22, of which 12 were waited for; matrix products, arithmetic and copies ran while one was open for 1% of the time, Pallas kernels for 27%

profile of v4, /device:TPU:0, one launch (start us, length us, event | category | flops | bytes accessed | tf_op | source)
XLA Modules:
  0.0 64.6 jit_solution(18432404803109430101)
XLA Ops:
  0.0 0.0 copy-start
  0.0 1.1 %pick_live.1 = (bf16[128,512]{1,0:T(8,128)(2,1)S(1)}, bf16[128,512]{1,0:T(8,128)(2,1)S(1)}) custom-call(s32[2,16]{1,0:T(2,128)} %bitcast.25, bf16[512,512]{1,0:T(8,128)(2,1)} %amps_hbm.1), custom_call_target="tpu_custom_call" | custom-call | tf_op jit(solution)/shard_map/pick_live/pallas_call | solution.py:55
  1.1 4.1 %collective-permute-start = (bf16[128,512]{1,0:T(8,128)(2,1)S(1)}, bf16[128,512]{1,0:T(8,128)(2,1)S(1)}, u32[]{:S(2)}, u32[]{:S(2)}) collective-permute-start(bf16[128,512]{1,0:T(8,128)(2,1)S(1)} %get-tuple-element.38), channel_id=1, source_target_pairs={{0,16},{1,0},{2,18},{3,2},{4,20},{5,4},{6,22},{7,6},{8,24},{9,8},{... | collective-permute-start | bytes 393224 | tf_op jit(solution)/shard_map/ppermute | solution.py:294
  5.2 0.0 collective-permute-start.3
  5.2 1.5 %collective-permute-start.1 = (bf16[128,512]{1,0:T(8,128)(2,1)S(1)}, bf16[128,512]{1,0:T(8,128)(2,1)S(1)}, u32[]{:S(2)}, u32[]{:S(2)}) collective-permute-start(bf16[128,512]{1,0:T(8,128)(2,1)S(1)} %get-tuple-element.39), channel_id=1, source_target_pairs={{0,16},{1,0},{2,18},{3,2},{4,20},{5,4},{6,22},{7,6},{8,24},{9,8},{... | collective-permute-start | bytes 393224 | tf_op jit(solution)/shard_map/ppermute | solution.py:294
  6.7 0.0 collective-permute-start.2
  6.7 2.4 %collective-permute-done = bf16[128,512]{1,0:T(8,128)(2,1)S(1)} collective-permute-done((bf16[128,512]{1,0:T(8,128)(2,1)S(1)}, bf16[128,512]{1,0:T(8,128)(2,1)S(1)}, u32[]{:S(2)}, u32[]{:S(2)}) %collective-permute-start) | collective-permute-done | bytes 131104 | tf_op jit(solution)/shard_map/ppermute | solution.py:294
  9.1 0.0 collective-permute-done.3
  9.2 1.6 %collective-permute-start.4 = (bf16[128,512]{1,0:T(8,128)(2,1)S(1)}, bf16[128,512]{1,0:T(8,128)(2,1)S(1)}, u32[]{:S(2)}, u32[]{:S(2)}) collective-permute-start(bf16[128,512]{1,0:T(8,128)(2,1)S(1)} %get-tuple-element.46.after.refs_0_), channel_id=1, source_target_pairs={{0,4},{1,5},{2,6},{3,7},{4,0},{5,1},{6,2},{7,3},{8,12},{9,13},{10,... | collective-permute-start | bytes 393224 | tf_op jit(solution)/shard_map/ppermute | solution.py:264
  10.7 6.0 %collective-permute-start.5 = (bf16[128,512]{1,0:T(8,128)(2,1)S(1)}, bf16[128,512]{1,0:T(8,128)(2,1)S(1)}, u32[]{:S(2)}, u32[]{:S(2)}) collective-permute-start(bf16[128,512]{1,0:T(8,128)(2,1)S(1)} %get-tuple-element.46.after.refs_0_), channel_id=1, source_target_pairs={{0,8},{1,9},{2,10},{3,11},{4,12},{5,13},{6,14},{7,15},{8,0},{9,1},... | collective-permute-start | bytes 393224 | tf_op jit(solution)/shard_map/ppermute | solution.py:264
  16.7 0.0 collective-permute-start.6
  16.7 5.9 %stage_integrals.1 = (bf16[4096,2048]{1,0:T(8,128)(2,1)S(1)}, f32[8,128]{1,0:T(8,128)S(1)}) custom-call(bf16[4096,2048]{1,0:T(8,128)(2,1)} %ints_hbm.1, bf16[128,512]{1,0:T(8,128)(2,1)S(1)} %get-tuple-element.46.after.refs_0_), custom_call_target="tpu_custom_call" | custom-call | flops 1 | bytes 1 | tf_op jit(solution)/shard_map/stage_integrals/pallas_call | solution.py:94
  22.6 0.0 collective-permute-done.1
  22.7 0.0 collective-permute-done.2
  22.7 0.0 collective-permute-done.4.refs_1_
  22.7 0.0 collective-permute-done.5.refs_2_
  22.7 2.2 %collective-permute-done.6.refs_3_ = bf16[128,512]{1,0:T(8,128)(2,1)S(1)} collective-permute-done((bf16[128,512]{1,0:T(8,128)(2,1)S(1)}, bf16[128,512]{1,0:T(8,128)(2,1)S(1)}, u32[]{:S(2)}, u32[]{:S(2)}) %collective-permute-start.6) | collective-permute-done | bytes 131104 | tf_op jit(solution)/shard_map/ppermute | solution.py:264
  24.9 0.1 pad_maximum_fusion.2
  25.0 0.1 collective-permute-start.10
  25.0 0.6 collective-permute-start.7
  25.6 0.8 %collective-permute-start.8 = (bf16[128,512]{1,0:T(8,128)(2,1)S(1)}, bf16[128,512]{1,0:T(8,128)(2,1)S(1)}, u32[]{:S(2)}, u32[]{:S(2)}) collective-permute-start(bf16[128,512]{1,0:T(8,128)(2,1)S(1)} %get-tuple-element.63.refs_0_), channel_id=1, source_target_pairs={{0,8},{1,9},{2,10},{3,11},{4,12},{5,13},{6,14},{7,15},{8,0},{9,1},... | collective-permute-start | bytes 393224 | tf_op jit(solution)/shard_map/ppermute | solution.py:264
  26.4 2.2 %collective-permute-start.9 = (bf16[128,512]{1,0:T(8,128)(2,1)S(1)}, bf16[128,512]{1,0:T(8,128)(2,1)S(1)}, u32[]{:S(2)}, u32[]{:S(2)}) collective-permute-start(bf16[128,512]{1,0:T(8,128)(2,1)S(1)} %get-tuple-element.63.refs_0_), channel_id=1, source_target_pairs={{0,12},{1,13},{2,14},{3,15},{4,8},{5,9},{6,10},{7,11},{8,4},{9,5},... | collective-permute-start | bytes 393224 | tf_op jit(solution)/shard_map/ppermute | solution.py:264
  28.6 0.0 collective-permute-done.10.refs_4_
  28.6 0.0 copy-done
  28.6 3.1 %away_product.2 = (s16[128,2048]{1,0:T(8,128)(2,1)S(1)}, f32[2,2048]{1,0:T(2,128)S(1)}) custom-call(s32[2,8]{1,0:T(2,128)S(1)} %copy-done, bf16[128,512]{1,0:T(8,128)(2,1)S(1)} %get-tuple-element.46.after.refs_0_, bf16[128,512]{1,0:T(8,128)(2,1)S(1)} %collective-permute-done.4.refs_1_, bf16[128,512]{1,0:T(8,128)(2,1)S(1)} %collective-permute-done.5.refs_2_, ...), custom_call_target="tpu_custom_call" | custom-call | flops 1 | bytes 1 | tf_op jit(solution)/shard_map/away_product/pallas_call | solution.py:166
  31.8 0.0 collective-permute-done.7.refs_1_
  31.8 0.2 collective-permute-done.8.refs_2_
  32.0 3.0 %collective-permute-done.9.refs_3_ = bf16[128,512]{1,0:T(8,128)(2,1)S(1)} collective-permute-done((bf16[128,512]{1,0:T(8,128)(2,1)S(1)}, bf16[128,512]{1,0:T(8,128)(2,1)S(1)}, u32[]{:S(2)}, u32[]{:S(2)}) %collective-permute-start.9) | collective-permute-done | bytes 131104 | tf_op jit(solution)/shard_map/ppermute | solution.py:264
  35.0 0.1 pad_maximum_fusion.3
  35.0 0.1 collective-permute-start.19
  35.1 2.9 %collective-permute-start.14 = (s16[128,2048]{1,0:T(8,128)(2,1)S(1)}, s16[128,2048]{1,0:T(8,128)(2,1)S(1)}, u32[]{:S(2)}, u32[]{:S(2)}) collective-permute-start(s16[128,2048]{1,0:T(8,128)(2,1)S(1)} %get-tuple-element.58), channel_id=1, source_target_pairs={{0,1},{1,0},{2,3},{3,2},{4,5},{5,4},{6,7},{7,6},{8,9},{9,8},{10,11... | collective-permute-start | bytes 1572872 | tf_op jit(solution)/shard_map/ppermute | solution.py:304
  38.0 1.6 %collective-permute-start.11 = (bf16[256,512]{1,0:T(8,128)(2,1)S(1)}, bf16[256,512]{1,0:T(8,128)(2,1)S(1)}, u32[]{:S(2)}, u32[]{:S(2)}) collective-permute-start(bf16[256,512]{1,0:T(8,128)(2,1)S(1)} %pad_maximum_fusion.4), channel_id=1, source_target_pairs={{0,4},{1,5},{2,6},{3,7},{4,0},{5,1},{6,2},{7,3},{8,12},{9,13},{10,... | collective-permute-start | bytes 786440 | tf_op jit(solution)/shard_map/ppermute | solution.py:264
  39.6 0.3 collective-permute-start.12
  39.9 1.6 %collective-permute-start.13 = (bf16[256,512]{1,0:T(8,128)(2,1)S(1)}, bf16[256,512]{1,0:T(8,128)(2,1)S(1)}, u32[]{:S(2)}, u32[]{:S(2)}) collective-permute-start(bf16[256,512]{1,0:T(8,128)(2,1)S(1)} %pad_maximum_fusion.4), channel_id=1, source_target_pairs={{0,12},{1,13},{2,14},{3,15},{4,8},{5,9},{6,10},{7,11},{8,4},{9,5},... | collective-permute-start | bytes 786440 | tf_op jit(solution)/shard_map/ppermute | solution.py:264
  41.5 0.0 collective-permute-done.19.refs_4_
  41.5 3.1 %away_product.3 = (s16[128,2048]{1,0:T(8,128)(2,1)S(1)}, f32[4,2048]{1,0:T(4,128)S(1)}) custom-call(s32[2,8]{1,0:T(2,128)S(1)} %copy-done, bf16[128,512]{1,0:T(8,128)(2,1)S(1)} %get-tuple-element.63.refs_0_, bf16[128,512]{1,0:T(8,128)(2,1)S(1)} %collective-permute-done.7.refs_1_, bf16[128,512]{1,0:T(8,128)(2,1)S(1)} %collective-permute-done.8.refs_2_, ...), custom_call_target="tpu_custom_call" | custom-call | flops 1 | bytes 1 | tf_op jit(solution)/shard_map/away_product/pallas_call | solution.py:166
  44.6 0.0 copy-start.1
  44.6 0.1 collective-permute-start.21
  44.8 1.6 %collective-permute-done.11 = bf16[256,512]{1,0:T(8,128)(2,1)S(1)} collective-permute-done((bf16[256,512]{1,0:T(8,128)(2,1)S(1)}, bf16[256,512]{1,0:T(8,128)(2,1)S(1)}, u32[]{:S(2)}, u32[]{:S(2)}) %collective-permute-start.11) | collective-permute-done | bytes 262176 | tf_op jit(solution)/shard_map/ppermute | solution.py:264
  46.4 2.4 %collective-permute-done.12 = bf16[256,512]{1,0:T(8,128)(2,1)S(1)} collective-permute-done((bf16[256,512]{1,0:T(8,128)(2,1)S(1)}, bf16[256,512]{1,0:T(8,128)(2,1)S(1)}, u32[]{:S(2)}, u32[]{:S(2)}) %collective-permute-start.12) | collective-permute-done | bytes 262176 | tf_op jit(solution)/shard_map/ppermute | solution.py:264
  48.8 4.4 %collective-permute-done.13 = bf16[256,512]{1,0:T(8,128)(2,1)S(1)} collective-permute-done((bf16[256,512]{1,0:T(8,128)(2,1)S(1)}, bf16[256,512]{1,0:T(8,128)(2,1)S(1)}, u32[]{:S(2)}, u32[]{:S(2)}) %collective-permute-start.13) | collective-permute-done | bytes 262176 | tf_op jit(solution)/shard_map/ppermute | solution.py:264
  53.2 0.0 collective-permute-done.14.refs_0_
  53.2 0.0 collective-permute-start.18
  53.2 0.5 collective-permute-start.17
  53.7 0.0 collective-permute-start.16
  53.7 0.5 collective-permute-start.15
  54.2 0.1 pad_maximum_fusion.near_ref
  54.3 0.4 collective-permute-done.18
  54.7 0.3 collective-permute-start.20
  55.0 0.1 collective-permute-done.17
  55.1 0.4 collective-permute-done.16
  55.5 0.4 collective-permute-done.15
  55.9 0.1 pad_maximum_fusion.1.other_ref
  56.0 5.4 %own_product.1.own_ref = f32[256,2048]{1,0:T(8,128)S(1)} custom-call(s32[2,8]{1,0:T(2,128)S(1)} %copy-done, bf16[4,256,512]{2,1,0:T(8,128)(2,1)S(1)} %pad_maximum_fusion.near_ref, bf16[4,256,512]{2,1,0:T(8,128)(2,1)S(1)} %pad_maximum_fusion.1.other_ref, bf16[4096,2048]{1,0:T(8,128)(2,1)S(1)} %get-tuple-element.50.refs_5_.ints_ref), custom_call_target="tpu_custom_call" | custom-call | flops 1 | bytes 1 | tf_op jit(solution)/shard_map/own_product/pallas_call | solution.py:166
  61.4 1.1 %collective-permute-done.20.scale_ref = f32[4,2048]{1,0:T(4,128)S(1)} collective-permute-done((f32[4,2048]{1,0:T(4,128)S(1)}, f32[4,2048]{1,0:T(4,128)S(1)}, u32[]{:S(2)}, u32[]{:S(2)}) %collective-permute-start.20) | collective-permute-done | bytes 32800 | tf_op jit(solution)/shard_map/ppermute | solution.py:309
  62.5 0.0 collective-permute-done.21.refs_1_
  62.5 0.0 copy-done.1
  62.5 2.1 %join.1 = bf16[512,2048]{1,0:T(8,128)(2,1)} custom-call(s32[2,16]{1,0:T(2,128)S(1)} %bitcast.26, f32[256,2048]{1,0:T(8,128)S(1)} %own_product.1.own_ref, f32[4,2048]{1,0:T(4,128)S(1)} %collective-permute-done.20.scale_ref, s16[128,2048]{1,0:T(8,128)(2,1)S(1)} %collective-permute-done.14.refs_0_, s16[128,2048]{1,0:T(8,128)(2,1)S(1)} %collective-permute-done.21.refs_1_), custom_call_target="tpu_custom_call" | custom-call | tf_op jit(solution)/shard_map/join/pallas_call | solution.py:224
  (3 shorter events, 0.1 us)
Async XLA Ops:
  0.0 28.6 %copy-start = (s32[2,8]{1,0:T(2,128)S(1)}, s32[2,8]{1,0:T(2,128)}, u32[]{:S(2)}) copy-start(s32[2,8]{1,0:T(2,128)} %int_screen_ref.5) | copy-start | bytes 196
  1.1 8.0 %collective-permute-start = (bf16[128,512]{1,0:T(8,128)(2,1)S(1)}, bf16[128,512]{1,0:T(8,128)(2,1)S(1)}, u32[]{:S(2)}, u32[]{:S(2)}) collective-permute-start(bf16[128,512]{1,0:T(8,128)(2,1)S(1)} %get-tuple-element.38), channel_id=1, source_target_pairs={{0,16},{1,0},{2,18},{3,2},{4,20},{5,4},{6,22},{7,6},{8,24},{9,8},{... | collective-permute-start | bytes 393224 | tf_op jit(solution)/shard_map/ppermute | solution.py:294
  5.2 3.9 %collective-permute-start.3 = (bf16[128,512]{1,0:T(8,128)(2,1)S(1)}, bf16[128,512]{1,0:T(8,128)(2,1)S(1)}, u32[]{:S(2)}, u32[]{:S(2)}) collective-permute-start(bf16[128,512]{1,0:T(8,128)(2,1)S(1)} %get-tuple-element.38), channel_id=1, source_target_pairs={{0,2},{1,16},{2,0},{3,18},{4,6},{5,20},{6,4},{7,22},{8,10},{9,24},... | collective-permute-start | bytes 393224 | tf_op jit(solution)/shard_map/ppermute | solution.py:294
  5.2 17.5 %collective-permute-start.1 = (bf16[128,512]{1,0:T(8,128)(2,1)S(1)}, bf16[128,512]{1,0:T(8,128)(2,1)S(1)}, u32[]{:S(2)}, u32[]{:S(2)}) collective-permute-start(bf16[128,512]{1,0:T(8,128)(2,1)S(1)} %get-tuple-element.39), channel_id=1, source_target_pairs={{0,16},{1,0},{2,18},{3,2},{4,20},{5,4},{6,22},{7,6},{8,24},{9,8},{... | collective-permute-start | bytes 393224 | tf_op jit(solution)/shard_map/ppermute | solution.py:294
  6.7 15.9 %collective-permute-start.2 = (bf16[128,512]{1,0:T(8,128)(2,1)S(1)}, bf16[128,512]{1,0:T(8,128)(2,1)S(1)}, u32[]{:S(2)}, u32[]{:S(2)}) collective-permute-start(bf16[128,512]{1,0:T(8,128)(2,1)S(1)} %get-tuple-element.39), channel_id=1, source_target_pairs={{0,2},{1,16},{2,0},{3,18},{4,6},{5,20},{6,4},{7,22},{8,10},{9,24},... | collective-permute-start | bytes 393224 | tf_op jit(solution)/shard_map/ppermute | solution.py:294
  9.2 13.5 %collective-permute-start.4 = (bf16[128,512]{1,0:T(8,128)(2,1)S(1)}, bf16[128,512]{1,0:T(8,128)(2,1)S(1)}, u32[]{:S(2)}, u32[]{:S(2)}) collective-permute-start(bf16[128,512]{1,0:T(8,128)(2,1)S(1)} %get-tuple-element.46.after.refs_0_), channel_id=1, source_target_pairs={{0,4},{1,5},{2,6},{3,7},{4,0},{5,1},{6,2},{7,3},{8,12},{9,13},{10,... | collective-permute-start | bytes 393224 | tf_op jit(solution)/shard_map/ppermute | solution.py:264
  10.7 12.0 %collective-permute-start.5 = (bf16[128,512]{1,0:T(8,128)(2,1)S(1)}, bf16[128,512]{1,0:T(8,128)(2,1)S(1)}, u32[]{:S(2)}, u32[]{:S(2)}) collective-permute-start(bf16[128,512]{1,0:T(8,128)(2,1)S(1)} %get-tuple-element.46.after.refs_0_), channel_id=1, source_target_pairs={{0,8},{1,9},{2,10},{3,11},{4,12},{5,13},{6,14},{7,15},{8,0},{9,1},... | collective-permute-start | bytes 393224 | tf_op jit(solution)/shard_map/ppermute | solution.py:264
  16.7 8.2 %collective-permute-start.6 = (bf16[128,512]{1,0:T(8,128)(2,1)S(1)}, bf16[128,512]{1,0:T(8,128)(2,1)S(1)}, u32[]{:S(2)}, u32[]{:S(2)}) collective-permute-start(bf16[128,512]{1,0:T(8,128)(2,1)S(1)} %get-tuple-element.46.after.refs_0_), channel_id=1, source_target_pairs={{0,12},{1,13},{2,14},{3,15},{4,8},{5,9},{6,10},{7,11},{8,4},{9,5},... | collective-permute-start | bytes 393224 | tf_op jit(solution)/shard_map/ppermute | solution.py:264
  25.0 3.7 %collective-permute-start.10 = (bf16[4,128,512]{2,1,0:T(8,128)(2,1)S(1)}, bf16[4,128,512]{2,1,0:T(8,128)(2,1)S(1)}, u32[]{:S(2)}, u32[]{:S(2)}) collective-permute-start(bf16[4,128,512]{2,1,0:T(8,128)(2,1)S(1)} %pad_maximum_fusion.2), channel_id=1, source_target_pairs={{0,2},{1,3},{2,0},{3,1},{4,6},{5,7},{6,4},{7,5},{8,10},{9,11},{10,... | collective-permute-start | bytes 1572872 | tf_op jit(solution)/shard_map/ppermute | solution.py:285
  25.0 6.7 %collective-permute-start.7 = (bf16[128,512]{1,0:T(8,128)(2,1)S(1)}, bf16[128,512]{1,0:T(8,128)(2,1)S(1)}, u32[]{:S(2)}, u32[]{:S(2)}) collective-permute-start(bf16[128,512]{1,0:T(8,128)(2,1)S(1)} %get-tuple-element.63.refs_0_), channel_id=1, source_target_pairs={{0,4},{1,5},{2,6},{3,7},{4,0},{5,1},{6,2},{7,3},{8,12},{9,13},{10,... | collective-permute-start | bytes 393224 | tf_op jit(solution)/shard_map/ppermute | solution.py:264
  25.6 6.3 %collective-permute-start.8 = (bf16[128,512]{1,0:T(8,128)(2,1)S(1)}, bf16[128,512]{1,0:T(8,128)(2,1)S(1)}, u32[]{:S(2)}, u32[]{:S(2)}) collective-permute-start(bf16[128,512]{1,0:T(8,128)(2,1)S(1)} %get-tuple-element.63.refs_0_), channel_id=1, source_target_pairs={{0,8},{1,9},{2,10},{3,11},{4,12},{5,13},{6,14},{7,15},{8,0},{9,1},... | collective-permute-start | bytes 393224 | tf_op jit(solution)/shard_map/ppermute | solution.py:264
  26.4 8.5 %collective-permute-start.9 = (bf16[128,512]{1,0:T(8,128)(2,1)S(1)}, bf16[128,512]{1,0:T(8,128)(2,1)S(1)}, u32[]{:S(2)}, u32[]{:S(2)}) collective-permute-start(bf16[128,512]{1,0:T(8,128)(2,1)S(1)} %get-tuple-element.63.refs_0_), channel_id=1, source_target_pairs={{0,12},{1,13},{2,14},{3,15},{4,8},{5,9},{6,10},{7,11},{8,4},{9,5},... | collective-permute-start | bytes 393224 | tf_op jit(solution)/shard_map/ppermute | solution.py:264
  35.0 6.5 %collective-permute-start.19 = (bf16[4,128,512]{2,1,0:T(8,128)(2,1)S(1)}, bf16[4,128,512]{2,1,0:T(8,128)(2,1)S(1)}, u32[]{:S(2)}, u32[]{:S(2)}) collective-permute-start(bf16[4,128,512]{2,1,0:T(8,128)(2,1)S(1)} %pad_maximum_fusion.3), channel_id=1, source_target_pairs={{0,2},{1,3},{2,0},{3,1},{4,6},{5,7},{6,4},{7,5},{8,10},{9,11},{10,... | collective-permute-start | bytes 1572872 | tf_op jit(solution)/shard_map/ppermute | solution.py:285
  35.1 18.1 %collective-permute-start.14 = (s16[128,2048]{1,0:T(8,128)(2,1)S(1)}, s16[128,2048]{1,0:T(8,128)(2,1)S(1)}, u32[]{:S(2)}, u32[]{:S(2)}) collective-permute-start(s16[128,2048]{1,0:T(8,128)(2,1)S(1)} %get-tuple-element.58), channel_id=1, source_target_pairs={{0,1},{1,0},{2,3},{3,2},{4,5},{5,4},{6,7},{7,6},{8,9},{9,8},{10,11... | collective-permute-start | bytes 1572872 | tf_op jit(solution)/shard_map/ppermute | solution.py:304
  38.0 8.4 %collective-permute-start.11 = (bf16[256,512]{1,0:T(8,128)(2,1)S(1)}, bf16[256,512]{1,0:T(8,128)(2,1)S(1)}, u32[]{:S(2)}, u32[]{:S(2)}) collective-permute-start(bf16[256,512]{1,0:T(8,128)(2,1)S(1)} %pad_maximum_fusion.4), channel_id=1, source_target_pairs={{0,4},{1,5},{2,6},{3,7},{4,0},{5,1},{6,2},{7,3},{8,12},{9,13},{10,... | collective-permute-start | bytes 786440 | tf_op jit(solution)/shard_map/ppermute | solution.py:264
  39.6 9.2 %collective-permute-start.12 = (bf16[256,512]{1,0:T(8,128)(2,1)S(1)}, bf16[256,512]{1,0:T(8,128)(2,1)S(1)}, u32[]{:S(2)}, u32[]{:S(2)}) collective-permute-start(bf16[256,512]{1,0:T(8,128)(2,1)S(1)} %pad_maximum_fusion.4), channel_id=1, source_target_pairs={{0,8},{1,9},{2,10},{3,11},{4,12},{5,13},{6,14},{7,15},{8,0},{9,1},... | collective-permute-start | bytes 786440 | tf_op jit(solution)/shard_map/ppermute | solution.py:264
  39.9 13.3 %collective-permute-start.13 = (bf16[256,512]{1,0:T(8,128)(2,1)S(1)}, bf16[256,512]{1,0:T(8,128)(2,1)S(1)}, u32[]{:S(2)}, u32[]{:S(2)}) collective-permute-start(bf16[256,512]{1,0:T(8,128)(2,1)S(1)} %pad_maximum_fusion.4), channel_id=1, source_target_pairs={{0,12},{1,13},{2,14},{3,15},{4,8},{5,9},{6,10},{7,11},{8,4},{9,5},... | collective-permute-start | bytes 786440 | tf_op jit(solution)/shard_map/ppermute | solution.py:264
  44.6 17.8 %copy-start.1 = (s32[16,2]{0,1:T(2,128)S(1)}, s32[16,2]{0,1:T(2,128)}, u32[]{:S(2)}) copy-start(s32[16,2]{0,1:T(2,128)} %param.6) | copy-start | bytes 388
  44.6 17.8 %collective-permute-start.21 = (s16[128,2048]{1,0:T(8,128)(2,1)S(1)}, s16[128,2048]{1,0:T(8,128)(2,1)S(1)}, u32[]{:S(2)}, u32[]{:S(2)}) collective-permute-start(s16[128,2048]{1,0:T(8,128)(2,1)S(1)} %get-tuple-element.70), channel_id=1, source_target_pairs={{0,1},{1,0},{2,3},{3,2},{4,5},{5,4},{6,7},{7,6},{8,9},{9,8},{10,11... | collective-permute-start | bytes 1572872 | tf_op jit(solution)/shard_map/ppermute | solution.py:309
  53.2 1.5 %collective-permute-start.18 = (bf16[256,512]{1,0:T(8,128)(2,1)S(1)}, bf16[256,512]{1,0:T(8,128)(2,1)S(1)}, u32[]{:S(2)}, u32[]{:S(2)}) collective-permute-start(bf16[256,512]{1,0:T(8,128)(2,1)S(1)} %collective-permute-done.13), channel_id=1, source_target_pairs={{0,2},{1,3},{2,0},{3,1},{4,6},{5,7},{6,4},{7,5},{8,10},{9,11},{10,... | collective-permute-start | bytes 786440 | tf_op jit(solution)/shard_map/ppermute | solution.py:311
  53.2 1.9 %collective-permute-start.17 = (bf16[256,512]{1,0:T(8,128)(2,1)S(1)}, bf16[256,512]{1,0:T(8,128)(2,1)S(1)}, u32[]{:S(2)}, u32[]{:S(2)}) collective-permute-start(bf16[256,512]{1,0:T(8,128)(2,1)S(1)} %collective-permute-done.12), channel_id=1, source_target_pairs={{0,2},{1,3},{2,0},{3,1},{4,6},{5,7},{6,4},{7,5},{8,10},{9,11},{10,... | collective-permute-start | bytes 786440 | tf_op jit(solution)/shard_map/ppermute | solution.py:311
  53.7 1.8 %collective-permute-start.16 = (bf16[256,512]{1,0:T(8,128)(2,1)S(1)}, bf16[256,512]{1,0:T(8,128)(2,1)S(1)}, u32[]{:S(2)}, u32[]{:S(2)}) collective-permute-start(bf16[256,512]{1,0:T(8,128)(2,1)S(1)} %collective-permute-done.11), channel_id=1, source_target_pairs={{0,2},{1,3},{2,0},{3,1},{4,6},{5,7},{6,4},{7,5},{8,10},{9,11},{10,... | collective-permute-start | bytes 786440 | tf_op jit(solution)/shard_map/ppermute | solution.py:311
  53.7 2.1 %collective-permute-start.15 = (bf16[256,512]{1,0:T(8,128)(2,1)S(1)}, bf16[256,512]{1,0:T(8,128)(2,1)S(1)}, u32[]{:S(2)}, u32[]{:S(2)}) collective-permute-start(bf16[256,512]{1,0:T(8,128)(2,1)S(1)} %pad_maximum_fusion.4), channel_id=1, source_target_pairs={{0,2},{1,3},{2,0},{3,1},{4,6},{5,7},{6,4},{7,5},{8,10},{9,11},{10,... | collective-permute-start | bytes 786440 | tf_op jit(solution)/shard_map/ppermute | solution.py:311
  54.7 7.7 %collective-permute-start.20 = (f32[4,2048]{1,0:T(4,128)S(1)}, f32[4,2048]{1,0:T(4,128)S(1)}, u32[]{:S(2)}, u32[]{:S(2)}) collective-permute-start(f32[4,2048]{1,0:T(4,128)S(1)} %get-tuple-element.68), channel_id=1, source_target_pairs={{0,1},{1,0},{2,3},{3,2},{4,5},{5,4},{6,7},{7,6},{8,9},{9,8},{10,11... | collective-permute-start | bytes 98312 | tf_op jit(solution)/shard_map/ppermute | solution.py:309

commit v5 on v4

--- a/solution.py
+++ b/solution.py
@@ -103,11 +103,11 @@
     )(in_hbm(integrals), after)
 
 
-def lay_out(near, other_ref, panel):
-    depth = other_ref.shape[2]
-    own = lax.rem(lax.axis_index("pan"), 2 * other_ref.shape[0])
-    for step in range(2 * other_ref.shape[0]):
-        held = other_ref[step // 2] if step % 2 else near[step // 2][...]
+def lay_out(near, other, panel):
+    depth = near[0].shape[1]
+    own = lax.rem(lax.axis_index("pan"), 2 * len(near))
+    for step in range(2 * len(near)):
+        held = (other if step % 2 else near)[step // 2][...]
         panel[:, pl.ds(pl.multiple_of((own ^ step) * depth, depth), depth)] = held
 
 
@@ -132,20 +132,34 @@
     return jnp.dot(panel[rows, :], ints, preferred_element_type=jnp.float32)
 
 
-def own_kernel(pair_size, int_screen_ref, near_ref, other_ref, ints_ref, *refs):
-    sum_ref, panel = refs[-2:]
+def own_kernel(pair_size, near_count, part, int_screen_ref, *refs):
+    near, other, refs = refs[:near_count], refs[near_count : 2 * near_count], refs[2 * near_count :]
+    ints_ref, (sum_ref, panel) = refs[0], refs[-2:]
     keep = int_keep(int_screen_ref, ints_ref.shape, pair_size)
-    lay_out([near_ref.at[place] for place in range(near_ref.shape[0])], other_ref, panel)
+    depth, width = near[0].shape[1], panel.shape[1]
+    own = lax.rem(lax.axis_index("pan"), ints_ref.shape[0] // depth)
+    half = (own // (2 * near_count)) ^ part
+    for at in range(2 * near_count):
+        held = (other if at % 2 else near)[at // 2][...]
+        column = lax.rem(own ^ at, 2 * near_count) * depth
+        panel[:, pl.ds(pl.multiple_of(column, depth), depth)] = held
+    depth_rows = pl.ds(pl.multiple_of(half * width, width), width)
     for row, column in product_blocks(panel, ints_ref):
-        sums = block_sums(panel, ints_ref, row, column) * keep
-        sum_ref[row : row + sums.shape[0], column : column + COLUMN_TILE] = sums
+        rows, columns = slice(row, row + min(ROW_TILE, panel.shape[0])), slice(column, column + COLUMN_TILE)
+        sums = jnp.dot(panel[rows, :], ints_ref[depth_rows, columns], preferred_element_type=jnp.float32)
+        if part:
+            sums = sums + refs[1][rows, columns]
+        sum_ref[rows, columns] = sums * keep if part else sums
 
 
 def away_kernel(pair_size, near_count, int_screen_ref, *refs):
-    near, (other_ref, ints_ref, before_ref) = refs[:near_count], refs[near_count : near_count + 3]
+    near, refs = refs[:near_count], refs[near_count:]
+    other, refs = (refs[0], refs[1:]) if refs[0].ndim == 3 else (refs[:near_count], refs[near_count:])
+    other = [other.at[place] for place in range(near_count)] if not isinstance(other, (tuple, list)) else other
+    ints_ref, before_ref = refs[:2]
     code_ref, scale_ref, panel = refs[-3:]
     keep = int_keep(int_screen_ref, ints_ref.shape, pair_size)
-    lay_out(near, other_ref, panel)
+    lay_out(near, other, panel)
     first = scale_ref.shape[0] - code_ref.shape[0] // TS
     if first:
         scale_ref[:first, :] = before_ref[...]
@@ -161,7 +175,7 @@
             scale_ref[slot : slot + 1, columns] = top * (1.0 / CODE_MAX)
 
 
-def product(kernel, int_screen, arrays, gates, row_count, ints, out_rows_types, name):
+def product(kernel, int_screen, arrays, gates, row_count, ints, out_rows_types, name, parts=1):
     int_count, ab_count = ints.shape
     return pl.pallas_call(
         kernel,
@@ -170,7 +184,7 @@
         + [WHOLE] * len(arrays)
         + [pl.BlockSpec(memory_space=pl.ANY)] * len(gates),
         out_specs=[WHOLE] * len(out_rows_types),
-        scratch_shapes=[pltpu.VMEM((row_count, int_count), ints.dtype)],
+        scratch_shapes=[pltpu.VMEM((row_count, int_count // parts), ints.dtype)],
         compiler_params=pltpu.CompilerParams(vmem_limit_bytes=PRODUCT_VMEM),
         cost_estimate=LIGHT,
         name=name,
@@ -281,15 +295,24 @@
     amp_screen = amp_screen.T
     picked = pick_live(amplitudes, amp_screen, pair_size)
 
-    def away_product(near, before, gates):
-        other = lax.ppermute(jnp.stack(near), AXES, flip(1))
+    def crossed(near):
+        return [lax.ppermute(block, AXES, flip(1)) for block in near]
+
+    def away_product(near, other, before, gates):
         rows = near[0].shape[0]
         scale_rows = rows // TS + (0 if before is None else before.shape[0])
         before = gates[0] if before is None else before
         return product(
-            functools.partial(away_kernel, pair_size, len(near)), int_screen, [*near, other, ints, before], gates,
+            functools.partial(away_kernel, pair_size, len(near)), int_screen, [*near, *other, ints, before], gates,
             rows, ints, ((rows, jnp.int16), (scale_rows, jnp.float32)), "away_product",
         )
+
+    def own_half(near, before, part):
+        rows = own_block.shape[0]
+        return product(
+            functools.partial(own_kernel, pair_size, len(near), part), int_screen,
+            [*near, *crossed(near), ints, *before], [], rows, ints, ((rows, jnp.float32),), "own_product", 2,
+        )[0]
 
     arrived = [(lax.ppermute(part, AXES, first), lax.ppermute(part, AXES, across)) for part in picked]
     own_block = jnp.concatenate([jnp.where(is_own, part, pair[0]) for part, pair in zip(picked, arrived)], axis=0)
@@ -299,20 +322,19 @@
     near_a = near_blocks(away_a, flip, block_count)
     near_a, staged = lax.optimization_barrier((near_a, staged))
     away_b, near_a = lax.optimization_barrier((away_b, near_a))
+    other_a = [lax.ppermute(jnp.stack(near_a), AXES, flip(1))]
+    code_a, scale_a = away_product(near_a, other_a, None, [staged])
+    came_a = lax.ppermute(code_a, AXES, swap)
     near_b = near_blocks(away_b, flip, block_count)
-    code_a, scale_a = away_product(near_a, None, [staged])
-    came_a = lax.ppermute(code_a, AXES, swap)
     near_b, scale_a = lax.optimization_barrier((near_b, scale_a))
     own_block, near_b = lax.optimization_barrier((own_block, near_b))
     own_near = near_blocks(own_block, flip, block_count)
-    code_b, scales = away_product(near_b, scale_a, [])
+    code_b, scales = away_product(near_b, crossed(near_b), scale_a, [])
     came_b, came_scales = lax.ppermute(code_b, AXES, swap), lax.ppermute(scales, AXES, swap)
-    own_near, came_a = lax.optimization_barrier((own_near, came_a))
-    own_other = jnp.stack([lax.ppermute(block, AXES, flip(1)) for block in own_near])
-    (own_sum,) = product(
-        functools.partial(own_kernel, pair_size), int_screen, [jnp.stack(own_near), own_other, ints], [],
-        own_block.shape[0], ints, ((own_block.shape[0], jnp.float32),), "own_product",
-    )
+    half = len(own_near) // 2
+    near_low, near_high = own_near[:half], own_near[half:]
+    near_low, came_a = lax.optimization_barrier((near_low, came_a))
+    own_sum = own_half(near_high, [own_half(near_low, [], 0)], 1)
     return join(amp_screen, own_sum, came_scales, (came_a, came_b), row_count)
 
 

time: 64.7 us -> 63.1 us (0.975)
  waiting for transfers between devices: 18.5 us -> 10.3 us
  starting transfers between devices: 24.7 us -> 30.7 us
  Pallas kernels: 20.8 us -> 21.6 us
    ppermute x9, waiting for transfers between devices: 13.7 us -> 6.97 us  [near_blocks(): lax.ppermute(block, AXES, flip(bits))]
    ppermute x1, starting transfers between devices: 0.27 us -> 3.04 us  [two_group_shards(): lax.ppermute(scales, AXES, swap)]
    ppermute x1, starting transfers between devices: 0.14 us -> 2.91 us  [two_group_shards(): lax.ppermute(code_b, AXES, swap)]
    ppermute x1, waiting for transfers between devices: 1.06 us -> 0.01 us  [two_group_shards(): lax.ppermute(scales, AXES, swap)]
    ppermute x6 -> x9, waiting for transfers between devices: 1.24 us -> 0.35 us  [the longest x8 0.34 us: crossed(): return [lax.ppermute(block, AXES, flip(1)) for block in near]]
    pallas_call x3 -> x4, Pallas kernels: 11.6 us -> 12.5 us  [product(): pl.pallas_call(kernel, out_shape=[jax.ShapeDtypeStruct((rows, ab_count),...]
    ppermute x6 -> x9, starting transfers between devices: 1.17 us -> 1.62 us  [the longest x8 1.54 us: crossed(): return [lax.ppermute(block, AXES, flip(1)) for block in near]]
  transfers between devices with their start and end apart: 22 -> 25, of which waited for: 12 -> 6; matrix products, arithmetic and copies ran while one was open for 1% -> 0% of each run, Pallas kernels for 27% -> 29%
where the time goes in v5:
time: 63.1 us; the launch traced here: 63 us
  starting transfers between devices  30.7 us (49%)
  Pallas kernels  21.6 us (34%)
  waiting for transfers between devices  10.3 us (16%)
    ppermute x9, starting transfers between devices, near_blocks(): lax.ppermute(block, AXES, flip(bits))  14.6 us
    pallas_call x4, Pallas kernels, product(): pl.pallas_call(kernel, out_shape=[jax.ShapeDtypeStruct((rows, ab_count),...  12.5 us
    ppermute x9, waiting for transfers between devices, near_blocks(): lax.ppermute(block, AXES, flip(bits))  6.97 us
    pallas_call x1, Pallas kernels, stage(): pl.pallas_call(stage_kernel, out_shape=[pltpu.VMEM(integrals.shape, integ...  5.92 us
    ppermute x2, starting transfers between devices, two_group_shards(): lax.ppermute(part, AXES, first)  5.61 us
    ppermute x1, starting transfers between devices, two_group_shards(): lax.ppermute(scales, AXES, swap)  3.04 us
    ppermute x1, starting transfers between devices, two_group_shards(): came_a = lax.ppermute(code_a, AXES, swap)  2.92 us
    ppermute x1, starting transfers between devices, two_group_shards(): lax.ppermute(code_b, AXES, swap)  2.91 us
  transfers between devices with their start and end apart: 25, of which 6 were waited for; matrix products, arithmetic and copies ran while one was open for 0% of the time, Pallas kernels for 29%

profile of v5, /device:TPU:0, one launch (start us, length us, event | category | flops | bytes accessed | tf_op | source)
XLA Modules:
  0.0 63.0 jit_solution(12524101429228638761)
XLA Ops:
  0.0 1.1 %pick_live.1 = (bf16[128,512]{1,0:T(8,128)(2,1)S(1)}, bf16[128,512]{1,0:T(8,128)(2,1)S(1)}) custom-call(s32[2,16]{1,0:T(2,128)} %bitcast.9, bf16[512,512]{1,0:T(8,128)(2,1)} %amps_hbm.1), custom_call_target="tpu_custom_call" | custom-call | tf_op jit(solution)/shard_map/pick_live/pallas_call | solution.py:55
  1.1 4.1 %collective-permute-start = (bf16[128,512]{1,0:T(8,128)(2,1)S(1)}, bf16[128,512]{1,0:T(8,128)(2,1)S(1)}, u32[]{:S(2)}, u32[]{:S(2)}) collective-permute-start(bf16[128,512]{1,0:T(8,128)(2,1)S(1)} %get-tuple-element.36), channel_id=1, source_target_pairs={{0,16},{1,0},{2,18},{3,2},{4,20},{5,4},{6,22},{7,6},{8,24},{9,8},{... | collective-permute-start | bytes 393224 | tf_op jit(solution)/shard_map/ppermute | solution.py:317
  5.2 0.0 collective-permute-start.3
  5.2 1.5 %collective-permute-start.1 = (bf16[128,512]{1,0:T(8,128)(2,1)S(1)}, bf16[128,512]{1,0:T(8,128)(2,1)S(1)}, u32[]{:S(2)}, u32[]{:S(2)}) collective-permute-start(bf16[128,512]{1,0:T(8,128)(2,1)S(1)} %get-tuple-element.37), channel_id=1, source_target_pairs={{0,16},{1,0},{2,18},{3,2},{4,20},{5,4},{6,22},{7,6},{8,24},{9,8},{... | collective-permute-start | bytes 393224 | tf_op jit(solution)/shard_map/ppermute | solution.py:317
  6.7 0.0 collective-permute-start.2
  6.7 2.4 %collective-permute-done = bf16[128,512]{1,0:T(8,128)(2,1)S(1)} collective-permute-done((bf16[128,512]{1,0:T(8,128)(2,1)S(1)}, bf16[128,512]{1,0:T(8,128)(2,1)S(1)}, u32[]{:S(2)}, u32[]{:S(2)}) %collective-permute-start) | collective-permute-done | bytes 131104 | tf_op jit(solution)/shard_map/ppermute | solution.py:317
  9.1 0.0 collective-permute-done.3
  9.2 0.0 copy-start
  9.2 1.6 %collective-permute-start.4 = (bf16[128,512]{1,0:T(8,128)(2,1)S(1)}, bf16[128,512]{1,0:T(8,128)(2,1)S(1)}, u32[]{:S(2)}, u32[]{:S(2)}) collective-permute-start(bf16[128,512]{1,0:T(8,128)(2,1)S(1)} %get-tuple-element.44.after.refs_0_), channel_id=1, source_target_pairs={{0,4},{1,5},{2,6},{3,7},{4,0},{5,1},{6,2},{7,3},{8,12},{9,13},{10,... | collective-permute-start | bytes 393224 | tf_op jit(solution)/shard_map/ppermute | solution.py:278
  10.7 6.0 %collective-permute-start.5 = (bf16[128,512]{1,0:T(8,128)(2,1)S(1)}, bf16[128,512]{1,0:T(8,128)(2,1)S(1)}, u32[]{:S(2)}, u32[]{:S(2)}) collective-permute-start(bf16[128,512]{1,0:T(8,128)(2,1)S(1)} %get-tuple-element.44.after.refs_0_), channel_id=1, source_target_pairs={{0,8},{1,9},{2,10},{3,11},{4,12},{5,13},{6,14},{7,15},{8,0},{9,1},... | collective-permute-start | bytes 393224 | tf_op jit(solution)/shard_map/ppermute | solution.py:278
  16.7 0.0 collective-permute-start.6
  16.7 5.9 %stage_integrals.1 = (bf16[4096,2048]{1,0:T(8,128)(2,1)S(1)}, f32[8,128]{1,0:T(8,128)S(1)}) custom-call(bf16[4096,2048]{1,0:T(8,128)(2,1)} %ints_hbm.1, bf16[128,512]{1,0:T(8,128)(2,1)S(1)} %get-tuple-element.44.after.refs_0_), custom_call_target="tpu_custom_call" | custom-call | flops 1 | bytes 1 | tf_op jit(solution)/shard_map/stage_integrals/pallas_call | solution.py:94
  22.6 0.0 collective-permute-done.1
  22.6 0.0 collective-permute-done.2
  22.7 0.0 collective-permute-done.4.refs_1_
  22.7 0.0 collective-permute-done.5.refs_2_
  22.7 2.2 %collective-permute-done.6.refs_3_ = bf16[128,512]{1,0:T(8,128)(2,1)S(1)} collective-permute-done((bf16[128,512]{1,0:T(8,128)(2,1)S(1)}, bf16[128,512]{1,0:T(8,128)(2,1)S(1)}, u32[]{:S(2)}, u32[]{:S(2)}) %collective-permute-start.6) | collective-permute-done | bytes 131104 | tf_op jit(solution)/shard_map/ppermute | solution.py:278
  24.9 0.1 pad_maximum_fusion
  25.0 0.1 collective-permute-start.10
  25.0 0.6 collective-permute-start.7
  25.6 0.8 %collective-permute-start.8 = (bf16[128,512]{1,0:T(8,128)(2,1)S(1)}, bf16[128,512]{1,0:T(8,128)(2,1)S(1)}, u32[]{:S(2)}, u32[]{:S(2)}) collective-permute-start(bf16[128,512]{1,0:T(8,128)(2,1)S(1)} %get-tuple-element.59.refs_0_), channel_id=1, source_target_pairs={{0,8},{1,9},{2,10},{3,11},{4,12},{5,13},{6,14},{7,15},{8,0},{9,1},... | collective-permute-start | bytes 393224 | tf_op jit(solution)/shard_map/ppermute | solution.py:278
  26.4 2.1 %collective-permute-start.9 = (bf16[128,512]{1,0:T(8,128)(2,1)S(1)}, bf16[128,512]{1,0:T(8,128)(2,1)S(1)}, u32[]{:S(2)}, u32[]{:S(2)}) collective-permute-start(bf16[128,512]{1,0:T(8,128)(2,1)S(1)} %get-tuple-element.59.refs_0_), channel_id=1, source_target_pairs={{0,12},{1,13},{2,14},{3,15},{4,8},{5,9},{6,10},{7,11},{8,4},{9,5},... | collective-permute-start | bytes 393224 | tf_op jit(solution)/shard_map/ppermute | solution.py:278
  28.6 0.0 collective-permute-done.10.refs_4_
  28.6 0.0 copy-done
  28.6 3.1 %away_product.2 = (s16[128,2048]{1,0:T(8,128)(2,1)S(1)}, f32[2,2048]{1,0:T(2,128)S(1)}) custom-call(s32[2,8]{1,0:T(2,128)S(1)} %copy-done, bf16[128,512]{1,0:T(8,128)(2,1)S(1)} %get-tuple-element.44.after.refs_0_, bf16[128,512]{1,0:T(8,128)(2,1)S(1)} %collective-permute-done.4.refs_1_, bf16[128,512]{1,0:T(8,128)(2,1)S(1)} %collective-permute-done.5.refs_2_, ...), custom_call_target="tpu_custom_call" | custom-call | flops 1 | bytes 1 | tf_op jit(solution)/shard_map/away_product/pallas_call | solution.py:180
  31.7 2.9 %collective-permute-start.16 = (s16[128,2048]{1,0:T(8,128)(2,1)S(1)}, s16[128,2048]{1,0:T(8,128)(2,1)S(1)}, u32[]{:S(2)}, u32[]{:S(2)}) collective-permute-start(s16[128,2048]{1,0:T(8,128)(2,1)S(1)} %get-tuple-element.56), channel_id=1, source_target_pairs={{0,1},{1,0},{2,3},{3,2},{4,5},{5,4},{6,7},{7,6},{8,9},{9,8},{10,11... | collective-permute-start | bytes 1572872 | tf_op jit(solution)/shard_map/ppermute | solution.py:327
  34.7 0.0 collective-permute-done.7.refs_1_
  34.7 0.0 collective-permute-done.8.refs_2_
  34.7 0.3 collective-permute-done.9.refs_3_
  34.9 0.0 collective-permute-start.19
  34.9 0.5 collective-permute-start.20
  35.4 0.0 collective-permute-start.21
  35.4 0.5 collective-permute-start.22
  36.0 0.3 collective-permute-done.19.refs_4_
  36.3 1.4 %collective-permute-start.15 = (bf16[256,512]{1,0:T(8,128)(2,1)S(1)}, bf16[256,512]{1,0:T(8,128)(2,1)S(1)}, u32[]{:S(2)}, u32[]{:S(2)}) collective-permute-start(bf16[256,512]{1,0:T(8,128)(2,1)S(1)} %pad_maximum_fusion.1.refs_0_), channel_id=1, source_target_pairs={{0,4},{1,5},{2,6},{3,7},{4,0},{5,1},{6,2},{7,3},{8,12},{9,13},{10,... | collective-permute-start | bytes 786440 | tf_op jit(solution)/shard_map/ppermute | solution.py:278
  37.7 0.0 collective-permute-done.20.refs_5_
  37.7 0.0 collective-permute-start.11
  37.7 0.0 collective-permute-done.21.refs_6_
  37.7 2.1 %collective-permute-start.12 = (bf16[256,512]{1,0:T(8,128)(2,1)S(1)}, bf16[256,512]{1,0:T(8,128)(2,1)S(1)}, u32[]{:S(2)}, u32[]{:S(2)}) collective-permute-start(bf16[256,512]{1,0:T(8,128)(2,1)S(1)} %pad_maximum_fusion.1.refs_0_), channel_id=1, source_target_pairs={{0,12},{1,13},{2,14},{3,15},{4,8},{5,9},{6,10},{7,11},{8,4},{9,5},... | collective-permute-start | bytes 786440 | tf_op jit(solution)/shard_map/ppermute | solution.py:278
  39.8 0.0 collective-permute-done.22.refs_7_
  39.8 3.1 %away_product.3 = (s16[128,2048]{1,0:T(8,128)(2,1)S(1)}, f32[4,2048]{1,0:T(4,128)S(1)}) custom-call(s32[2,8]{1,0:T(2,128)S(1)} %copy-done, bf16[128,512]{1,0:T(8,128)(2,1)S(1)} %get-tuple-element.59.refs_0_, bf16[128,512]{1,0:T(8,128)(2,1)S(1)} %collective-permute-done.7.refs_1_, bf16[128,512]{1,0:T(8,128)(2,1)S(1)} %collective-permute-done.8.refs_2_, ...), custom_call_target="tpu_custom_call" | custom-call | flops 1 | bytes 1 | tf_op jit(solution)/shard_map/away_product/pallas_call | solution.py:180
  42.9 2.9 %collective-permute-start.24 = (s16[128,2048]{1,0:T(8,128)(2,1)S(1)}, s16[128,2048]{1,0:T(8,128)(2,1)S(1)}, u32[]{:S(2)}, u32[]{:S(2)}) collective-permute-start(s16[128,2048]{1,0:T(8,128)(2,1)S(1)} %get-tuple-element.66), channel_id=1, source_target_pairs={{0,1},{1,0},{2,3},{3,2},{4,5},{5,4},{6,7},{7,6},{8,9},{9,8},{10,11... | collective-permute-start | bytes 1572872 | tf_op jit(solution)/shard_map/ppermute | solution.py:333
  45.8 0.0 collective-permute-done.15.refs_1_
  45.8 0.6 collective-permute-done.16.refs_0_
  46.4 0.0 collective-permute-start.17
  46.4 0.5 collective-permute-start.18
  46.9 0.0 collective-permute-done.11.refs_0_
  46.9 0.0 collective-permute-start.13
  46.9 4.5 %collective-permute-done.12.refs_1_ = bf16[256,512]{1,0:T(8,128)(2,1)S(1)} collective-permute-done((bf16[256,512]{1,0:T(8,128)(2,1)S(1)}, bf16[256,512]{1,0:T(8,128)(2,1)S(1)}, u32[]{:S(2)}, u32[]{:S(2)}) %collective-permute-start.12) | collective-permute-done | bytes 262176 | tf_op jit(solution)/shard_map/ppermute | solution.py:278
  51.4 0.0 collective-permute-start.14
  51.5 0.0 collective-permute-done.17.refs_2_
  51.5 3.0 %collective-permute-start.23 = (f32[4,2048]{1,0:T(4,128)S(1)}, f32[4,2048]{1,0:T(4,128)S(1)}, u32[]{:S(2)}, u32[]{:S(2)}) collective-permute-start(f32[4,2048]{1,0:T(4,128)S(1)} %get-tuple-element.64), channel_id=1, source_target_pairs={{0,1},{1,0},{2,3},{3,2},{4,5},{5,4},{6,7},{7,6},{8,9},{9,8},{10,11... | collective-permute-start | bytes 98312 | tf_op jit(solution)/shard_map/ppermute | solution.py:333
  54.5 0.0 collective-permute-done.18.refs_3_
  54.5 3.1 %own_product.2.refs_5_ = f32[256,2048]{1,0:T(8,128)S(1)} custom-call(s32[2,8]{1,0:T(2,128)S(1)} %copy-done, bf16[256,512]{1,0:T(8,128)(2,1)S(1)} %pad_maximum_fusion.1.refs_0_, bf16[256,512]{1,0:T(8,128)(2,1)S(1)} %collective-permute-done.15.refs_1_, bf16[256,512]{1,0:T(8,128)(2,1)S(1)} %collective-permute-done.17.refs_2_, ...), custom_call_target="tpu_custom_call" | custom-call | flops 1 | bytes 1 | tf_op jit(solution)/shard_map/own_product/pallas_call | solution.py:180
  57.6 0.0 copy-start.1
  57.6 0.0 collective-permute-done.13.refs_2_
  57.7 0.0 collective-permute-done.14.refs_3_
  57.7 3.1 %own_product.3.own_ref = f32[256,2048]{1,0:T(8,128)S(1)} custom-call(s32[2,8]{1,0:T(2,128)S(1)} %copy-done, bf16[256,512]{1,0:T(8,128)(2,1)S(1)} %collective-permute-done.11.refs_0_, bf16[256,512]{1,0:T(8,128)(2,1)S(1)} %collective-permute-done.12.refs_1_, bf16[256,512]{1,0:T(8,128)(2,1)S(1)} %collective-permute-done.13.refs_2_, ...), custom_call_target="tpu_custom_call" | custom-call | flops 1 | bytes 1 | tf_op jit(solution)/shard_map/own_product/pallas_call | solution.py:180
  60.8 0.0 collective-permute-done.23.scale_ref
  60.8 0.0 collective-permute-done.24.refs_1_
  60.8 0.0 copy-done.1
  60.8 2.1 %join.1 = bf16[512,2048]{1,0:T(8,128)(2,1)} custom-call(s32[2,16]{1,0:T(2,128)S(1)} %bitcast.10, f32[256,2048]{1,0:T(8,128)S(1)} %own_product.3.own_ref, f32[4,2048]{1,0:T(4,128)S(1)} %collective-permute-done.23.scale_ref, s16[128,2048]{1,0:T(8,128)(2,1)S(1)} %collective-permute-done.16.refs_0_, s16[128,2048]{1,0:T(8,128)(2,1)S(1)} %collective-permute-done.24.refs_1_), custom_call_target="tpu_custom_call" | custom-call | tf_op jit(solution)/shard_map/join/pallas_call | solution.py:238
  (3 shorter events, 0.1 us)
Async XLA Ops:
  1.1 8.0 %collective-permute-start = (bf16[128,512]{1,0:T(8,128)(2,1)S(1)}, bf16[128,512]{1,0:T(8,128)(2,1)S(1)}, u32[]{:S(2)}, u32[]{:S(2)}) collective-permute-start(bf16[128,512]{1,0:T(8,128)(2,1)S(1)} %get-tuple-element.36), channel_id=1, source_target_pairs={{0,16},{1,0},{2,18},{3,2},{4,20},{5,4},{6,22},{7,6},{8,24},{9,8},{... | collective-permute-start | bytes 393224 | tf_op jit(solution)/shard_map/ppermute | solution.py:317
  5.2 3.9 %collective-permute-start.3 = (bf16[128,512]{1,0:T(8,128)(2,1)S(1)}, bf16[128,512]{1,0:T(8,128)(2,1)S(1)}, u32[]{:S(2)}, u32[]{:S(2)}) collective-permute-start(bf16[128,512]{1,0:T(8,128)(2,1)S(1)} %get-tuple-element.36), channel_id=1, source_target_pairs={{0,2},{1,16},{2,0},{3,18},{4,6},{5,20},{6,4},{7,22},{8,10},{9,24},... | collective-permute-start | bytes 393224 | tf_op jit(solution)/shard_map/ppermute | solution.py:317
  5.2 17.5 %collective-permute-start.1 = (bf16[128,512]{1,0:T(8,128)(2,1)S(1)}, bf16[128,512]{1,0:T(8,128)(2,1)S(1)}, u32[]{:S(2)}, u32[]{:S(2)}) collective-permute-start(bf16[128,512]{1,0:T(8,128)(2,1)S(1)} %get-tuple-element.37), channel_id=1, source_target_pairs={{0,16},{1,0},{2,18},{3,2},{4,20},{5,4},{6,22},{7,6},{8,24},{9,8},{... | collective-permute-start | bytes 393224 | tf_op jit(solution)/shard_map/ppermute | solution.py:317
  6.7 16.0 %collective-permute-start.2 = (bf16[128,512]{1,0:T(8,128)(2,1)S(1)}, bf16[128,512]{1,0:T(8,128)(2,1)S(1)}, u32[]{:S(2)}, u32[]{:S(2)}) collective-permute-start(bf16[128,512]{1,0:T(8,128)(2,1)S(1)} %get-tuple-element.37), channel_id=1, source_target_pairs={{0,2},{1,16},{2,0},{3,18},{4,6},{5,20},{6,4},{7,22},{8,10},{9,24},... | collective-permute-start | bytes 393224 | tf_op jit(solution)/shard_map/ppermute | solution.py:317
  9.2 19.4 %copy-start = (s32[2,8]{1,0:T(2,128)S(1)}, s32[2,8]{1,0:T(2,128)}, u32[]{:S(2)}) copy-start(s32[2,8]{1,0:T(2,128)} %int_screen_ref.7) | copy-start | bytes 196
  9.2 13.5 %collective-permute-start.4 = (bf16[128,512]{1,0:T(8,128)(2,1)S(1)}, bf16[128,512]{1,0:T(8,128)(2,1)S(1)}, u32[]{:S(2)}, u32[]{:S(2)}) collective-permute-start(bf16[128,512]{1,0:T(8,128)(2,1)S(1)} %get-tuple-element.44.after.refs_0_), channel_id=1, source_target_pairs={{0,4},{1,5},{2,6},{3,7},{4,0},{5,1},{6,2},{7,3},{8,12},{9,13},{10,... | collective-permute-start | bytes 393224 | tf_op jit(solution)/shard_map/ppermute | solution.py:278
  10.7 12.0 %collective-permute-start.5 = (bf16[128,512]{1,0:T(8,128)(2,1)S(1)}, bf16[128,512]{1,0:T(8,128)(2,1)S(1)}, u32[]{:S(2)}, u32[]{:S(2)}) collective-permute-start(bf16[128,512]{1,0:T(8,128)(2,1)S(1)} %get-tuple-element.44.after.refs_0_), channel_id=1, source_target_pairs={{0,8},{1,9},{2,10},{3,11},{4,12},{5,13},{6,14},{7,15},{8,0},{9,1},... | collective-permute-start | bytes 393224 | tf_op jit(solution)/shard_map/ppermute | solution.py:278
  16.7 8.2 %collective-permute-start.6 = (bf16[128,512]{1,0:T(8,128)(2,1)S(1)}, bf16[128,512]{1,0:T(8,128)(2,1)S(1)}, u32[]{:S(2)}, u32[]{:S(2)}) collective-permute-start(bf16[128,512]{1,0:T(8,128)(2,1)S(1)} %get-tuple-element.44.after.refs_0_), channel_id=1, source_target_pairs={{0,12},{1,13},{2,14},{3,15},{4,8},{5,9},{6,10},{7,11},{8,4},{9,5},... | collective-permute-start | bytes 393224 | tf_op jit(solution)/shard_map/ppermute | solution.py:278
  25.0 3.6 %collective-permute-start.10 = (bf16[4,128,512]{2,1,0:T(8,128)(2,1)S(1)}, bf16[4,128,512]{2,1,0:T(8,128)(2,1)S(1)}, u32[]{:S(2)}, u32[]{:S(2)}) collective-permute-start(bf16[4,128,512]{2,1,0:T(8,128)(2,1)S(1)} %pad_maximum_fusion), channel_id=1, source_target_pairs={{0,2},{1,3},{2,0},{3,1},{4,6},{5,7},{6,4},{7,5},{8,10},{9,11},{10,... | collective-permute-start | bytes 1572872 | tf_op jit(solution)/shard_map/ppermute | solution.py:325
  25.0 9.6 %collective-permute-start.7 = (bf16[128,512]{1,0:T(8,128)(2,1)S(1)}, bf16[128,512]{1,0:T(8,128)(2,1)S(1)}, u32[]{:S(2)}, u32[]{:S(2)}) collective-permute-start(bf16[128,512]{1,0:T(8,128)(2,1)S(1)} %get-tuple-element.59.refs_0_), channel_id=1, source_target_pairs={{0,4},{1,5},{2,6},{3,7},{4,0},{5,1},{6,2},{7,3},{8,12},{9,13},{10,... | collective-permute-start | bytes 393224 | tf_op jit(solution)/shard_map/ppermute | solution.py:278
  25.6 9.0 %collective-permute-start.8 = (bf16[128,512]{1,0:T(8,128)(2,1)S(1)}, bf16[128,512]{1,0:T(8,128)(2,1)S(1)}, u32[]{:S(2)}, u32[]{:S(2)}) collective-permute-start(bf16[128,512]{1,0:T(8,128)(2,1)S(1)} %get-tuple-element.59.refs_0_), channel_id=1, source_target_pairs={{0,8},{1,9},{2,10},{3,11},{4,12},{5,13},{6,14},{7,15},{8,0},{9,1},... | collective-permute-start | bytes 393224 | tf_op jit(solution)/shard_map/ppermute | solution.py:278
  26.4 8.5 %collective-permute-start.9 = (bf16[128,512]{1,0:T(8,128)(2,1)S(1)}, bf16[128,512]{1,0:T(8,128)(2,1)S(1)}, u32[]{:S(2)}, u32[]{:S(2)}) collective-permute-start(bf16[128,512]{1,0:T(8,128)(2,1)S(1)} %get-tuple-element.59.refs_0_), channel_id=1, source_target_pairs={{0,12},{1,13},{2,14},{3,15},{4,8},{5,9},{6,10},{7,11},{8,4},{9,5},... | collective-permute-start | bytes 393224 | tf_op jit(solution)/shard_map/ppermute | solution.py:278
  31.7 14.7 %collective-permute-start.16 = (s16[128,2048]{1,0:T(8,128)(2,1)S(1)}, s16[128,2048]{1,0:T(8,128)(2,1)S(1)}, u32[]{:S(2)}, u32[]{:S(2)}) collective-permute-start(s16[128,2048]{1,0:T(8,128)(2,1)S(1)} %get-tuple-element.56), channel_id=1, source_target_pairs={{0,1},{1,0},{2,3},{3,2},{4,5},{5,4},{6,7},{7,6},{8,9},{9,8},{10,11... | collective-permute-start | bytes 1572872 | tf_op jit(solution)/shard_map/ppermute | solution.py:327
  34.9 1.3 %collective-permute-start.19 = (bf16[128,512]{1,0:T(8,128)(2,1)S(1)}, bf16[128,512]{1,0:T(8,128)(2,1)S(1)}, u32[]{:S(2)}, u32[]{:S(2)}) collective-permute-start(bf16[128,512]{1,0:T(8,128)(2,1)S(1)} %get-tuple-element.59.refs_0_), channel_id=1, source_target_pairs={{0,2},{1,3},{2,0},{3,1},{4,6},{5,7},{6,4},{7,5},{8,10},{9,11},{10,... | collective-permute-start | bytes 393224 | tf_op jit(solution)/shard_map/ppermute | solution.py:299
  34.9 2.7 %collective-permute-start.20 = (bf16[128,512]{1,0:T(8,128)(2,1)S(1)}, bf16[128,512]{1,0:T(8,128)(2,1)S(1)}, u32[]{:S(2)}, u32[]{:S(2)}) collective-permute-start(bf16[128,512]{1,0:T(8,128)(2,1)S(1)} %collective-permute-done.7.refs_1_), channel_id=1, source_target_pairs={{0,2},{1,3},{2,0},{3,1},{4,6},{5,7},{6,4},{7,5},{8,10},{9,11},{10,... | collective-permute-start | bytes 393224 | tf_op jit(solution)/shard_map/ppermute | solution.py:299
  35.4 2.2 %collective-permute-start.21 = (bf16[128,512]{1,0:T(8,128)(2,1)S(1)}, bf16[128,512]{1,0:T(8,128)(2,1)S(1)}, u32[]{:S(2)}, u32[]{:S(2)}) collective-permute-start(bf16[128,512]{1,0:T(8,128)(2,1)S(1)} %collective-permute-done.8.refs_2_), channel_id=1, source_target_pairs={{0,2},{1,3},{2,0},{3,1},{4,6},{5,7},{6,4},{7,5},{8,10},{9,11},{10,... | collective-permute-start | bytes 393224 | tf_op jit(solution)/shard_map/ppermute | solution.py:299
  35.4 4.3 %collective-permute-start.22 = (bf16[128,512]{1,0:T(8,128)(2,1)S(1)}, bf16[128,512]{1,0:T(8,128)(2,1)S(1)}, u32[]{:S(2)}, u32[]{:S(2)}) collective-permute-start(bf16[128,512]{1,0:T(8,128)(2,1)S(1)} %collective-permute-done.9.refs_3_), channel_id=1, source_target_pairs={{0,2},{1,3},{2,0},{3,1},{4,6},{5,7},{6,4},{7,5},{8,10},{9,11},{10,... | collective-permute-start | bytes 393224 | tf_op jit(solution)/shard_map/ppermute | solution.py:299
  36.3 9.5 %collective-permute-start.15 = (bf16[256,512]{1,0:T(8,128)(2,1)S(1)}, bf16[256,512]{1,0:T(8,128)(2,1)S(1)}, u32[]{:S(2)}, u32[]{:S(2)}) collective-permute-start(bf16[256,512]{1,0:T(8,128)(2,1)S(1)} %pad_maximum_fusion.1.refs_0_), channel_id=1, source_target_pairs={{0,4},{1,5},{2,6},{3,7},{4,0},{5,1},{6,2},{7,3},{8,12},{9,13},{10,... | collective-permute-start | bytes 786440 | tf_op jit(solution)/shard_map/ppermute | solution.py:278
  37.7 9.2 %collective-permute-start.11 = (bf16[256,512]{1,0:T(8,128)(2,1)S(1)}, bf16[256,512]{1,0:T(8,128)(2,1)S(1)}, u32[]{:S(2)}, u32[]{:S(2)}) collective-permute-start(bf16[256,512]{1,0:T(8,128)(2,1)S(1)} %pad_maximum_fusion.1.refs_0_), channel_id=1, source_target_pairs={{0,8},{1,9},{2,10},{3,11},{4,12},{5,13},{6,14},{7,15},{8,0},{9,1},... | collective-permute-start | bytes 786440 | tf_op jit(solution)/shard_map/ppermute | solution.py:278
  37.7 13.8 %collective-permute-start.12 = (bf16[256,512]{1,0:T(8,128)(2,1)S(1)}, bf16[256,512]{1,0:T(8,128)(2,1)S(1)}, u32[]{:S(2)}, u32[]{:S(2)}) collective-permute-start(bf16[256,512]{1,0:T(8,128)(2,1)S(1)} %pad_maximum_fusion.1.refs_0_), channel_id=1, source_target_pairs={{0,12},{1,13},{2,14},{3,15},{4,8},{5,9},{6,10},{7,11},{8,4},{9,5},... | collective-permute-start | bytes 786440 | tf_op jit(solution)/shard_map/ppermute | solution.py:278
  42.9 17.9 %collective-permute-start.24 = (s16[128,2048]{1,0:T(8,128)(2,1)S(1)}, s16[128,2048]{1,0:T(8,128)(2,1)S(1)}, u32[]{:S(2)}, u32[]{:S(2)}) collective-permute-start(s16[128,2048]{1,0:T(8,128)(2,1)S(1)} %get-tuple-element.66), channel_id=1, source_target_pairs={{0,1},{1,0},{2,3},{3,2},{4,5},{5,4},{6,7},{7,6},{8,9},{9,8},{10,11... | collective-permute-start | bytes 1572872 | tf_op jit(solution)/shard_map/ppermute | solution.py:333
  46.4 5.1 %collective-permute-start.17 = (bf16[256,512]{1,0:T(8,128)(2,1)S(1)}, bf16[256,512]{1,0:T(8,128)(2,1)S(1)}, u32[]{:S(2)}, u32[]{:S(2)}) collective-permute-start(bf16[256,512]{1,0:T(8,128)(2,1)S(1)} %pad_maximum_fusion.1.refs_0_), channel_id=1, source_target_pairs={{0,2},{1,3},{2,0},{3,1},{4,6},{5,7},{6,4},{7,5},{8,10},{9,11},{10,... | collective-permute-start | bytes 786440 | tf_op jit(solution)/shard_map/ppermute | solution.py:299
  46.4 8.1 %collective-permute-start.18 = (bf16[256,512]{1,0:T(8,128)(2,1)S(1)}, bf16[256,512]{1,0:T(8,128)(2,1)S(1)}, u32[]{:S(2)}, u32[]{:S(2)}) collective-permute-start(bf16[256,512]{1,0:T(8,128)(2,1)S(1)} %collective-permute-done.15.refs_1_), channel_id=1, source_target_pairs={{0,2},{1,3},{2,0},{3,1},{4,6},{5,7},{6,4},{7,5},{8,10},{9,11},{10,... | collective-permute-start | bytes 786440 | tf_op jit(solution)/shard_map/ppermute | solution.py:299
  46.9 10.7 %collective-permute-start.13 = (bf16[256,512]{1,0:T(8,128)(2,1)S(1)}, bf16[256,512]{1,0:T(8,128)(2,1)S(1)}, u32[]{:S(2)}, u32[]{:S(2)}) collective-permute-start(bf16[256,512]{1,0:T(8,128)(2,1)S(1)} %collective-permute-done.11.refs_0_), channel_id=1, source_target_pairs={{0,2},{1,3},{2,0},{3,1},{4,6},{5,7},{6,4},{7,5},{8,10},{9,11},{10,... | collective-permute-start | bytes 786440 | tf_op jit(solution)/shard_map/ppermute | solution.py:299
  51.4 6.2 %collective-permute-start.14 = (bf16[256,512]{1,0:T(8,128)(2,1)S(1)}, bf16[256,512]{1,0:T(8,128)(2,1)S(1)}, u32[]{:S(2)}, u32[]{:S(2)}) collective-permute-start(bf16[256,512]{1,0:T(8,128)(2,1)S(1)} %collective-permute-done.12.refs_1_), channel_id=1, source_target_pairs={{0,2},{1,3},{2,0},{3,1},{4,6},{5,7},{6,4},{7,5},{8,10},{9,11},{10,... | collective-permute-start | bytes 786440 | tf_op jit(solution)/shard_map/ppermute | solution.py:299
  51.5 9.4 %collective-permute-start.23 = (f32[4,2048]{1,0:T(4,128)S(1)}, f32[4,2048]{1,0:T(4,128)S(1)}, u32[]{:S(2)}, u32[]{:S(2)}) collective-permute-start(f32[4,2048]{1,0:T(4,128)S(1)} %get-tuple-element.64), channel_id=1, source_target_pairs={{0,1},{1,0},{2,3},{3,2},{4,5},{5,4},{6,7},{7,6},{8,9},{9,8},{10,11... | collective-permute-start | bytes 98312 | tf_op jit(solution)/shard_map/ppermute | solution.py:333
  57.6 3.2 %copy-start.1 = (s32[16,2]{0,1:T(2,128)S(1)}, s32[16,2]{0,1:T(2,128)}, u32[]{:S(2)}) copy-start(s32[16,2]{0,1:T(2,128)} %param.6) | copy-start | bytes 388

commit v6 on v5

--- a/solution.py
+++ b/solution.py
@@ -13,6 +13,8 @@
 AXES = ("pan", "grp")
 SLOT_CHUNKS = ((0, 2), (2, 4))
 CODE_MAX = 32767.0
+DIGITS = 8192.0
+SCALE_ROWS = 8
 STAGE_COPIES = 8
 LEAST_SCALE = 1e-33
 ROW_TILE = 128
@@ -21,6 +23,7 @@
 SMALL_VMEM = 8 * 1024 * 1024
 PRODUCT_VMEM = 16 * 1024 * 1024
 LIGHT = pl.CostEstimate(flops=1, bytes_accessed=1, transcendentals=0)
+MEDIUM = pl.CostEstimate(flops=1 << 30, bytes_accessed=1, transcendentals=0)
 WHOLE = pl.BlockSpec(memory_space=pltpu.VMEM)
 
 
@@ -152,7 +155,11 @@
         sum_ref[rows, columns] = sums * keep if part else sums
 
 
-def away_kernel(pair_size, near_count, int_screen_ref, *refs):
+def scale_of(digits, exponent):
+    return digits * jnp.exp2(exponent) * (1.0 / (DIGITS * CODE_MAX))
+
+
+def away_kernel(pair_size, near_count, first, int_screen_ref, *refs):
     near, refs = refs[:near_count], refs[near_count:]
     other, refs = (refs[0], refs[1:]) if refs[0].ndim == 3 else (refs[:near_count], refs[near_count:])
     other = [other.at[place] for place in range(near_count)] if not isinstance(other, (tuple, list)) else other
@@ -160,9 +167,7 @@
     code_ref, scale_ref, panel = refs[-3:]
     keep = int_keep(int_screen_ref, ints_ref.shape, pair_size)
     lay_out(near, other, panel)
-    first = scale_ref.shape[0] - code_ref.shape[0] // TS
-    if first:
-        scale_ref[:first, :] = before_ref[...]
+    scale_ref[...] = before_ref[...] if first else jnp.zeros_like(scale_ref)
     for row, column in product_blocks(panel, ints_ref):
         sums = block_sums(panel, ints_ref, row, column) * keep
         columns = slice(column, column + COLUMN_TILE)
@@ -170,28 +175,32 @@
             slot, rows = first + (row + at) // TS, slice(row + at, row + at + TS)
             part = sums[at : at + TS]
             top = jnp.maximum(jnp.max(jnp.abs(part), axis=0, keepdims=True), LEAST_SCALE)
-            code = jnp.round(part * (CODE_MAX / top))
+            exponent = jnp.floor(jnp.log2(top))
+            digits = jnp.ceil(top / jnp.exp2(exponent) * DIGITS)
+            code = jnp.round(part * (1.0 / scale_of(digits, exponent)))
             code_ref[rows, columns] = code.astype(jnp.int32).astype(jnp.int16)
-            scale_ref[slot : slot + 1, columns] = top * (1.0 / CODE_MAX)
-
-
-def product(kernel, int_screen, arrays, gates, row_count, ints, out_rows_types, name, parts=1):
+            scale_ref[slot : slot + 1, columns] = digits
+            scale_ref[SCALE_ROWS + slot : SCALE_ROWS + slot + 1, columns] = exponent
+    if first:
+        code_ref[panel.shape[0] :, :] = scale_ref[...].astype(jnp.int32).astype(jnp.int16)
+
+
+def product(kernel, int_screen, arrays, row_count, ints, out_rows_types, cost, name, parts=1):
     int_count, ab_count = ints.shape
     return pl.pallas_call(
         kernel,
         out_shape=[jax.ShapeDtypeStruct((rows, ab_count), dtype) for rows, dtype in out_rows_types],
         in_specs=[pl.BlockSpec(memory_space=pltpu.SMEM)]
-        + [WHOLE] * len(arrays)
-        + [pl.BlockSpec(memory_space=pl.ANY)] * len(gates),
+        + [WHOLE] * len(arrays),
         out_specs=[WHOLE] * len(out_rows_types),
         scratch_shapes=[pltpu.VMEM((row_count, int_count // parts), ints.dtype)],
         compiler_params=pltpu.CompilerParams(vmem_limit_bytes=PRODUCT_VMEM),
-        cost_estimate=LIGHT,
+        cost_estimate=cost,
         name=name,
-    )(int_screen, *arrays, *gates)
-
-
-def join_kernel(screen_ref, own_ref, scale_ref, *refs):
+    )(int_screen, *arrays)
+
+
+def join_kernel(screen_ref, own_ref, *refs):
     code_refs, (out_hbm, held, sem) = refs[: len(SLOT_CHUNKS)], refs[len(SLOT_CHUNKS) :]
     grp_index = lax.axis_index("grp")
     first_tile = grp_index * BLOCK_TILES
@@ -206,6 +215,9 @@
         columns = slice(part * JOIN_TILE, (part + 1) * JOIN_TILE)
         held_part = held.at[part]
         held_part[...] = jnp.zeros_like(held_part)
+        last_ref = code_refs[-1]
+        coded = last_ref[last_ref.shape[0] - 2 * SCALE_ROWS :, columns].astype(jnp.float32)
+        scales = scale_of(coded[:SCALE_ROWS], coded[SCALE_ROWS:])
         for slot in range(LIVE_MAX):
 
             @pl.when(slot < own_count)
@@ -218,7 +230,7 @@
                 @pl.when(slot < count)
                 def _():
                     code = code_ref[(slot - first) * TS : (slot - first + 1) * TS, columns].astype(jnp.float32)
-                    away = code * scale_ref[slot : slot + 1, columns]
+                    away = code * scales[slot : slot + 1]
                     at = jnp.int32(-1)
                     for own_slot in range(LIVE_MAX):
                         at = jnp.where((own_slot < own_count) & (own_slots[own_slot] == slots[slot]), own_slot, at)
@@ -232,9 +244,9 @@
         copy.wait()
 
 
-def join(amp_screen, own_sum, scales, codes, row_count):
+def join(amp_screen, own_sum, codes, row_count):
     ab_count = own_sum.shape[1]
-    arrays = [own_sum, scales, *codes]
+    arrays = [own_sum, *codes]
     return pl.pallas_call(
         join_kernel,
         out_shape=jax.ShapeDtypeStruct((row_count, ab_count), jnp.bfloat16),
@@ -298,20 +310,19 @@
     def crossed(near):
         return [lax.ppermute(block, AXES, flip(1)) for block in near]
 
-    def away_product(near, other, before, gates):
+    def away_product(near, other, before, first):
         rows = near[0].shape[0]
-        scale_rows = rows // TS + (0 if before is None else before.shape[0])
-        before = gates[0] if before is None else before
+        code_rows = rows + (2 * SCALE_ROWS if first else 0)
         return product(
-            functools.partial(away_kernel, pair_size, len(near)), int_screen, [*near, *other, ints, before], gates,
-            rows, ints, ((rows, jnp.int16), (scale_rows, jnp.float32)), "away_product",
+            functools.partial(away_kernel, pair_size, len(near), first), int_screen, [*near, *other, ints, before],
+            rows, ints, ((code_rows, jnp.int16), (2 * SCALE_ROWS, jnp.float32)), LIGHT, "away_product",
         )
 
     def own_half(near, before, part):
         rows = own_block.shape[0]
         return product(
             functools.partial(own_kernel, pair_size, len(near), part), int_screen,
-            [*near, *crossed(near), ints, *before], [], rows, ints, ((rows, jnp.float32),), "own_product", 2,
+            [*near, *crossed(near), ints, *before], rows, ints, ((rows, jnp.float32),), MEDIUM, "own_product", 2,
         )[0]
 
     arrived = [(lax.ppermute(part, AXES, first), lax.ppermute(part, AXES, across)) for part in picked]
@@ -323,19 +334,20 @@
     near_a, staged = lax.optimization_barrier((near_a, staged))
     away_b, near_a = lax.optimization_barrier((away_b, near_a))
     other_a = [lax.ppermute(jnp.stack(near_a), AXES, flip(1))]
-    code_a, scale_a = away_product(near_a, other_a, None, [staged])
+    code_a, scale_a = away_product(near_a, other_a, staged, 0)
     came_a = lax.ppermute(code_a, AXES, swap)
     near_b = near_blocks(away_b, flip, block_count)
     near_b, scale_a = lax.optimization_barrier((near_b, scale_a))
     own_block, near_b = lax.optimization_barrier((own_block, near_b))
     own_near = near_blocks(own_block, flip, block_count)
-    code_b, scales = away_product(near_b, crossed(near_b), scale_a, [])
-    came_b, came_scales = lax.ppermute(code_b, AXES, swap), lax.ppermute(scales, AXES, swap)
+    code_b, _ = away_product(near_b, crossed(near_b), scale_a, SLOT_CHUNKS[1][0])
+    came_b = lax.ppermute(code_b, AXES, swap)
     half = len(own_near) // 2
     near_low, near_high = own_near[:half], own_near[half:]
-    near_low, came_a = lax.optimization_barrier((near_low, came_a))
-    own_sum = own_half(near_high, [own_half(near_low, [], 0)], 1)
-    return join(amp_screen, own_sum, came_scales, (came_a, came_b), row_count)
+    own_sum = own_half(near_low, [], 0)
+    near_high, came_a = lax.optimization_barrier((near_high, came_a))
+    own_sum = own_half(near_high, [own_sum], 1)
+    return join(amp_screen, own_sum, (came_a, came_b), row_count)
 
 
 def column_pairs(piece_width, pair_size, pair_count):

time: 63.1 us -> 62.8 us (level)
  waiting for transfers between devices: 10.3 us -> 8.26 us
  starting transfers between devices: 30.7 us -> 31.7 us
  Pallas kernels: 21.6 us -> 22.5 us
    ppermute x2 -> x1, starting transfers between devices: 5.95 us -> 2.68 us  [two_group_shards(): came_b = lax.ppermute(code_b, AXES, swap)]
    ppermute x2, starting transfers between devices: 5.61 us -> 7.41 us  [two_group_shards(): lax.ppermute(part, AXES, first)]
    ppermute x2 -> x1, waiting for transfers between devices: 0.01 us -> 1.4 us  [two_group_shards(): came_b = lax.ppermute(code_b, AXES, swap)]
    ppermute x1, starting transfers between devices: 2.92 us -> 4.3 us  [two_group_shards(): came_a = lax.ppermute(code_a, AXES, swap)]
    ppermute x2, waiting for transfers between devices: 2.42 us -> 1.07 us  [two_group_shards(): lax.ppermute(part, AXES, first)]
    ppermute x9, waiting for transfers between devices: 6.97 us -> 5.76 us  [near_blocks(): lax.ppermute(block, AXES, flip(bits))]
    pallas_call x4, Pallas kernels: 12.5 us -> 13.3 us  [product(): pl.pallas_call(kernel, out_shape=[jax.ShapeDtypeStruct((rows, ab_count),...]
  transfers between devices with their start and end apart: 25 -> 24, of which waited for: 6 -> 5; matrix products, arithmetic and copies ran while one was open for 0% -> 0% of each run, Pallas kernels for 29% -> 31%
where the time goes in v6:
time: 62.8 us
  starting transfers between devices  31.7 us (50%)
  Pallas kernels  22.5 us (36%)
  waiting for transfers between devices  8.26 us (13%)
    ppermute x9, starting transfers between devices, near_blocks(): lax.ppermute(block, AXES, flip(bits))  15 us
    pallas_call x4, Pallas kernels, product(): pl.pallas_call(kernel, out_shape=[jax.ShapeDtypeStruct((rows, ab_count),...  13.3 us
    ppermute x2, starting transfers between devices, two_group_shards(): lax.ppermute(part, AXES, first)  7.41 us
    pallas_call x1, Pallas kernels, stage(): pl.pallas_call(stage_kernel, out_shape=[pltpu.VMEM(integrals.shape, integ...  5.92 us
    ppermute x9, waiting for transfers between devices, near_blocks(): lax.ppermute(block, AXES, flip(bits))  5.76 us
    ppermute x1, starting transfers between devices, two_group_shards(): came_a = lax.ppermute(code_a, AXES, swap)  4.3 us
    ppermute x1, starting transfers between devices, two_group_shards(): came_b = lax.ppermute(code_b, AXES, swap)  2.68 us
    pallas_call x1, Pallas kernels, join(): pl.pallas_call(join_kernel, out_shape=jax.ShapeDtypeStruct((row_count, ab...  2.21 us
  transfers between devices with their start and end apart: 24, of which 5 were waited for; matrix products, arithmetic and copies ran while one was open for 0% of the time, Pallas kernels for 31%

profile of v6, /device:TPU:0, one launch (start us, length us, event | category | flops | bytes accessed | tf_op | source)
XLA Modules:
  0.0 62.8 jit_solution(13386743482026772991)
XLA Ops:
  0.0 1.1 %pick_live.1 = (bf16[128,512]{1,0:T(8,128)(2,1)S(1)}, bf16[128,512]{1,0:T(8,128)(2,1)S(1)}) custom-call(s32[2,16]{1,0:T(2,128)} %bitcast.9, bf16[512,512]{1,0:T(8,128)(2,1)} %amps_hbm.1), custom_call_target="tpu_custom_call" | custom-call | tf_op jit(solution)/shard_map/pick_live/pallas_call | solution.py:58
  1.1 0.5 collective-permute-start.3
  1.6 4.9 %collective-permute-start = (bf16[128,512]{1,0:T(8,128)(2,1)S(1)}, bf16[128,512]{1,0:T(8,128)(2,1)S(1)}, u32[]{:S(2)}, u32[]{:S(2)}) collective-permute-start(bf16[128,512]{1,0:T(8,128)(2,1)S(1)} %get-tuple-element.35), channel_id=1, source_target_pairs={{0,16},{1,0},{2,18},{3,2},{4,20},{5,4},{6,22},{7,6},{8,24},{9,8},{... | collective-permute-start | bytes 393224 | tf_op jit(solution)/shard_map/ppermute | solution.py:328
  6.5 0.0 collective-permute-start.2
  6.5 2.5 %collective-permute-start.1 = (bf16[128,512]{1,0:T(8,128)(2,1)S(1)}, bf16[128,512]{1,0:T(8,128)(2,1)S(1)}, u32[]{:S(2)}, u32[]{:S(2)}) collective-permute-start(bf16[128,512]{1,0:T(8,128)(2,1)S(1)} %get-tuple-element.36), channel_id=1, source_target_pairs={{0,16},{1,0},{2,18},{3,2},{4,20},{5,4},{6,22},{7,6},{8,24},{9,8},{... | collective-permute-start | bytes 393224 | tf_op jit(solution)/shard_map/ppermute | solution.py:328
  9.0 0.0 collective-permute-done.3
  9.0 1.1 %collective-permute-done = bf16[128,512]{1,0:T(8,128)(2,1)S(1)} collective-permute-done((bf16[128,512]{1,0:T(8,128)(2,1)S(1)}, bf16[128,512]{1,0:T(8,128)(2,1)S(1)}, u32[]{:S(2)}, u32[]{:S(2)}) %collective-permute-start) | collective-permute-done | bytes 131104 | tf_op jit(solution)/shard_map/ppermute | solution.py:328
  10.1 0.0 copy-start
  10.1 7.0 %collective-permute-start.6 = (bf16[128,512]{1,0:T(8,128)(2,1)S(1)}, bf16[128,512]{1,0:T(8,128)(2,1)S(1)}, u32[]{:S(2)}, u32[]{:S(2)}) collective-permute-start(bf16[128,512]{1,0:T(8,128)(2,1)S(1)} %get-tuple-element.43.after.refs_0_), channel_id=1, source_target_pairs={{0,12},{1,13},{2,14},{3,15},{4,8},{5,9},{6,10},{7,11},{8,4},{9,5},... | collective-permute-start | bytes 393224 | tf_op jit(solution)/shard_map/ppermute | solution.py:290
  17.2 0.0 collective-permute-start.5
  17.2 0.6 %collective-permute-start.4 = (bf16[128,512]{1,0:T(8,128)(2,1)S(1)}, bf16[128,512]{1,0:T(8,128)(2,1)S(1)}, u32[]{:S(2)}, u32[]{:S(2)}) collective-permute-start(bf16[128,512]{1,0:T(8,128)(2,1)S(1)} %get-tuple-element.43.after.refs_0_), channel_id=1, source_target_pairs={{0,4},{1,5},{2,6},{3,7},{4,0},{5,1},{6,2},{7,3},{8,12},{9,13},{10,... | collective-permute-start | bytes 393224 | tf_op jit(solution)/shard_map/ppermute | solution.py:290
  17.8 5.9 %stage_integrals.1 = (bf16[4096,2048]{1,0:T(8,128)(2,1)S(1)}, f32[8,128]{1,0:T(8,128)S(1)}) custom-call(bf16[4096,2048]{1,0:T(8,128)(2,1)} %ints_hbm.1, bf16[128,512]{1,0:T(8,128)(2,1)S(1)} %get-tuple-element.43.after.refs_0_), custom_call_target="tpu_custom_call" | custom-call | flops 1 | bytes 1 | tf_op jit(solution)/shard_map/stage_integrals/pallas_call | solution.py:97
  23.7 0.0 collective-permute-done.2
  23.7 0.0 collective-permute-done.1
  23.8 0.0 collective-permute-done.6.refs_3_
  23.8 0.0 collective-permute-done.5.refs_2_
  23.8 0.8 %collective-permute-done.4.refs_1_ = bf16[128,512]{1,0:T(8,128)(2,1)S(1)} collective-permute-done((bf16[128,512]{1,0:T(8,128)(2,1)S(1)}, bf16[128,512]{1,0:T(8,128)(2,1)S(1)}, u32[]{:S(2)}, u32[]{:S(2)}) %collective-permute-start.4) | collective-permute-done | bytes 131104 | tf_op jit(solution)/shard_map/ppermute | solution.py:290
  24.7 0.1 pad_maximum_fusion
  24.7 0.1 collective-permute-start.10
  24.8 2.1 %collective-permute-start.9 = (bf16[128,512]{1,0:T(8,128)(2,1)S(1)}, bf16[128,512]{1,0:T(8,128)(2,1)S(1)}, u32[]{:S(2)}, u32[]{:S(2)}) collective-permute-start(bf16[128,512]{1,0:T(8,128)(2,1)S(1)} %get-tuple-element.59.refs_0_), channel_id=1, source_target_pairs={{0,12},{1,13},{2,14},{3,15},{4,8},{5,9},{6,10},{7,11},{8,4},{9,5},... | collective-permute-start | bytes 393224 | tf_op jit(solution)/shard_map/ppermute | solution.py:290
  26.9 0.1 collective-permute-start.8
  27.0 1.4 %collective-permute-start.7 = (bf16[128,512]{1,0:T(8,128)(2,1)S(1)}, bf16[128,512]{1,0:T(8,128)(2,1)S(1)}, u32[]{:S(2)}, u32[]{:S(2)}) collective-permute-start(bf16[128,512]{1,0:T(8,128)(2,1)S(1)} %get-tuple-element.59.refs_0_), channel_id=1, source_target_pairs={{0,4},{1,5},{2,6},{3,7},{4,0},{5,1},{6,2},{7,3},{8,12},{9,13},{10,... | collective-permute-start | bytes 393224 | tf_op jit(solution)/shard_map/ppermute | solution.py:290
  28.4 0.0 collective-permute-done.10.refs_4_
  28.4 0.0 copy-done
  28.4 3.2 %away_product.2 = (s16[128,2048]{1,0:T(8,128)(2,1)S(1)}, f32[16,2048]{1,0:T(8,128)S(1)}) custom-call(s32[2,8]{1,0:T(2,128)S(1)} %copy-done, bf16[128,512]{1,0:T(8,128)(2,1)S(1)} %get-tuple-element.43.after.refs_0_, bf16[128,512]{1,0:T(8,128)(2,1)S(1)} %collective-permute-done.4.refs_1_, bf16[128,512]{1,0:T(8,128)(2,1)S(1)} %collective-permute-done.5.refs_2_, ...), custom_call_target="tpu_custom_call" | custom-call | flops 1 | bytes 1 | tf_op jit(solution)/shard_map/away_product/pallas_call | solution.py:190
  31.6 4.3 %collective-permute-start.13 = (s16[128,2048]{1,0:T(8,128)(2,1)S(1)}, s16[128,2048]{1,0:T(8,128)(2,1)S(1)}, u32[]{:S(2)}, u32[]{:S(2)}) collective-permute-start(s16[128,2048]{1,0:T(8,128)(2,1)S(1)} %get-tuple-element.55), channel_id=1, source_target_pairs={{0,1},{1,0},{2,3},{3,2},{4,5},{5,4},{6,7},{7,6},{8,9},{9,8},{10,11... | collective-permute-start | bytes 1572872 | tf_op jit(solution)/shard_map/ppermute | solution.py:338
  35.9 0.0 collective-permute-done.9.refs_3_
  35.9 0.0 collective-permute-done.8.refs_2_
  35.9 0.0 collective-permute-done.7.refs_1_
  35.9 0.1 collective-permute-start.19
  36.0 0.5 collective-permute-start.20
  36.5 0.1 collective-permute-start.21
  36.6 1.5 %collective-permute-start.16 = (bf16[256,512]{1,0:T(8,128)(2,1)S(1)}, bf16[256,512]{1,0:T(8,128)(2,1)S(1)}, u32[]{:S(2)}, u32[]{:S(2)}) collective-permute-start(bf16[256,512]{1,0:T(8,128)(2,1)S(1)} %pad_maximum_fusion.1.refs_0_), channel_id=1, source_target_pairs={{0,4},{1,5},{2,6},{3,7},{4,0},{5,1},{6,2},{7,3},{8,12},{9,13},{10,... | collective-permute-start | bytes 786440 | tf_op jit(solution)/shard_map/ppermute | solution.py:290
  38.1 0.0 collective-permute-done.19.refs_4_
  38.1 0.2 collective-permute-start.12
  38.3 0.0 collective-permute-done.20.refs_5_
  38.3 0.0 collective-permute-start.22
  38.3 0.0 collective-permute-done.21.refs_6_
  38.3 2.1 %collective-permute-start.11 = (bf16[256,512]{1,0:T(8,128)(2,1)S(1)}, bf16[256,512]{1,0:T(8,128)(2,1)S(1)}, u32[]{:S(2)}, u32[]{:S(2)}) collective-permute-start(bf16[256,512]{1,0:T(8,128)(2,1)S(1)} %pad_maximum_fusion.1.refs_0_), channel_id=1, source_target_pairs={{0,8},{1,9},{2,10},{3,11},{4,12},{5,13},{6,14},{7,15},{8,0},{9,1},... | collective-permute-start | bytes 786440 | tf_op jit(solution)/shard_map/ppermute | solution.py:290
  40.4 0.0 collective-permute-done.22.refs_7_
  40.4 3.8 %away_product.3 = (s16[144,2048]{1,0:T(8,128)(2,1)S(1)}, f32[16,2048]{1,0:T(8,128)}) custom-call(s32[2,8]{1,0:T(2,128)S(1)} %copy-done, bf16[128,512]{1,0:T(8,128)(2,1)S(1)} %get-tuple-element.59.refs_0_, bf16[128,512]{1,0:T(8,128)(2,1)S(1)} %collective-permute-done.7.refs_1_, bf16[128,512]{1,0:T(8,128)(2,1)S(1)} %collective-permute-done.8.refs_2_, ...), custom_call_target="tpu_custom_call" | custom-call | flops 1 | bytes 1 | tf_op jit(solution)/shard_map/away_product/pallas_call | solution.py:190
  44.2 2.7 %collective-permute-start.23 = (s16[144,2048]{1,0:T(8,128)(2,1)S(1)}, s16[144,2048]{1,0:T(8,128)(2,1)S(1)}, u32[]{:S(2)}, u32[]{:S(2)}) collective-permute-start(s16[144,2048]{1,0:T(8,128)(2,1)S(1)} %get-tuple-element.64), channel_id=1, source_target_pairs={{0,1},{1,0},{2,3},{3,2},{4,5},{5,4},{6,7},{7,6},{8,9},{9,8},{10,11... | collective-permute-start | bytes 1769480 | tf_op jit(solution)/shard_map/ppermute | solution.py:344
  46.9 4.0 %collective-permute-done.16.refs_1_ = bf16[256,512]{1,0:T(8,128)(2,1)S(1)} collective-permute-done((bf16[256,512]{1,0:T(8,128)(2,1)S(1)}, bf16[256,512]{1,0:T(8,128)(2,1)S(1)}, u32[]{:S(2)}, u32[]{:S(2)}) %collective-permute-start.16) | collective-permute-done | bytes 262176 | tf_op jit(solution)/shard_map/ppermute | solution.py:290
  50.9 0.0 collective-permute-start.17
  50.9 0.0 collective-permute-done.12.refs_1_
  50.9 0.5 collective-permute-start.18
  51.4 0.9 %collective-permute-done.11.refs_0_ = bf16[256,512]{1,0:T(8,128)(2,1)S(1)} collective-permute-done((bf16[256,512]{1,0:T(8,128)(2,1)S(1)}, bf16[256,512]{1,0:T(8,128)(2,1)S(1)}, u32[]{:S(2)}, u32[]{:S(2)}) %collective-permute-start.11) | collective-permute-done | bytes 262176 | tf_op jit(solution)/shard_map/ppermute | solution.py:290
  52.3 0.0 collective-permute-done.13.refs_0_
  52.3 0.0 collective-permute-start.14
  52.3 0.5 collective-permute-start.15
  52.8 0.0 collective-permute-done.17.refs_2_
  52.8 0.0 collective-permute-done.18.refs_3_
  52.8 3.1 %own_product.2.refs_5_ = f32[256,2048]{1,0:T(8,128)S(1)} custom-call(s32[2,8]{1,0:T(2,128)S(1)} %copy-done, bf16[256,512]{1,0:T(8,128)(2,1)S(1)} %pad_maximum_fusion.1.refs_0_, bf16[256,512]{1,0:T(8,128)(2,1)S(1)} %collective-permute-done.16.refs_1_, bf16[256,512]{1,0:T(8,128)(2,1)S(1)} %collective-permute-done.17.refs_2_, ...), custom_call_target="tpu_custom_call" | custom-call | flops 1073741824 | bytes 1 | tf_op jit(solution)/shard_map/own_product/pallas_call | solution.py:190
  56.0 0.0 copy-start.1
  56.0 0.0 collective-permute-done.14.refs_2_
  56.0 0.0 collective-permute-done.15.refs_3_
  56.0 3.1 %own_product.3.own_ref = f32[256,2048]{1,0:T(8,128)S(1)} custom-call(s32[2,8]{1,0:T(2,128)S(1)} %copy-done, bf16[256,512]{1,0:T(8,128)(2,1)S(1)} %collective-permute-done.11.refs_0_, bf16[256,512]{1,0:T(8,128)(2,1)S(1)} %collective-permute-done.12.refs_1_, bf16[256,512]{1,0:T(8,128)(2,1)S(1)} %collective-permute-done.14.refs_2_, ...), custom_call_target="tpu_custom_call" | custom-call | flops 1073741824 | bytes 1 | tf_op jit(solution)/shard_map/own_product/pallas_call | solution.py:190
  59.1 1.4 %collective-permute-done.23.refs_1_ = s16[144,2048]{1,0:T(8,128)(2,1)S(1)} collective-permute-done((s16[144,2048]{1,0:T(8,128)(2,1)S(1)}, s16[144,2048]{1,0:T(8,128)(2,1)S(1)}, u32[]{:S(2)}, u32[]{:S(2)}) %collective-permute-start.23) | collective-permute-done | bytes 589856 | tf_op jit(solution)/shard_map/ppermute | solution.py:344
  60.5 0.0 copy-done.1
  60.5 2.2 %join.1 = bf16[512,2048]{1,0:T(8,128)(2,1)} custom-call(s32[2,16]{1,0:T(2,128)S(1)} %bitcast.10, f32[256,2048]{1,0:T(8,128)S(1)} %own_product.3.own_ref, s16[128,2048]{1,0:T(8,128)(2,1)S(1)} %collective-permute-done.13.refs_0_, s16[144,2048]{1,0:T(8,128)(2,1)S(1)} %collective-permute-done.23.refs_1_), custom_call_target="tpu_custom_call" | custom-call | tf_op jit(solution)/shard_map/join/pallas_call | solution.py:250
  (3 shorter events, 0.1 us)
Async XLA Ops:
  1.1 7.9 %collective-permute-start.3 = (bf16[128,512]{1,0:T(8,128)(2,1)S(1)}, bf16[128,512]{1,0:T(8,128)(2,1)S(1)}, u32[]{:S(2)}, u32[]{:S(2)}) collective-permute-start(bf16[128,512]{1,0:T(8,128)(2,1)S(1)} %get-tuple-element.35), channel_id=1, source_target_pairs={{0,2},{1,16},{2,0},{3,18},{4,6},{5,20},{6,4},{7,22},{8,10},{9,24},... | collective-permute-start | bytes 393224 | tf_op jit(solution)/shard_map/ppermute | solution.py:328
  1.6 8.5 %collective-permute-start = (bf16[128,512]{1,0:T(8,128)(2,1)S(1)}, bf16[128,512]{1,0:T(8,128)(2,1)S(1)}, u32[]{:S(2)}, u32[]{:S(2)}) collective-permute-start(bf16[128,512]{1,0:T(8,128)(2,1)S(1)} %get-tuple-element.35), channel_id=1, source_target_pairs={{0,16},{1,0},{2,18},{3,2},{4,20},{5,4},{6,22},{7,6},{8,24},{9,8},{... | collective-permute-start | bytes 393224 | tf_op jit(solution)/shard_map/ppermute | solution.py:328
  6.5 17.3 %collective-permute-start.2 = (bf16[128,512]{1,0:T(8,128)(2,1)S(1)}, bf16[128,512]{1,0:T(8,128)(2,1)S(1)}, u32[]{:S(2)}, u32[]{:S(2)}) collective-permute-start(bf16[128,512]{1,0:T(8,128)(2,1)S(1)} %get-tuple-element.36), channel_id=1, source_target_pairs={{0,2},{1,16},{2,0},{3,18},{4,6},{5,20},{6,4},{7,22},{8,10},{9,24},... | collective-permute-start | bytes 393224 | tf_op jit(solution)/shard_map/ppermute | solution.py:328
  6.5 17.3 %collective-permute-start.1 = (bf16[128,512]{1,0:T(8,128)(2,1)S(1)}, bf16[128,512]{1,0:T(8,128)(2,1)S(1)}, u32[]{:S(2)}, u32[]{:S(2)}) collective-permute-start(bf16[128,512]{1,0:T(8,128)(2,1)S(1)} %get-tuple-element.36), channel_id=1, source_target_pairs={{0,16},{1,0},{2,18},{3,2},{4,20},{5,4},{6,22},{7,6},{8,24},{9,8},{... | collective-permute-start | bytes 393224 | tf_op jit(solution)/shard_map/ppermute | solution.py:328
  10.1 18.3 %copy-start = (s32[2,8]{1,0:T(2,128)S(1)}, s32[2,8]{1,0:T(2,128)}, u32[]{:S(2)}) copy-start(s32[2,8]{1,0:T(2,128)} %int_screen_ref.7) | copy-start | bytes 196
  10.1 13.7 %collective-permute-start.6 = (bf16[128,512]{1,0:T(8,128)(2,1)S(1)}, bf16[128,512]{1,0:T(8,128)(2,1)S(1)}, u32[]{:S(2)}, u32[]{:S(2)}) collective-permute-start(bf16[128,512]{1,0:T(8,128)(2,1)S(1)} %get-tuple-element.43.after.refs_0_), channel_id=1, source_target_pairs={{0,12},{1,13},{2,14},{3,15},{4,8},{5,9},{6,10},{7,11},{8,4},{9,5},... | collective-permute-start | bytes 393224 | tf_op jit(solution)/shard_map/ppermute | solution.py:290
  17.2 6.6 %collective-permute-start.5 = (bf16[128,512]{1,0:T(8,128)(2,1)S(1)}, bf16[128,512]{1,0:T(8,128)(2,1)S(1)}, u32[]{:S(2)}, u32[]{:S(2)}) collective-permute-start(bf16[128,512]{1,0:T(8,128)(2,1)S(1)} %get-tuple-element.43.after.refs_0_), channel_id=1, source_target_pairs={{0,8},{1,9},{2,10},{3,11},{4,12},{5,13},{6,14},{7,15},{8,0},{9,1},... | collective-permute-start | bytes 393224 | tf_op jit(solution)/shard_map/ppermute | solution.py:290
  17.2 7.5 %collective-permute-start.4 = (bf16[128,512]{1,0:T(8,128)(2,1)S(1)}, bf16[128,512]{1,0:T(8,128)(2,1)S(1)}, u32[]{:S(2)}, u32[]{:S(2)}) collective-permute-start(bf16[128,512]{1,0:T(8,128)(2,1)S(1)} %get-tuple-element.43.after.refs_0_), channel_id=1, source_target_pairs={{0,4},{1,5},{2,6},{3,7},{4,0},{5,1},{6,2},{7,3},{8,12},{9,13},{10,... | collective-permute-start | bytes 393224 | tf_op jit(solution)/shard_map/ppermute | solution.py:290
  24.7 3.6 %collective-permute-start.10 = (bf16[4,128,512]{2,1,0:T(8,128)(2,1)S(1)}, bf16[4,128,512]{2,1,0:T(8,128)(2,1)S(1)}, u32[]{:S(2)}, u32[]{:S(2)}) collective-permute-start(bf16[4,128,512]{2,1,0:T(8,128)(2,1)S(1)} %pad_maximum_fusion), channel_id=1, source_target_pairs={{0,2},{1,3},{2,0},{3,1},{4,6},{5,7},{6,4},{7,5},{8,10},{9,11},{10,... | collective-permute-start | bytes 1572872 | tf_op jit(solution)/shard_map/ppermute | solution.py:336
  24.8 11.1 %collective-permute-start.9 = (bf16[128,512]{1,0:T(8,128)(2,1)S(1)}, bf16[128,512]{1,0:T(8,128)(2,1)S(1)}, u32[]{:S(2)}, u32[]{:S(2)}) collective-permute-start(bf16[128,512]{1,0:T(8,128)(2,1)S(1)} %get-tuple-element.59.refs_0_), channel_id=1, source_target_pairs={{0,12},{1,13},{2,14},{3,15},{4,8},{5,9},{6,10},{7,11},{8,4},{9,5},... | collective-permute-start | bytes 393224 | tf_op jit(solution)/shard_map/ppermute | solution.py:290
  26.9 9.0 %collective-permute-start.8 = (bf16[128,512]{1,0:T(8,128)(2,1)S(1)}, bf16[128,512]{1,0:T(8,128)(2,1)S(1)}, u32[]{:S(2)}, u32[]{:S(2)}) collective-permute-start(bf16[128,512]{1,0:T(8,128)(2,1)S(1)} %get-tuple-element.59.refs_0_), channel_id=1, source_target_pairs={{0,8},{1,9},{2,10},{3,11},{4,12},{5,13},{6,14},{7,15},{8,0},{9,1},... | collective-permute-start | bytes 393224 | tf_op jit(solution)/shard_map/ppermute | solution.py:290
  27.0 9.0 %collective-permute-start.7 = (bf16[128,512]{1,0:T(8,128)(2,1)S(1)}, bf16[128,512]{1,0:T(8,128)(2,1)S(1)}, u32[]{:S(2)}, u32[]{:S(2)}) collective-permute-start(bf16[128,512]{1,0:T(8,128)(2,1)S(1)} %get-tuple-element.59.refs_0_), channel_id=1, source_target_pairs={{0,4},{1,5},{2,6},{3,7},{4,0},{5,1},{6,2},{7,3},{8,12},{9,13},{10,... | collective-permute-start | bytes 393224 | tf_op jit(solution)/shard_map/ppermute | solution.py:290
  31.6 20.7 %collective-permute-start.13 = (s16[128,2048]{1,0:T(8,128)(2,1)S(1)}, s16[128,2048]{1,0:T(8,128)(2,1)S(1)}, u32[]{:S(2)}, u32[]{:S(2)}) collective-permute-start(s16[128,2048]{1,0:T(8,128)(2,1)S(1)} %get-tuple-element.55), channel_id=1, source_target_pairs={{0,1},{1,0},{2,3},{3,2},{4,5},{5,4},{6,7},{7,6},{8,9},{9,8},{10,11... | collective-permute-start | bytes 1572872 | tf_op jit(solution)/shard_map/ppermute | solution.py:338
  35.9 2.2 %collective-permute-start.19 = (bf16[128,512]{1,0:T(8,128)(2,1)S(1)}, bf16[128,512]{1,0:T(8,128)(2,1)S(1)}, u32[]{:S(2)}, u32[]{:S(2)}) collective-permute-start(bf16[128,512]{1,0:T(8,128)(2,1)S(1)} %get-tuple-element.59.refs_0_), channel_id=1, source_target_pairs={{0,2},{1,3},{2,0},{3,1},{4,6},{5,7},{6,4},{7,5},{8,10},{9,11},{10,... | collective-permute-start | bytes 393224 | tf_op jit(solution)/shard_map/ppermute | solution.py:311
  36.0 2.3 %collective-permute-start.20 = (bf16[128,512]{1,0:T(8,128)(2,1)S(1)}, bf16[128,512]{1,0:T(8,128)(2,1)S(1)}, u32[]{:S(2)}, u32[]{:S(2)}) collective-permute-start(bf16[128,512]{1,0:T(8,128)(2,1)S(1)} %collective-permute-done.7.refs_1_), channel_id=1, source_target_pairs={{0,2},{1,3},{2,0},{3,1},{4,6},{5,7},{6,4},{7,5},{8,10},{9,11},{10,... | collective-permute-start | bytes 393224 | tf_op jit(solution)/shard_map/ppermute | solution.py:311
  36.5 1.8 %collective-permute-start.21 = (bf16[128,512]{1,0:T(8,128)(2,1)S(1)}, bf16[128,512]{1,0:T(8,128)(2,1)S(1)}, u32[]{:S(2)}, u32[]{:S(2)}) collective-permute-start(bf16[128,512]{1,0:T(8,128)(2,1)S(1)} %collective-permute-done.8.refs_2_), channel_id=1, source_target_pairs={{0,2},{1,3},{2,0},{3,1},{4,6},{5,7},{6,4},{7,5},{8,10},{9,11},{10,... | collective-permute-start | bytes 393224 | tf_op jit(solution)/shard_map/ppermute | solution.py:311
  36.6 14.3 %collective-permute-start.16 = (bf16[256,512]{1,0:T(8,128)(2,1)S(1)}, bf16[256,512]{1,0:T(8,128)(2,1)S(1)}, u32[]{:S(2)}, u32[]{:S(2)}) collective-permute-start(bf16[256,512]{1,0:T(8,128)(2,1)S(1)} %pad_maximum_fusion.1.refs_0_), channel_id=1, source_target_pairs={{0,4},{1,5},{2,6},{3,7},{4,0},{5,1},{6,2},{7,3},{8,12},{9,13},{10,... | collective-permute-start | bytes 786440 | tf_op jit(solution)/shard_map/ppermute | solution.py:290
  38.1 12.8 %collective-permute-start.12 = (bf16[256,512]{1,0:T(8,128)(2,1)S(1)}, bf16[256,512]{1,0:T(8,128)(2,1)S(1)}, u32[]{:S(2)}, u32[]{:S(2)}) collective-permute-start(bf16[256,512]{1,0:T(8,128)(2,1)S(1)} %pad_maximum_fusion.1.refs_0_), channel_id=1, source_target_pairs={{0,12},{1,13},{2,14},{3,15},{4,8},{5,9},{6,10},{7,11},{8,4},{9,5},... | collective-permute-start | bytes 786440 | tf_op jit(solution)/shard_map/ppermute | solution.py:290
  38.3 2.1 %collective-permute-start.22 = (bf16[128,512]{1,0:T(8,128)(2,1)S(1)}, bf16[128,512]{1,0:T(8,128)(2,1)S(1)}, u32[]{:S(2)}, u32[]{:S(2)}) collective-permute-start(bf16[128,512]{1,0:T(8,128)(2,1)S(1)} %collective-permute-done.9.refs_3_), channel_id=1, source_target_pairs={{0,2},{1,3},{2,0},{3,1},{4,6},{5,7},{6,4},{7,5},{8,10},{9,11},{10,... | collective-permute-start | bytes 393224 | tf_op jit(solution)/shard_map/ppermute | solution.py:311
  38.3 14.0 %collective-permute-start.11 = (bf16[256,512]{1,0:T(8,128)(2,1)S(1)}, bf16[256,512]{1,0:T(8,128)(2,1)S(1)}, u32[]{:S(2)}, u32[]{:S(2)}) collective-permute-start(bf16[256,512]{1,0:T(8,128)(2,1)S(1)} %pad_maximum_fusion.1.refs_0_), channel_id=1, source_target_pairs={{0,8},{1,9},{2,10},{3,11},{4,12},{5,13},{6,14},{7,15},{8,0},{9,1},... | collective-permute-start | bytes 786440 | tf_op jit(solution)/shard_map/ppermute | solution.py:290
  44.2 16.3 %collective-permute-start.23 = (s16[144,2048]{1,0:T(8,128)(2,1)S(1)}, s16[144,2048]{1,0:T(8,128)(2,1)S(1)}, u32[]{:S(2)}, u32[]{:S(2)}) collective-permute-start(s16[144,2048]{1,0:T(8,128)(2,1)S(1)} %get-tuple-element.64), channel_id=1, source_target_pairs={{0,1},{1,0},{2,3},{3,2},{4,5},{5,4},{6,7},{7,6},{8,9},{9,8},{10,11... | collective-permute-start | bytes 1769480 | tf_op jit(solution)/shard_map/ppermute | solution.py:344
  50.9 2.0 %collective-permute-start.17 = (bf16[256,512]{1,0:T(8,128)(2,1)S(1)}, bf16[256,512]{1,0:T(8,128)(2,1)S(1)}, u32[]{:S(2)}, u32[]{:S(2)}) collective-permute-start(bf16[256,512]{1,0:T(8,128)(2,1)S(1)} %pad_maximum_fusion.1.refs_0_), channel_id=1, source_target_pairs={{0,2},{1,3},{2,0},{3,1},{4,6},{5,7},{6,4},{7,5},{8,10},{9,11},{10,... | collective-permute-start | bytes 786440 | tf_op jit(solution)/shard_map/ppermute | solution.py:311
  50.9 2.0 %collective-permute-start.18 = (bf16[256,512]{1,0:T(8,128)(2,1)S(1)}, bf16[256,512]{1,0:T(8,128)(2,1)S(1)}, u32[]{:S(2)}, u32[]{:S(2)}) collective-permute-start(bf16[256,512]{1,0:T(8,128)(2,1)S(1)} %collective-permute-done.16.refs_1_), channel_id=1, source_target_pairs={{0,2},{1,3},{2,0},{3,1},{4,6},{5,7},{6,4},{7,5},{8,10},{9,11},{10,... | collective-permute-start | bytes 786440 | tf_op jit(solution)/shard_map/ppermute | solution.py:311
  52.3 3.7 %collective-permute-start.14 = (bf16[256,512]{1,0:T(8,128)(2,1)S(1)}, bf16[256,512]{1,0:T(8,128)(2,1)S(1)}, u32[]{:S(2)}, u32[]{:S(2)}) collective-permute-start(bf16[256,512]{1,0:T(8,128)(2,1)S(1)} %collective-permute-done.11.refs_0_), channel_id=1, source_target_pairs={{0,2},{1,3},{2,0},{3,1},{4,6},{5,7},{6,4},{7,5},{8,10},{9,11},{10,... | collective-permute-start | bytes 786440 | tf_op jit(solution)/shard_map/ppermute | solution.py:311
  52.3 3.7 %collective-permute-start.15 = (bf16[256,512]{1,0:T(8,128)(2,1)S(1)}, bf16[256,512]{1,0:T(8,128)(2,1)S(1)}, u32[]{:S(2)}, u32[]{:S(2)}) collective-permute-start(bf16[256,512]{1,0:T(8,128)(2,1)S(1)} %collective-permute-done.12.refs_1_), channel_id=1, source_target_pairs={{0,2},{1,3},{2,0},{3,1},{4,6},{5,7},{6,4},{7,5},{8,10},{9,11},{10,... | collective-permute-start | bytes 786440 | tf_op jit(solution)/shard_map/ppermute | solution.py:311
  56.0 4.6 %copy-start.1 = (s32[16,2]{0,1:T(2,128)S(1)}, s32[16,2]{0,1:T(2,128)}, u32[]{:S(2)}) copy-start(s32[16,2]{0,1:T(2,128)} %param.6) | copy-start | bytes 388

commit v7 on v6

--- a/solution.py
+++ b/solution.py
@@ -185,19 +185,20 @@
         code_ref[panel.shape[0] :, :] = scale_ref[...].astype(jnp.int32).astype(jnp.int16)
 
 
-def product(kernel, int_screen, arrays, row_count, ints, out_rows_types, cost, name, parts=1):
+def product(kernel, int_screen, arrays, gates, row_count, ints, out_rows_types, cost, name, parts=1):
     int_count, ab_count = ints.shape
     return pl.pallas_call(
         kernel,
         out_shape=[jax.ShapeDtypeStruct((rows, ab_count), dtype) for rows, dtype in out_rows_types],
         in_specs=[pl.BlockSpec(memory_space=pltpu.SMEM)]
-        + [WHOLE] * len(arrays),
+        + [WHOLE] * len(arrays)
+        + [pl.BlockSpec(memory_space=pl.ANY)] * len(gates),
         out_specs=[WHOLE] * len(out_rows_types),
         scratch_shapes=[pltpu.VMEM((row_count, int_count // parts), ints.dtype)],
         compiler_params=pltpu.CompilerParams(vmem_limit_bytes=PRODUCT_VMEM),
         cost_estimate=cost,
         name=name,
-    )(int_screen, *arrays)
+    )(int_screen, *arrays, *gates)
 
 
 def join_kernel(screen_ref, own_ref, *refs):
@@ -314,7 +315,7 @@
         rows = near[0].shape[0]
         code_rows = rows + (2 * SCALE_ROWS if first else 0)
         return product(
-            functools.partial(away_kernel, pair_size, len(near), first), int_screen, [*near, *other, ints, before],
+            functools.partial(away_kernel, pair_size, len(near), first), int_screen, [*near, *other, ints, before], [],
             rows, ints, ((code_rows, jnp.int16), (2 * SCALE_ROWS, jnp.float32)), LIGHT, "away_product",
         )
 
@@ -322,7 +323,7 @@
         rows = own_block.shape[0]
         return product(
             functools.partial(own_kernel, pair_size, len(near), part), int_screen,
-            [*near, *crossed(near), ints, *before], rows, ints, ((rows, jnp.float32),), MEDIUM, "own_product", 2,
+            [*near, *crossed(near), ints, *before], [gate], rows, ints, ((rows, jnp.float32),), MEDIUM, "own_product", 2,
         )[0]
 
     arrived = [(lax.ppermute(part, AXES, first), lax.ppermute(part, AXES, across)) for part in picked]
@@ -338,7 +339,7 @@
     came_a = lax.ppermute(code_a, AXES, swap)
     near_b = near_blocks(away_b, flip, block_count)
     near_b, scale_a = lax.optimization_barrier((near_b, scale_a))
-    own_block, near_b = lax.optimization_barrier((own_block, near_b))
+    own_block, gate = lax.optimization_barrier((own_block, scale_a))
     own_near = near_blocks(own_block, flip, block_count)
     code_b, _ = away_product(near_b, crossed(near_b), scale_a, SLOT_CHUNKS[1][0])
     came_b = lax.ppermute(code_b, AXES, swap)

time: 62.8 us -> 61.8 us (0.984)
  starting transfers between devices: 31.7 us -> 26.8 us
  waiting for transfers between devices: 8.26 us -> 12.1 us
    ppermute x2, starting transfers between devices: 7.41 us -> 5.61 us  [two_group_shards(): lax.ppermute(part, AXES, first)]
    ppermute x9, waiting for transfers between devices: 5.76 us -> 7.24 us  [near_blocks(): lax.ppermute(block, AXES, flip(bits))]
    ppermute x1, starting transfers between devices: 4.3 us -> 2.92 us  [two_group_shards(): came_a = lax.ppermute(code_a, AXES, swap)]
    ppermute x2, waiting for transfers between devices: 1.07 us -> 2.42 us  [two_group_shards(): lax.ppermute(part, AXES, first)]
    ppermute x9, starting transfers between devices: 15 us -> 14.2 us  [near_blocks(): lax.ppermute(block, AXES, flip(bits))]
    ppermute x8, starting transfers between devices: 1.71 us -> 1.03 us  [crossed(): return [lax.ppermute(block, AXES, flip(1)) for block in near]]
  transfers between devices with their start and end apart: 24 -> 24, of which waited for: 5 -> 7; matrix products, arithmetic and copies ran while one was open for 0% -> 0% of each run, Pallas kernels for 31% -> 31%
where the time goes in v7:
time: 61.8 us; the launch traced here: 61.7 us
  starting transfers between devices  26.8 us (43%)
  Pallas kernels  22.4 us (36%)
  waiting for transfers between devices  12.1 us (20%)
    ppermute x9, starting transfers between devices, near_blocks(): lax.ppermute(block, AXES, flip(bits))  14.2 us
    pallas_call x4, Pallas kernels, product(): pl.pallas_call(kernel, out_shape=[jax.ShapeDtypeStruct((rows, ab_count),...  13.3 us
    ppermute x9, waiting for transfers between devices, near_blocks(): lax.ppermute(block, AXES, flip(bits))  7.24 us
    pallas_call x1, Pallas kernels, stage(): pl.pallas_call(stage_kernel, out_shape=[pltpu.VMEM(integrals.shape, integ...  5.92 us
    ppermute x2, starting transfers between devices, two_group_shards(): lax.ppermute(part, AXES, first)  5.61 us
    ppermute x1, starting transfers between devices, two_group_shards(): came_b = lax.ppermute(code_b, AXES, swap)  2.95 us
    ppermute x1, starting transfers between devices, two_group_shards(): came_a = lax.ppermute(code_a, AXES, swap)  2.92 us
    ppermute x2, waiting for transfers between devices, two_group_shards(): lax.ppermute(part, AXES, first)  2.42 us
  transfers between devices with their start and end apart: 24, of which 7 were waited for; matrix products, arithmetic and copies ran while one was open for 0% of the time, Pallas kernels for 31%

profile of v7, /device:TPU:0, one launch (start us, length us, event | category | flops | bytes accessed | tf_op | source)
XLA Modules:
  0.0 61.7 jit_solution(13347663119298063356)
XLA Ops:
  0.0 1.1 %pick_live.1 = (bf16[128,512]{1,0:T(8,128)(2,1)S(1)}, bf16[128,512]{1,0:T(8,128)(2,1)S(1)}) custom-call(s32[2,16]{1,0:T(2,128)} %bitcast.9, bf16[512,512]{1,0:T(8,128)(2,1)} %amps_hbm.1), custom_call_target="tpu_custom_call" | custom-call | tf_op jit(solution)/shard_map/pick_live/pallas_call | solution.py:58
  1.1 4.1 %collective-permute-start = (bf16[128,512]{1,0:T(8,128)(2,1)S(1)}, bf16[128,512]{1,0:T(8,128)(2,1)S(1)}, u32[]{:S(2)}, u32[]{:S(2)}) collective-permute-start(bf16[128,512]{1,0:T(8,128)(2,1)S(1)} %get-tuple-element.32), channel_id=1, source_target_pairs={{0,16},{1,0},{2,18},{3,2},{4,20},{5,4},{6,22},{7,6},{8,24},{9,8},{... | collective-permute-start | bytes 393224 | tf_op jit(solution)/shard_map/ppermute | solution.py:329
  5.2 0.0 collective-permute-start.3
  5.2 1.5 %collective-permute-start.1 = (bf16[128,512]{1,0:T(8,128)(2,1)S(1)}, bf16[128,512]{1,0:T(8,128)(2,1)S(1)}, u32[]{:S(2)}, u32[]{:S(2)}) collective-permute-start(bf16[128,512]{1,0:T(8,128)(2,1)S(1)} %get-tuple-element.33), channel_id=1, source_target_pairs={{0,16},{1,0},{2,18},{3,2},{4,20},{5,4},{6,22},{7,6},{8,24},{9,8},{... | collective-permute-start | bytes 393224 | tf_op jit(solution)/shard_map/ppermute | solution.py:329
  6.7 0.0 collective-permute-start.2
  6.7 2.4 %collective-permute-done = bf16[128,512]{1,0:T(8,128)(2,1)S(1)} collective-permute-done((bf16[128,512]{1,0:T(8,128)(2,1)S(1)}, bf16[128,512]{1,0:T(8,128)(2,1)S(1)}, u32[]{:S(2)}, u32[]{:S(2)}) %collective-permute-start) | collective-permute-done | bytes 131104 | tf_op jit(solution)/shard_map/ppermute | solution.py:329
  9.1 0.0 collective-permute-done.3
  9.2 0.0 copy-start
  9.2 1.6 %collective-permute-start.4 = (bf16[128,512]{1,0:T(8,128)(2,1)S(1)}, bf16[128,512]{1,0:T(8,128)(2,1)S(1)}, u32[]{:S(2)}, u32[]{:S(2)}) collective-permute-start(bf16[128,512]{1,0:T(8,128)(2,1)S(1)} %get-tuple-element.40.after.refs_0_), channel_id=1, source_target_pairs={{0,4},{1,5},{2,6},{3,7},{4,0},{5,1},{6,2},{7,3},{8,12},{9,13},{10,... | collective-permute-start | bytes 393224 | tf_op jit(solution)/shard_map/ppermute | solution.py:291
  10.7 6.0 %collective-permute-start.5 = (bf16[128,512]{1,0:T(8,128)(2,1)S(1)}, bf16[128,512]{1,0:T(8,128)(2,1)S(1)}, u32[]{:S(2)}, u32[]{:S(2)}) collective-permute-start(bf16[128,512]{1,0:T(8,128)(2,1)S(1)} %get-tuple-element.40.after.refs_0_), channel_id=1, source_target_pairs={{0,8},{1,9},{2,10},{3,11},{4,12},{5,13},{6,14},{7,15},{8,0},{9,1},... | collective-permute-start | bytes 393224 | tf_op jit(solution)/shard_map/ppermute | solution.py:291
  16.7 0.0 collective-permute-start.6
  16.7 5.9 %stage_integrals.1 = (bf16[4096,2048]{1,0:T(8,128)(2,1)S(1)}, f32[8,128]{1,0:T(8,128)S(1)}) custom-call(bf16[4096,2048]{1,0:T(8,128)(2,1)} %ints_hbm.1, bf16[128,512]{1,0:T(8,128)(2,1)S(1)} %get-tuple-element.40.after.refs_0_), custom_call_target="tpu_custom_call" | custom-call | flops 1 | bytes 1 | tf_op jit(solution)/shard_map/stage_integrals/pallas_call | solution.py:97
  22.6 0.0 collective-permute-done.1
  22.6 0.0 collective-permute-done.2
  22.7 0.0 collective-permute-done.4.refs_1_
  22.7 0.0 collective-permute-done.5.refs_2_
  22.7 2.2 %collective-permute-done.6.refs_3_ = bf16[128,512]{1,0:T(8,128)(2,1)S(1)} collective-permute-done((bf16[128,512]{1,0:T(8,128)(2,1)S(1)}, bf16[128,512]{1,0:T(8,128)(2,1)S(1)}, u32[]{:S(2)}, u32[]{:S(2)}) %collective-permute-start.6) | collective-permute-done | bytes 131104 | tf_op jit(solution)/shard_map/ppermute | solution.py:291
  24.9 0.1 pad_maximum_fusion
  25.0 0.1 collective-permute-start.10
  25.0 0.6 collective-permute-start.7
  25.6 0.8 %collective-permute-start.8 = (bf16[128,512]{1,0:T(8,128)(2,1)S(1)}, bf16[128,512]{1,0:T(8,128)(2,1)S(1)}, u32[]{:S(2)}, u32[]{:S(2)}) collective-permute-start(bf16[128,512]{1,0:T(8,128)(2,1)S(1)} %get-tuple-element.54.refs_0_), channel_id=1, source_target_pairs={{0,8},{1,9},{2,10},{3,11},{4,12},{5,13},{6,14},{7,15},{8,0},{9,1},... | collective-permute-start | bytes 393224 | tf_op jit(solution)/shard_map/ppermute | solution.py:291
  26.4 2.1 %collective-permute-start.9 = (bf16[128,512]{1,0:T(8,128)(2,1)S(1)}, bf16[128,512]{1,0:T(8,128)(2,1)S(1)}, u32[]{:S(2)}, u32[]{:S(2)}) collective-permute-start(bf16[128,512]{1,0:T(8,128)(2,1)S(1)} %get-tuple-element.54.refs_0_), channel_id=1, source_target_pairs={{0,12},{1,13},{2,14},{3,15},{4,8},{5,9},{6,10},{7,11},{8,4},{9,5},... | collective-permute-start | bytes 393224 | tf_op jit(solution)/shard_map/ppermute | solution.py:291
  28.6 0.0 collective-permute-done.10.refs_4_
  28.6 0.0 copy-done
  28.6 3.2 %away_product.2 = (s16[128,2048]{1,0:T(8,128)(2,1)S(1)}, f32[16,2048]{1,0:T(8,128)S(1)}) custom-call(s32[2,8]{1,0:T(2,128)S(1)} %copy-done, bf16[128,512]{1,0:T(8,128)(2,1)S(1)} %get-tuple-element.40.after.refs_0_, bf16[128,512]{1,0:T(8,128)(2,1)S(1)} %collective-permute-done.4.refs_1_, bf16[128,512]{1,0:T(8,128)(2,1)S(1)} %collective-permute-done.5.refs_2_, ...), custom_call_target="tpu_custom_call" | custom-call | flops 1 | bytes 1 | tf_op jit(solution)/shard_map/away_product/pallas_call | solution.py:190
  31.8 2.9 %collective-permute-start.13 = (s16[128,2048]{1,0:T(8,128)(2,1)S(1)}, s16[128,2048]{1,0:T(8,128)(2,1)S(1)}, u32[]{:S(2)}, u32[]{:S(2)}) collective-permute-start(s16[128,2048]{1,0:T(8,128)(2,1)S(1)} %get-tuple-element.49), channel_id=1, source_target_pairs={{0,1},{1,0},{2,3},{3,2},{4,5},{5,4},{6,7},{7,6},{8,9},{9,8},{10,11... | collective-permute-start | bytes 1572872 | tf_op jit(solution)/shard_map/ppermute | solution.py:339
  34.7 0.0 collective-permute-done.7.refs_1_
  34.7 0.0 collective-permute-done.8.refs_2_
  34.7 0.2 collective-permute-done.9.refs_3_
  34.9 0.0 collective-permute-start.19
  34.9 0.5 collective-permute-start.20
  35.4 0.0 collective-permute-start.21
  35.5 0.3 collective-permute-start.11
  35.8 0.5 collective-permute-done.19.refs_4_
  36.3 1.4 %collective-permute-start.16 = (bf16[256,512]{1,0:T(8,128)(2,1)S(1)}, bf16[256,512]{1,0:T(8,128)(2,1)S(1)}, u32[]{:S(2)}, u32[]{:S(2)}) collective-permute-start(bf16[256,512]{1,0:T(8,128)(2,1)S(1)} %pad_maximum_fusion.1.refs_0_), channel_id=1, source_target_pairs={{0,4},{1,5},{2,6},{3,7},{4,0},{5,1},{6,2},{7,3},{8,12},{9,13},{10,... | collective-permute-start | bytes 786440 | tf_op jit(solution)/shard_map/ppermute | solution.py:291
  37.7 0.0 collective-permute-done.20.refs_5_
  37.7 0.0 collective-permute-start.22
  37.7 0.0 collective-permute-done.21.refs_6_
  37.7 1.4 %collective-permute-start.12 = (bf16[256,512]{1,0:T(8,128)(2,1)S(1)}, bf16[256,512]{1,0:T(8,128)(2,1)S(1)}, u32[]{:S(2)}, u32[]{:S(2)}) collective-permute-start(bf16[256,512]{1,0:T(8,128)(2,1)S(1)} %pad_maximum_fusion.1.refs_0_), channel_id=1, source_target_pairs={{0,12},{1,13},{2,14},{3,15},{4,8},{5,9},{6,10},{7,11},{8,4},{9,5},... | collective-permute-start | bytes 786440 | tf_op jit(solution)/shard_map/ppermute | solution.py:291
  39.1 0.0 collective-permute-done.22.refs_7_
  39.1 3.8 %away_product.3 = (s16[144,2048]{1,0:T(8,128)(2,1)S(1)}, f32[16,2048]{1,0:T(8,128)}) custom-call(s32[2,8]{1,0:T(2,128)S(1)} %copy-done, bf16[128,512]{1,0:T(8,128)(2,1)S(1)} %get-tuple-element.54.refs_0_, bf16[128,512]{1,0:T(8,128)(2,1)S(1)} %collective-permute-done.7.refs_1_, bf16[128,512]{1,0:T(8,128)(2,1)S(1)} %collective-permute-done.8.refs_2_, ...), custom_call_target="tpu_custom_call" | custom-call | flops 1 | bytes 1 | tf_op jit(solution)/shard_map/away_product/pallas_call | solution.py:190
  42.9 2.9 %collective-permute-start.23 = (s16[144,2048]{1,0:T(8,128)(2,1)S(1)}, s16[144,2048]{1,0:T(8,128)(2,1)S(1)}, u32[]{:S(2)}, u32[]{:S(2)}) collective-permute-start(s16[144,2048]{1,0:T(8,128)(2,1)S(1)} %get-tuple-element.58), channel_id=1, source_target_pairs={{0,1},{1,0},{2,3},{3,2},{4,5},{5,4},{6,7},{7,6},{8,9},{9,8},{10,11... | collective-permute-start | bytes 1769480 | tf_op jit(solution)/shard_map/ppermute | solution.py:345
  45.9 0.0 collective-permute-done.11.refs_0_
  45.9 0.0 collective-permute-start.17
  45.9 3.3 %collective-permute-done.16.refs_1_ = bf16[256,512]{1,0:T(8,128)(2,1)S(1)} collective-permute-done((bf16[256,512]{1,0:T(8,128)(2,1)S(1)}, bf16[256,512]{1,0:T(8,128)(2,1)S(1)}, u32[]{:S(2)}, u32[]{:S(2)}) %collective-permute-start.16) | collective-permute-done | bytes 262176 | tf_op jit(solution)/shard_map/ppermute | solution.py:291
  49.2 0.0 collective-permute-start.18
  49.2 1.5 %collective-permute-done.12.refs_1_ = bf16[256,512]{1,0:T(8,128)(2,1)S(1)} collective-permute-done((bf16[256,512]{1,0:T(8,128)(2,1)S(1)}, bf16[256,512]{1,0:T(8,128)(2,1)S(1)}, u32[]{:S(2)}, u32[]{:S(2)}) %collective-permute-start.12) | collective-permute-done | bytes 262176 | tf_op jit(solution)/shard_map/ppermute | solution.py:291
  50.7 0.0 collective-permute-done.13.refs_0_
  50.7 0.0 collective-permute-start.14
  50.7 0.5 collective-permute-start.15
  51.3 0.0 collective-permute-done.17.refs_2_
  51.3 0.0 collective-permute-done.18.refs_3_
  51.3 3.1 %own_product.2.refs_5_ = f32[256,2048]{1,0:T(8,128)S(1)} custom-call(s32[2,8]{1,0:T(2,128)S(1)} %copy-done, bf16[256,512]{1,0:T(8,128)(2,1)S(1)} %pad_maximum_fusion.1.refs_0_, bf16[256,512]{1,0:T(8,128)(2,1)S(1)} %collective-permute-done.16.refs_1_, bf16[256,512]{1,0:T(8,128)(2,1)S(1)} %collective-permute-done.17.refs_2_, ...), custom_call_target="tpu_custom_call" | custom-call | flops 1073741824 | bytes 1 | tf_op jit(solution)/shard_map/own_product/pallas_call | solution.py:190
  54.4 0.0 copy-start.1
  54.4 0.0 collective-permute-done.14.refs_2_
  54.4 0.0 collective-permute-done.15.refs_3_
  54.4 3.1 %own_product.3.own_ref = f32[256,2048]{1,0:T(8,128)S(1)} custom-call(s32[2,8]{1,0:T(2,128)S(1)} %copy-done, bf16[256,512]{1,0:T(8,128)(2,1)S(1)} %collective-permute-done.11.refs_0_, bf16[256,512]{1,0:T(8,128)(2,1)S(1)} %collective-permute-done.12.refs_1_, bf16[256,512]{1,0:T(8,128)(2,1)S(1)} %collective-permute-done.14.refs_2_, ...), custom_call_target="tpu_custom_call" | custom-call | flops 1073741824 | bytes 1 | tf_op jit(solution)/shard_map/own_product/pallas_call | solution.py:190
  57.6 2.0 %collective-permute-done.23.refs_1_ = s16[144,2048]{1,0:T(8,128)(2,1)S(1)} collective-permute-done((s16[144,2048]{1,0:T(8,128)(2,1)S(1)}, s16[144,2048]{1,0:T(8,128)(2,1)S(1)}, u32[]{:S(2)}, u32[]{:S(2)}) %collective-permute-start.23) | collective-permute-done | bytes 589856 | tf_op jit(solution)/shard_map/ppermute | solution.py:345
  59.5 0.0 copy-done.1
  59.5 2.1 %join.1 = bf16[512,2048]{1,0:T(8,128)(2,1)} custom-call(s32[2,16]{1,0:T(2,128)S(1)} %bitcast.10, f32[256,2048]{1,0:T(8,128)S(1)} %own_product.3.own_ref, s16[128,2048]{1,0:T(8,128)(2,1)S(1)} %collective-permute-done.13.refs_0_, s16[144,2048]{1,0:T(8,128)(2,1)S(1)} %collective-permute-done.23.refs_1_), custom_call_target="tpu_custom_call" | custom-call | tf_op jit(solution)/shard_map/join/pallas_call | solution.py:251
  (3 shorter events, 0.1 us)
Async XLA Ops:
  1.1 8.0 %collective-permute-start = (bf16[128,512]{1,0:T(8,128)(2,1)S(1)}, bf16[128,512]{1,0:T(8,128)(2,1)S(1)}, u32[]{:S(2)}, u32[]{:S(2)}) collective-permute-start(bf16[128,512]{1,0:T(8,128)(2,1)S(1)} %get-tuple-element.32), channel_id=1, source_target_pairs={{0,16},{1,0},{2,18},{3,2},{4,20},{5,4},{6,22},{7,6},{8,24},{9,8},{... | collective-permute-start | bytes 393224 | tf_op jit(solution)/shard_map/ppermute | solution.py:329
  5.2 3.9 %collective-permute-start.3 = (bf16[128,512]{1,0:T(8,128)(2,1)S(1)}, bf16[128,512]{1,0:T(8,128)(2,1)S(1)}, u32[]{:S(2)}, u32[]{:S(2)}) collective-permute-start(bf16[128,512]{1,0:T(8,128)(2,1)S(1)} %get-tuple-element.32), channel_id=1, source_target_pairs={{0,2},{1,16},{2,0},{3,18},{4,6},{5,20},{6,4},{7,22},{8,10},{9,24},... | collective-permute-start | bytes 393224 | tf_op jit(solution)/shard_map/ppermute | solution.py:329
  5.2 17.5 %collective-permute-start.1 = (bf16[128,512]{1,0:T(8,128)(2,1)S(1)}, bf16[128,512]{1,0:T(8,128)(2,1)S(1)}, u32[]{:S(2)}, u32[]{:S(2)}) collective-permute-start(bf16[128,512]{1,0:T(8,128)(2,1)S(1)} %get-tuple-element.33), channel_id=1, source_target_pairs={{0,16},{1,0},{2,18},{3,2},{4,20},{5,4},{6,22},{7,6},{8,24},{9,8},{... | collective-permute-start | bytes 393224 | tf_op jit(solution)/shard_map/ppermute | solution.py:329
  6.7 16.0 %collective-permute-start.2 = (bf16[128,512]{1,0:T(8,128)(2,1)S(1)}, bf16[128,512]{1,0:T(8,128)(2,1)S(1)}, u32[]{:S(2)}, u32[]{:S(2)}) collective-permute-start(bf16[128,512]{1,0:T(8,128)(2,1)S(1)} %get-tuple-element.33), channel_id=1, source_target_pairs={{0,2},{1,16},{2,0},{3,18},{4,6},{5,20},{6,4},{7,22},{8,10},{9,24},... | collective-permute-start | bytes 393224 | tf_op jit(solution)/shard_map/ppermute | solution.py:329
  9.2 19.4 %copy-start = (s32[2,8]{1,0:T(2,128)S(1)}, s32[2,8]{1,0:T(2,128)}, u32[]{:S(2)}) copy-start(s32[2,8]{1,0:T(2,128)} %int_screen_ref.7) | copy-start | bytes 196
  9.2 13.5 %collective-permute-start.4 = (bf16[128,512]{1,0:T(8,128)(2,1)S(1)}, bf16[128,512]{1,0:T(8,128)(2,1)S(1)}, u32[]{:S(2)}, u32[]{:S(2)}) collective-permute-start(bf16[128,512]{1,0:T(8,128)(2,1)S(1)} %get-tuple-element.40.after.refs_0_), channel_id=1, source_target_pairs={{0,4},{1,5},{2,6},{3,7},{4,0},{5,1},{6,2},{7,3},{8,12},{9,13},{10,... | collective-permute-start | bytes 393224 | tf_op jit(solution)/shard_map/ppermute | solution.py:291
  10.7 12.0 %collective-permute-start.5 = (bf16[128,512]{1,0:T(8,128)(2,1)S(1)}, bf16[128,512]{1,0:T(8,128)(2,1)S(1)}, u32[]{:S(2)}, u32[]{:S(2)}) collective-permute-start(bf16[128,512]{1,0:T(8,128)(2,1)S(1)} %get-tuple-element.40.after.refs_0_), channel_id=1, source_target_pairs={{0,8},{1,9},{2,10},{3,11},{4,12},{5,13},{6,14},{7,15},{8,0},{9,1},... | collective-permute-start | bytes 393224 | tf_op jit(solution)/shard_map/ppermute | solution.py:291
  16.7 8.2 %collective-permute-start.6 = (bf16[128,512]{1,0:T(8,128)(2,1)S(1)}, bf16[128,512]{1,0:T(8,128)(2,1)S(1)}, u32[]{:S(2)}, u32[]{:S(2)}) collective-permute-start(bf16[128,512]{1,0:T(8,128)(2,1)S(1)} %get-tuple-element.40.after.refs_0_), channel_id=1, source_target_pairs={{0,12},{1,13},{2,14},{3,15},{4,8},{5,9},{6,10},{7,11},{8,4},{9,5},... | collective-permute-start | bytes 393224 | tf_op jit(solution)/shard_map/ppermute | solution.py:291
  25.0 3.6 %collective-permute-start.10 = (bf16[4,128,512]{2,1,0:T(8,128)(2,1)S(1)}, bf16[4,128,512]{2,1,0:T(8,128)(2,1)S(1)}, u32[]{:S(2)}, u32[]{:S(2)}) collective-permute-start(bf16[4,128,512]{2,1,0:T(8,128)(2,1)S(1)} %pad_maximum_fusion), channel_id=1, source_target_pairs={{0,2},{1,3},{2,0},{3,1},{4,6},{5,7},{6,4},{7,5},{8,10},{9,11},{10,... | collective-permute-start | bytes 1572872 | tf_op jit(solution)/shard_map/ppermute | solution.py:337
  25.0 9.7 %collective-permute-start.7 = (bf16[128,512]{1,0:T(8,128)(2,1)S(1)}, bf16[128,512]{1,0:T(8,128)(2,1)S(1)}, u32[]{:S(2)}, u32[]{:S(2)}) collective-permute-start(bf16[128,512]{1,0:T(8,128)(2,1)S(1)} %get-tuple-element.54.refs_0_), channel_id=1, source_target_pairs={{0,4},{1,5},{2,6},{3,7},{4,0},{5,1},{6,2},{7,3},{8,12},{9,13},{10,... | collective-permute-start | bytes 393224 | tf_op jit(solution)/shard_map/ppermute | solution.py:291
  25.6 9.1 %collective-permute-start.8 = (bf16[128,512]{1,0:T(8,128)(2,1)S(1)}, bf16[128,512]{1,0:T(8,128)(2,1)S(1)}, u32[]{:S(2)}, u32[]{:S(2)}) collective-permute-start(bf16[128,512]{1,0:T(8,128)(2,1)S(1)} %get-tuple-element.54.refs_0_), channel_id=1, source_target_pairs={{0,8},{1,9},{2,10},{3,11},{4,12},{5,13},{6,14},{7,15},{8,0},{9,1},... | collective-permute-start | bytes 393224 | tf_op jit(solution)/shard_map/ppermute | solution.py:291
  26.4 8.5 %collective-permute-start.9 = (bf16[128,512]{1,0:T(8,128)(2,1)S(1)}, bf16[128,512]{1,0:T(8,128)(2,1)S(1)}, u32[]{:S(2)}, u32[]{:S(2)}) collective-permute-start(bf16[128,512]{1,0:T(8,128)(2,1)S(1)} %get-tuple-element.54.refs_0_), channel_id=1, source_target_pairs={{0,12},{1,13},{2,14},{3,15},{4,8},{5,9},{6,10},{7,11},{8,4},{9,5},... | collective-permute-start | bytes 393224 | tf_op jit(solution)/shard_map/ppermute | solution.py:291
  31.8 19.0 %collective-permute-start.13 = (s16[128,2048]{1,0:T(8,128)(2,1)S(1)}, s16[128,2048]{1,0:T(8,128)(2,1)S(1)}, u32[]{:S(2)}, u32[]{:S(2)}) collective-permute-start(s16[128,2048]{1,0:T(8,128)(2,1)S(1)} %get-tuple-element.49), channel_id=1, source_target_pairs={{0,1},{1,0},{2,3},{3,2},{4,5},{5,4},{6,7},{7,6},{8,9},{9,8},{10,11... | collective-permute-start | bytes 1572872 | tf_op jit(solution)/shard_map/ppermute | solution.py:339
  34.9 1.3 %collective-permute-start.19 = (bf16[128,512]{1,0:T(8,128)(2,1)S(1)}, bf16[128,512]{1,0:T(8,128)(2,1)S(1)}, u32[]{:S(2)}, u32[]{:S(2)}) collective-permute-start(bf16[128,512]{1,0:T(8,128)(2,1)S(1)} %get-tuple-element.54.refs_0_), channel_id=1, source_target_pairs={{0,2},{1,3},{2,0},{3,1},{4,6},{5,7},{6,4},{7,5},{8,10},{9,11},{10,... | collective-permute-start | bytes 393224 | tf_op jit(solution)/shard_map/ppermute | solution.py:312
  34.9 2.8 %collective-permute-start.20 = (bf16[128,512]{1,0:T(8,128)(2,1)S(1)}, bf16[128,512]{1,0:T(8,128)(2,1)S(1)}, u32[]{:S(2)}, u32[]{:S(2)}) collective-permute-start(bf16[128,512]{1,0:T(8,128)(2,1)S(1)} %collective-permute-done.7.refs_1_), channel_id=1, source_target_pairs={{0,2},{1,3},{2,0},{3,1},{4,6},{5,7},{6,4},{7,5},{8,10},{9,11},{10,... | collective-permute-start | bytes 393224 | tf_op jit(solution)/shard_map/ppermute | solution.py:312
  35.4 2.3 %collective-permute-start.21 = (bf16[128,512]{1,0:T(8,128)(2,1)S(1)}, bf16[128,512]{1,0:T(8,128)(2,1)S(1)}, u32[]{:S(2)}, u32[]{:S(2)}) collective-permute-start(bf16[128,512]{1,0:T(8,128)(2,1)S(1)} %collective-permute-done.8.refs_2_), channel_id=1, source_target_pairs={{0,2},{1,3},{2,0},{3,1},{4,6},{5,7},{6,4},{7,5},{8,10},{9,11},{10,... | collective-permute-start | bytes 393224 | tf_op jit(solution)/shard_map/ppermute | solution.py:312
  35.5 10.4 %collective-permute-start.11 = (bf16[256,512]{1,0:T(8,128)(2,1)S(1)}, bf16[256,512]{1,0:T(8,128)(2,1)S(1)}, u32[]{:S(2)}, u32[]{:S(2)}) collective-permute-start(bf16[256,512]{1,0:T(8,128)(2,1)S(1)} %pad_maximum_fusion.1.refs_0_), channel_id=1, source_target_pairs={{0,8},{1,9},{2,10},{3,11},{4,12},{5,13},{6,14},{7,15},{8,0},{9,1},... | collective-permute-start | bytes 786440 | tf_op jit(solution)/shard_map/ppermute | solution.py:291
  36.3 12.9 %collective-permute-start.16 = (bf16[256,512]{1,0:T(8,128)(2,1)S(1)}, bf16[256,512]{1,0:T(8,128)(2,1)S(1)}, u32[]{:S(2)}, u32[]{:S(2)}) collective-permute-start(bf16[256,512]{1,0:T(8,128)(2,1)S(1)} %pad_maximum_fusion.1.refs_0_), channel_id=1, source_target_pairs={{0,4},{1,5},{2,6},{3,7},{4,0},{5,1},{6,2},{7,3},{8,12},{9,13},{10,... | collective-permute-start | bytes 786440 | tf_op jit(solution)/shard_map/ppermute | solution.py:291
  37.7 1.4 %collective-permute-start.22 = (bf16[128,512]{1,0:T(8,128)(2,1)S(1)}, bf16[128,512]{1,0:T(8,128)(2,1)S(1)}, u32[]{:S(2)}, u32[]{:S(2)}) collective-permute-start(bf16[128,512]{1,0:T(8,128)(2,1)S(1)} %collective-permute-done.9.refs_3_), channel_id=1, source_target_pairs={{0,2},{1,3},{2,0},{3,1},{4,6},{5,7},{6,4},{7,5},{8,10},{9,11},{10,... | collective-permute-start | bytes 393224 | tf_op jit(solution)/shard_map/ppermute | solution.py:312
  37.7 13.0 %collective-permute-start.12 = (bf16[256,512]{1,0:T(8,128)(2,1)S(1)}, bf16[256,512]{1,0:T(8,128)(2,1)S(1)}, u32[]{:S(2)}, u32[]{:S(2)}) collective-permute-start(bf16[256,512]{1,0:T(8,128)(2,1)S(1)} %pad_maximum_fusion.1.refs_0_), channel_id=1, source_target_pairs={{0,12},{1,13},{2,14},{3,15},{4,8},{5,9},{6,10},{7,11},{8,4},{9,5},... | collective-permute-start | bytes 786440 | tf_op jit(solution)/shard_map/ppermute | solution.py:291
  42.9 16.6 %collective-permute-start.23 = (s16[144,2048]{1,0:T(8,128)(2,1)S(1)}, s16[144,2048]{1,0:T(8,128)(2,1)S(1)}, u32[]{:S(2)}, u32[]{:S(2)}) collective-permute-start(s16[144,2048]{1,0:T(8,128)(2,1)S(1)} %get-tuple-element.58), channel_id=1, source_target_pairs={{0,1},{1,0},{2,3},{3,2},{4,5},{5,4},{6,7},{7,6},{8,9},{9,8},{10,11... | collective-permute-start | bytes 1769480 | tf_op jit(solution)/shard_map/ppermute | solution.py:345
  45.9 5.4 %collective-permute-start.17 = (bf16[256,512]{1,0:T(8,128)(2,1)S(1)}, bf16[256,512]{1,0:T(8,128)(2,1)S(1)}, u32[]{:S(2)}, u32[]{:S(2)}) collective-permute-start(bf16[256,512]{1,0:T(8,128)(2,1)S(1)} %pad_maximum_fusion.1.refs_0_), channel_id=1, source_target_pairs={{0,2},{1,3},{2,0},{3,1},{4,6},{5,7},{6,4},{7,5},{8,10},{9,11},{10,... | collective-permute-start | bytes 786440 | tf_op jit(solution)/shard_map/ppermute | solution.py:312
  49.2 2.0 %collective-permute-start.18 = (bf16[256,512]{1,0:T(8,128)(2,1)S(1)}, bf16[256,512]{1,0:T(8,128)(2,1)S(1)}, u32[]{:S(2)}, u32[]{:S(2)}) collective-permute-start(bf16[256,512]{1,0:T(8,128)(2,1)S(1)} %collective-permute-done.16.refs_1_), channel_id=1, source_target_pairs={{0,2},{1,3},{2,0},{3,1},{4,6},{5,7},{6,4},{7,5},{8,10},{9,11},{10,... | collective-permute-start | bytes 786440 | tf_op jit(solution)/shard_map/ppermute | solution.py:312
  50.7 3.7 %collective-permute-start.14 = (bf16[256,512]{1,0:T(8,128)(2,1)S(1)}, bf16[256,512]{1,0:T(8,128)(2,1)S(1)}, u32[]{:S(2)}, u32[]{:S(2)}) collective-permute-start(bf16[256,512]{1,0:T(8,128)(2,1)S(1)} %collective-permute-done.11.refs_0_), channel_id=1, source_target_pairs={{0,2},{1,3},{2,0},{3,1},{4,6},{5,7},{6,4},{7,5},{8,10},{9,11},{10,... | collective-permute-start | bytes 786440 | tf_op jit(solution)/shard_map/ppermute | solution.py:312
  50.7 3.7 %collective-permute-start.15 = (bf16[256,512]{1,0:T(8,128)(2,1)S(1)}, bf16[256,512]{1,0:T(8,128)(2,1)S(1)}, u32[]{:S(2)}, u32[]{:S(2)}) collective-permute-start(bf16[256,512]{1,0:T(8,128)(2,1)S(1)} %collective-permute-done.12.refs_1_), channel_id=1, source_target_pairs={{0,2},{1,3},{2,0},{3,1},{4,6},{5,7},{6,4},{7,5},{8,10},{9,11},{10,... | collective-permute-start | bytes 786440 | tf_op jit(solution)/shard_map/ppermute | solution.py:312
  54.4 5.1 %copy-start.1 = (s32[16,2]{0,1:T(2,128)S(1)}, s32[16,2]{0,1:T(2,128)}, u32[]{:S(2)}) copy-start(s32[16,2]{0,1:T(2,128)} %param.6) | copy-start | bytes 388
